TPU v7x, 512 devices: a whole 4x4x16 slice. The times are simulated.
512 devices in a mesh: leaf: 128 (over z, y, core), rep: 4 (over x).
Axes of the slice: x: 4, y: 4, z: 16, core: 2. Of those that a mesh axis runs over, the one named last changes fastest.
Arguments:
- basis: float32 [7, 128, 65536], P(None, 'rep', 'leaf'), may hold values from -6 to 6
- near_blocks: float32 [1024, 4, 4096], P('leaf'), may hold values from -0.375 to 0.375
- near_cols: int32 [1024, 4], P('leaf'), may hold values from 0 to 7
- bead_order: int32 [128, 512], P('leaf'), may hold values from 0 to 511, each once within a row
Outputs:
- factors: float32 [7, 128, 16384], P(None, 'rep', 'leaf')
Inputs may be any that keep to these rules, and one draw needn't show every extreme that they name: `near_cols`: block columns within the leaf; a block row may name a column twice. `bead_order`: each leaf's row is a permutation of its 512 rows.
All inputs are finite; a program needn't handle non-finite values.
Results may differ from a plain program's by a relative error of at most 0.00012.
Values sent between devices are 32-bit elements; how exact they have to be, the bound alone decides.
No kernel may reach another device: no remote copies, remote signals or barrier semaphores. Data moves between devices by JAX's collectives and lax.ppermute only.
A program may use at most 64 MiB of HBM per device.

v0:
```python
import math

import jax
import jax.numpy as jnp
from jax import lax
from jax.sharding import PartitionSpec as P


def swapped(value, axis, apart):
    mask = 2**apart
    pairs = [(source, source ^ mask) for source in range(lax.axis_size(axis))]
    return lax.ppermute(value, axis, pairs)


def near_field(ordered, tiles_flat, near_cols):
    levels, width, rows = ordered.shape
    block_rows, per_row = near_cols.shape
    blk = rows // block_rows
    blocked = ordered.reshape(levels, width, block_rows, blk)
    picked = jnp.take(blocked, near_cols.reshape(-1), axis=2).reshape(
        levels, width, block_rows, per_row, blk
    )
    tiles = tiles_flat.reshape(block_rows, per_row, blk, blk)
    image = jnp.einsum("qnij,lcqnj->lcqi", tiles, picked, precision=lax.Precision.HIGHEST)
    return image.reshape(levels, width, rows)


def merge_pair(lower, upper, q_lower, q_upper):
    width = lower.shape[0]
    panels = jnp.concatenate([lower, upper], axis=0)
    zeros = jnp.zeros((width, width), jnp.float32)
    blocks = jnp.concatenate(
        [jnp.concatenate([q_lower, zeros], axis=1), jnp.concatenate([zeros, q_upper], axis=1)],
        axis=0,
    )
    capacity = blocks + jnp.dot(panels, panels.T, precision=lax.Precision.HIGHEST) / width
    factor = jnp.linalg.cholesky(capacity)
    whitened = jax.scipy.linalg.solve_triangular(factor, panels, lower=True)
    merged = (
        jnp.eye(width, dtype=jnp.float32)
        + jnp.dot(whitened.T, whitened, precision=lax.Precision.HIGHEST) / width
    )
    return (whitened, merged)


def combine_level(mine, theirs, q_mine, q_theirs, side):
    is_lower = side == 0
    lower = jnp.where(is_lower, mine, theirs)
    upper = jnp.where(is_lower, theirs, mine)
    q_lower = jnp.where(is_lower, q_mine, q_theirs)
    q_upper = jnp.where(is_lower, q_theirs, q_mine)
    whitened, merged = merge_pair(lower, upper, q_lower, q_upper)
    width = mine.shape[0]
    own_half = lax.dynamic_slice_in_dim(whitened, side * width, width, 0)
    return (own_half, merged)


def local(basis, near_blocks, near_cols, bead_order):
    levels, narrow, rows = basis.shape
    inv_root = 1.0 / math.sqrt(rows)
    ordered = jnp.take(basis, bead_order[0], axis=2)
    image = near_field(ordered, near_blocks, near_cols)
    columns = (
        jnp.einsum(
            "lan,lbn->lab",
            lax.all_gather(ordered, "rep", axis=1, tiled=True),
            image,
            precision=lax.Precision.HIGHEST,
        )
        * inv_root
    )
    panels = lax.all_gather(columns, "rep", axis=2, tiled=True)
    width = panels.shape[1]
    leaf_index = lax.axis_index("leaf")
    rep_index = lax.axis_index("rep")
    root_half = math.sqrt(0.5)
    stacked = [panels[level] for level in range(levels)]
    capacity = jnp.eye(width, dtype=jnp.float32)
    halves = []
    for bit in range(levels):
        sent = jnp.stack([capacity] + stacked[bit:])
        received = swapped(sent, "leaf", bit)
        side = leaf_index >> bit & 1
        own_half, capacity = combine_level(stacked[bit], received[1], capacity, received[0], side)
        halves.append(own_half)
        for upper_level in range(bit + 1, levels):
            stacked[upper_level] = (
                stacked[upper_level] + received[upper_level - bit + 1]
            ) * root_half
    outputs = [lax.dynamic_slice_in_dim(half, rep_index * narrow, narrow, 1).T for half in halves]
    return jnp.stack(outputs)


def solution(mesh):
    return jax.shard_map(
        local,
        mesh=mesh,
        in_specs=(P(None, "rep", "leaf"), P("leaf", None, None), P("leaf", None), P("leaf", None)),
        out_specs=P(None, "rep", "leaf"),
        check_vma=False,
    )
```

profile of v0, /device:TPU:24, one launch (start us, length us, event | category | flops | bytes accessed | tf_op | source)
XLA Modules:
  0.0 619.4 jit_solution(285244315619191392)
XLA Ops:
  19.4 4.5 copy.62
  24.5 5.6 fusion.2
  30.9 24.6 %all-gather.2.cloned.1.call-done = f32[7,128,512]{2,1,0:T(8,128)} async-done(((f32[7,32,512]{2,1,0:T(8,128)}), f32[7,128,512]{2,1,0:T(8,128)}) %all-gather.2.cloned.1.call-update) | async-done | bytes 1835024 | tf_op jit(solution)/shard_map/all_gather | solution.py:66
  58.9 13.2 %all_gather.7 = f32[7,128,128]{1,2,0:T(8,128)S(1)} all-gather(f32[7,128,32]{1,2,0:T(8,128)S(1)} %convolution_multiply_fusion.7), channel_id=1, replica_groups=mesh['leaf'=128,'rep'=4] {'rep'}, dimensions={2}, use_global_device_ids=true | all-gather | bytes 573440 | tf_op jit(solution)/shard_map/all_gather | solution.py:72
  76.6 11.7 %cholesky.340 = f32[128,128]{1,0:T(8,128)S(1)} custom-call(f32[128,128]{1,0:T(8,128)S(1)} %cholesky.574), custom_call_target="Cholesky" | custom-call | tf_op jit(solution)/shard_map/jit(cholesky)/cholesky | solution.py:37
  88.4 9.8 %custom-call.23 = f32[1,128,128]{1,2,0:T(8,128)S(1)} custom-call(f32[1,128,128]{2,1,0:T(8,128)S(1)} %get-tuple-element.203), custom_call_target="InvertDiagBlocksLowerTriangular" | custom-call | tf_op jit(solution)/shard_map/jit(cholesky)/cholesky | solution.py:37
  98.7 11.7 %cholesky.357 = f32[128,128]{1,0:T(8,128)S(1)} custom-call(f32[128,128]{1,0:T(8,128)S(1)} %convolution_subtract_fusion.13), custom_call_target="Cholesky" | custom-call | tf_op jit(solution)/shard_map/jit(cholesky)/cholesky | solution.py:37
  113.1 4.2 while.14
  117.3 19.7 %custom-call.24 = f32[2,128,128]{1,2,0:T(8,128)S(1)} custom-call(f32[2,128,128]{2,1,0:T(8,128)S(1)} %get-tuple-element.51), custom_call_target="InvertDiagBlocksLowerTriangular" | custom-call | tf_op jit(solution)/shard_map/jit(_solve_triangular)/triangular_solve | solution.py:38
  141.1 11.7 %collective-permute-done.1 = f32[7,128,128]{1,2,0:T(8,128)S(1)} collective-permute-done((f32[7,128,128]{1,2,0:T(8,128)S(1)}, f32[7,128,128]{1,2,0:T(8,128)S(1)}, u32[]{:S(2)}, u32[]{:S(2)}) %collective-permute-start.1) | collective-permute-done | bytes 458784 | tf_op jit(solution)/shard_map/ppermute | solution.py:12
  153.5 11.7 %cholesky.374 = f32[128,128]{1,0:T(8,128)S(1)} custom-call(f32[128,128]{1,0:T(8,128)S(1)} %cholesky.577), custom_call_target="Cholesky" | custom-call | tf_op jit(solution)/shard_map/jit(cholesky)/cholesky | solution.py:37
  165.3 9.8 %custom-call.25 = f32[1,128,128]{1,2,0:T(8,128)S(1)} custom-call(f32[1,128,128]{2,1,0:T(8,128)S(1)} %get-tuple-element.199), custom_call_target="InvertDiagBlocksLowerTriangular" | custom-call | tf_op jit(solution)/shard_map/jit(cholesky)/cholesky | solution.py:37
  175.5 11.7 %cholesky.391 = f32[128,128]{1,0:T(8,128)S(1)} custom-call(f32[128,128]{1,0:T(8,128)S(1)} %convolution_subtract_fusion.11), custom_call_target="Cholesky" | custom-call | tf_op jit(solution)/shard_map/jit(cholesky)/cholesky | solution.py:37
  189.8 4.0 while.15
  193.8 19.7 %custom-call.26 = f32[2,128,128]{1,2,0:T(8,128)S(1)} custom-call(f32[2,128,128]{2,1,0:T(8,128)S(1)} %get-tuple-element.52), custom_call_target="InvertDiagBlocksLowerTriangular" | custom-call | tf_op jit(solution)/shard_map/jit(_solve_triangular)/triangular_solve | solution.py:38
  218.2 10.4 %collective-permute-done.2 = f32[6,128,128]{1,2,0:T(8,128)S(1)} collective-permute-done((f32[6,128,128]{1,2,0:T(8,128)S(1)}, f32[6,128,128]{1,2,0:T(8,128)S(1)}, u32[]{:S(2)}, u32[]{:S(2)}) %collective-permute-start.2) | collective-permute-done | bytes 393248 | tf_op jit(solution)/shard_map/ppermute | solution.py:12
  229.3 11.7 %cholesky.408 = f32[128,128]{1,0:T(8,128)S(1)} custom-call(f32[128,128]{1,0:T(8,128)S(1)} %cholesky.580), custom_call_target="Cholesky" | custom-call | tf_op jit(solution)/shard_map/jit(cholesky)/cholesky | solution.py:37
  241.1 9.8 %custom-call.27 = f32[1,128,128]{1,2,0:T(8,128)S(1)} custom-call(f32[1,128,128]{2,1,0:T(8,128)S(1)} %get-tuple-element.195), custom_call_target="InvertDiagBlocksLowerTriangular" | custom-call | tf_op jit(solution)/shard_map/jit(cholesky)/cholesky | solution.py:37
  251.3 11.7 %cholesky.425 = f32[128,128]{1,0:T(8,128)S(1)} custom-call(f32[128,128]{1,0:T(8,128)S(1)} %convolution_subtract_fusion.9), custom_call_target="Cholesky" | custom-call | tf_op jit(solution)/shard_map/jit(cholesky)/cholesky | solution.py:37
  265.6 4.2 while.16
  269.8 19.7 %custom-call.28 = f32[2,128,128]{1,2,0:T(8,128)S(1)} custom-call(f32[2,128,128]{2,1,0:T(8,128)S(1)} %get-tuple-element.53), custom_call_target="InvertDiagBlocksLowerTriangular" | custom-call | tf_op jit(solution)/shard_map/jit(_solve_triangular)/triangular_solve | solution.py:38
  294.6 6.2 %collective-permute-done.3 = f32[5,128,128]{1,2,0:T(8,128)S(1)} collective-permute-done((f32[5,128,128]{1,2,0:T(8,128)S(1)}, f32[5,128,128]{1,2,0:T(8,128)S(1)}, u32[]{:S(2)}, u32[]{:S(2)}) %collective-permute-start.3) | collective-permute-done | bytes 327712 | tf_op jit(solution)/shard_map/ppermute | solution.py:12
  301.5 11.7 %cholesky.442 = f32[128,128]{1,0:T(8,128)S(1)} custom-call(f32[128,128]{1,0:T(8,128)S(1)} %cholesky.583), custom_call_target="Cholesky" | custom-call | tf_op jit(solution)/shard_map/jit(cholesky)/cholesky | solution.py:37
  313.3 9.8 %custom-call.29 = f32[1,128,128]{1,2,0:T(8,128)S(1)} custom-call(f32[1,128,128]{2,1,0:T(8,128)S(1)} %get-tuple-element.191), custom_call_target="InvertDiagBlocksLowerTriangular" | custom-call | tf_op jit(solution)/shard_map/jit(cholesky)/cholesky | solution.py:37
  323.6 11.7 %cholesky.459 = f32[128,128]{1,0:T(8,128)S(1)} custom-call(f32[128,128]{1,0:T(8,128)S(1)} %convolution_subtract_fusion.7), custom_call_target="Cholesky" | custom-call | tf_op jit(solution)/shard_map/jit(cholesky)/cholesky | solution.py:37
  338.0 4.2 while.17
  342.2 19.7 %custom-call.30 = f32[2,128,128]{1,2,0:T(8,128)S(1)} custom-call(f32[2,128,128]{2,1,0:T(8,128)S(1)} %get-tuple-element.54), custom_call_target="InvertDiagBlocksLowerTriangular" | custom-call | tf_op jit(solution)/shard_map/jit(_solve_triangular)/triangular_solve | solution.py:38
  363.2 4.4 collective-permute-start.4
  368.0 9.3 %collective-permute-done.4 = f32[4,128,128]{1,2,0:T(8,128)S(1)} collective-permute-done((f32[4,128,128]{1,2,0:T(8,128)S(1)}, f32[4,128,128]{1,2,0:T(8,128)S(1)}, u32[]{:S(2)}, u32[]{:S(2)}) %collective-permute-start.4) | collective-permute-done | bytes 262176 | tf_op jit(solution)/shard_map/ppermute | solution.py:12
  377.9 11.7 %cholesky.476 = f32[128,128]{1,0:T(8,128)S(1)} custom-call(f32[128,128]{1,0:T(8,128)S(1)} %cholesky.586), custom_call_target="Cholesky" | custom-call | tf_op jit(solution)/shard_map/jit(cholesky)/cholesky | solution.py:37
  389.7 9.8 %custom-call.31 = f32[1,128,128]{1,2,0:T(8,128)S(1)} custom-call(f32[1,128,128]{2,1,0:T(8,128)S(1)} %get-tuple-element.187), custom_call_target="InvertDiagBlocksLowerTriangular" | custom-call | tf_op jit(solution)/shard_map/jit(cholesky)/cholesky | solution.py:37
  400.0 11.7 %cholesky.493 = f32[128,128]{1,0:T(8,128)S(1)} custom-call(f32[128,128]{1,0:T(8,128)S(1)} %convolution_subtract_fusion.5), custom_call_target="Cholesky" | custom-call | tf_op jit(solution)/shard_map/jit(cholesky)/cholesky | solution.py:37
  414.4 4.4 while.18
  418.8 19.7 %custom-call.32 = f32[2,128,128]{1,2,0:T(8,128)S(1)} custom-call(f32[2,128,128]{2,1,0:T(8,128)S(1)} %get-tuple-element.55), custom_call_target="InvertDiagBlocksLowerTriangular" | custom-call | tf_op jit(solution)/shard_map/jit(_solve_triangular)/triangular_solve | solution.py:38
  439.8 7.6 %collective-permute-start.5 = (f32[3,128,128]{1,2,0:T(8,128)S(1)}, f32[3,128,128]{1,2,0:T(8,128)S(1)}, u32[]{:S(2)}, u32[]{:S(2)}) collective-permute-start(f32[3,128,128]{1,2,0:T(8,128)S(1)} %pad_maximum_fusion.2), channel_id=1, source_target_pairs={{0,128},{4,132},{8,136},{12,140},{16,144},{20,148},{24,152},{28,15... | collective-permute-start | bytes 589832 | tf_op jit(solution)/shard_map/ppermute | solution.py:12
  447.7 15.4 %collective-permute-done.5 = f32[3,128,128]{1,2,0:T(8,128)S(1)} collective-permute-done((f32[3,128,128]{1,2,0:T(8,128)S(1)}, f32[3,128,128]{1,2,0:T(8,128)S(1)}, u32[]{:S(2)}, u32[]{:S(2)}) %collective-permute-start.5) | collective-permute-done | bytes 196640 | tf_op jit(solution)/shard_map/ppermute | solution.py:12
  463.8 11.7 %cholesky.510 = f32[128,128]{1,0:T(8,128)S(1)} custom-call(f32[128,128]{1,0:T(8,128)S(1)} %cholesky.589), custom_call_target="Cholesky" | custom-call | tf_op jit(solution)/shard_map/jit(cholesky)/cholesky | solution.py:37
  475.6 9.8 %custom-call.33 = f32[1,128,128]{1,2,0:T(8,128)S(1)} custom-call(f32[1,128,128]{2,1,0:T(8,128)S(1)} %get-tuple-element.183), custom_call_target="InvertDiagBlocksLowerTriangular" | custom-call | tf_op jit(solution)/shard_map/jit(cholesky)/cholesky | solution.py:37
  485.8 11.7 %cholesky.527 = f32[128,128]{1,0:T(8,128)S(1)} custom-call(f32[128,128]{1,0:T(8,128)S(1)} %convolution_subtract_fusion.3), custom_call_target="Cholesky" | custom-call | tf_op jit(solution)/shard_map/jit(cholesky)/cholesky | solution.py:37
  500.2 4.2 while.19
  504.4 19.7 %custom-call.34 = f32[2,128,128]{1,2,0:T(8,128)S(1)} custom-call(f32[2,128,128]{2,1,0:T(8,128)S(1)} %get-tuple-element.56), custom_call_target="InvertDiagBlocksLowerTriangular" | custom-call | tf_op jit(solution)/shard_map/jit(_solve_triangular)/triangular_solve | solution.py:38
  525.4 11.3 %collective-permute-start.6 = (f32[2,128,128]{1,2,0:T(8,128)S(1)}, f32[2,128,128]{1,2,0:T(8,128)S(1)}, u32[]{:S(2)}, u32[]{:S(2)}) collective-permute-start(f32[2,128,128]{1,2,0:T(8,128)S(1)} %pad_maximum_fusion.15), channel_id=1, source_target_pairs={{0,256},{4,260},{8,264},{12,268},{16,272},{20,276},{24,280},{28,28... | collective-permute-start | bytes 393224 | tf_op jit(solution)/shard_map/ppermute | solution.py:12
  536.8 12.4 %collective-permute-done.6 = f32[2,128,128]{1,2,0:T(8,128)S(1)} collective-permute-done((f32[2,128,128]{1,2,0:T(8,128)S(1)}, f32[2,128,128]{1,2,0:T(8,128)S(1)}, u32[]{:S(2)}, u32[]{:S(2)}) %collective-permute-start.6) | collective-permute-done | bytes 131104 | tf_op jit(solution)/shard_map/ppermute | solution.py:12
  549.8 11.7 %cholesky.544 = f32[128,128]{1,0:T(8,128)S(1)} custom-call(f32[128,128]{1,0:T(8,128)S(1)} %cholesky.592), custom_call_target="Cholesky" | custom-call | tf_op jit(solution)/shard_map/jit(cholesky)/cholesky | solution.py:37
  561.6 9.8 %custom-call.35 = f32[1,128,128]{1,2,0:T(8,128)S(1)} custom-call(f32[1,128,128]{2,1,0:T(8,128)S(1)} %get-tuple-element.179), custom_call_target="InvertDiagBlocksLowerTriangular" | custom-call | tf_op jit(solution)/shard_map/jit(cholesky)/cholesky | solution.py:37
  571.9 11.7 %cholesky.561 = f32[128,128]{1,0:T(8,128)S(1)} custom-call(f32[128,128]{1,0:T(8,128)S(1)} %convolution_subtract_fusion.1), custom_call_target="Cholesky" | custom-call | tf_op jit(solution)/shard_map/jit(cholesky)/cholesky | solution.py:37
  586.2 4.0 while.20
  590.2 19.7 %custom-call.36 = f32[2,128,128]{1,2,0:T(8,128)S(1)} custom-call(f32[2,128,128]{2,1,0:T(8,128)S(1)} %get-tuple-element.57), custom_call_target="InvertDiagBlocksLowerTriangular" | custom-call | tf_op jit(solution)/shard_map/jit(_solve_triangular)/triangular_solve | solution.py:38
  (253 shorter events, 86.5 us)
Async XLA Ops:
  6.5 7.4 %copy-start.1 = (s32[1,512]{1,0:T(1,128)S(1)}, s32[1,512]{1,0:T(1,128)}, u32[]{:S(2)}) copy-start(s32[1,512]{1,0:T(1,128)} %param.10) | copy-start | bytes 6148
  6.5 49.0 %all-gather.2.cloned.1.call-start = ((), (), s32[]{:S(2)}) async-start(), calls=%async_computation | async-start | bytes 2293760 | tf_op jit(solution)/shard_map/all_gather | solution.py:66
  8.4 8.0 %copy-start.2 = (s32[8,4]{0,1:T(4,128)S(1)}, s32[8,4]{0,1:T(4,128)}, u32[]{:S(2)}) copy-start(s32[8,4]{0,1:T(4,128)} %param.9) | copy-start | bytes 388
  19.4 4.5 copy-start
  72.2 3.8 collective-permute-start
  138.4 14.5 %collective-permute-start.1 = (f32[7,128,128]{1,2,0:T(8,128)S(1)}, f32[7,128,128]{1,2,0:T(8,128)S(1)}, u32[]{:S(2)}, u32[]{:S(2)}) collective-permute-start(f32[7,128,128]{1,2,0:T(8,128)S(1)} %get-tuple-element.118), channel_id=1, source_target_pairs={{0,8},{4,12},{8,0},{12,4},{16,24},{20,28},{24,16},{28,20},{32,40},... | collective-permute-start | bytes 1376264 | tf_op jit(solution)/shard_map/ppermute | solution.py:12
  214.9 13.7 %collective-permute-start.2 = (f32[6,128,128]{1,2,0:T(8,128)S(1)}, f32[6,128,128]{1,2,0:T(8,128)S(1)}, u32[]{:S(2)}, u32[]{:S(2)}) collective-permute-start(f32[6,128,128]{1,2,0:T(8,128)S(1)} %constant_dynamic-update-slice_fusion.6), channel_id=1, source_target_pairs={{0,16},{4,20},{8,24},{12,28},{16,0},{20,4},{24,8},{28,12},{32,48},... | collective-permute-start | bytes 1179656 | tf_op jit(solution)/shard_map/ppermute | solution.py:12
  290.9 9.9 %collective-permute-start.3 = (f32[5,128,128]{1,2,0:T(8,128)S(1)}, f32[5,128,128]{1,2,0:T(8,128)S(1)}, u32[]{:S(2)}, u32[]{:S(2)}) collective-permute-start(f32[5,128,128]{1,2,0:T(8,128)S(1)} %constant_dynamic-update-slice_fusion.11), channel_id=1, source_target_pairs={{0,32},{4,36},{8,40},{12,44},{16,48},{20,52},{24,56},{28,60},{32,0... | collective-permute-start | bytes 983048 | tf_op jit(solution)/shard_map/ppermute | solution.py:12
  363.2 14.1 %collective-permute-start.4 = (f32[4,128,128]{1,2,0:T(8,128)S(1)}, f32[4,128,128]{1,2,0:T(8,128)S(1)}, u32[]{:S(2)}, u32[]{:S(2)}) collective-permute-start(f32[4,128,128]{1,2,0:T(8,128)S(1)} %pad_maximum_fusion.1), channel_id=1, source_target_pairs={{0,64},{4,68},{8,72},{12,76},{16,80},{20,84},{24,88},{28,92},{32,9... | collective-permute-start | bytes 786440 | tf_op jit(solution)/shard_map/ppermute | solution.py:12
  439.8 23.3 %collective-permute-start.5 = (f32[3,128,128]{1,2,0:T(8,128)S(1)}, f32[3,128,128]{1,2,0:T(8,128)S(1)}, u32[]{:S(2)}, u32[]{:S(2)}) collective-permute-start(f32[3,128,128]{1,2,0:T(8,128)S(1)} %pad_maximum_fusion.2), channel_id=1, source_target_pairs={{0,128},{4,132},{8,136},{12,140},{16,144},{20,148},{24,152},{28,15... | collective-permute-start | bytes 589832 | tf_op jit(solution)/shard_map/ppermute | solution.py:12
  525.4 23.8 %collective-permute-start.6 = (f32[2,128,128]{1,2,0:T(8,128)S(1)}, f32[2,128,128]{1,2,0:T(8,128)S(1)}, u32[]{:S(2)}, u32[]{:S(2)}) collective-permute-start(f32[2,128,128]{1,2,0:T(8,128)S(1)} %pad_maximum_fusion.15), channel_id=1, source_target_pairs={{0,256},{4,260},{8,264},{12,268},{16,272},{20,276},{24,280},{28,28... | collective-permute-start | bytes 393224 | tf_op jit(solution)/shard_map/ppermute | solution.py:12
  611.1 0.7 copy-start.3
Sparse Core Ops, SparseCore 0:
  14.9 40.5 all-gather.1
where the time goes:
time: 629 us; the launch traced here: 619 us
  other arithmetic  384 us (61%)
  waiting for transfers between devices  91.7 us (15%)
  local copies, waits for them, and re-layouts  45.9 us (7%)
  starting transfers between devices  35 us (6%)
  between operations  23.6 us (4%)
  matrix products  23.5 us (4%)
  blocking collectives  13.2 us (2%)
    another operation x49, other arithmetic, merge_pair(): factor = jnp.linalg.cholesky(capacity)  242 us
    another operation x15, other arithmetic, merge_pair(): whitened = jax.scipy.linalg.solve_triangular(factor, panels, lower=True)  138 us
    ppermute x7, waiting for transfers between devices, swapped(): return lax.ppermute(value, axis, pairs)  67.1 us
    ppermute x7, starting transfers between devices, swapped(): return lax.ppermute(value, axis, pairs)  35 us
    another operation x50, local copies, waits for them, and re-layouts, merge_pair(): whitened = jax.scipy.linalg.solve_triangular(factor, panels, lower=True)  27 us
    all_gather x1, waiting for transfers between devices, local(): lax.all_gather(ordered, 'rep', axis=1, tiled=True)  24.6 us
    all_gather x1, blocking collectives, local(): panels = lax.all_gather(columns, 'rep', axis=2, tiled=True)  13.2 us
  transfers between devices with their start and end apart: 8, of which 8 were waited for; matrix products, arithmetic and copies ran while one was open for 3% of the time, Pallas kernels for 0%

commit v1 on v0

v1 whole, which is shorter than its diff:
```python
import functools
import math

import jax
import jax.numpy as jnp
from jax import lax
from jax.experimental import pallas as pl
from jax.experimental.pallas import tpu as pltpu
from jax.sharding import PartitionSpec as P

F32 = jnp.float32
BF16 = jnp.bfloat16
PANEL = 32
VMEM_BYTES = 48 * 1024 * 1024


def parts(x):
    high = x.astype(BF16)
    return high, (x - high.astype(F32)).astype(BF16)


def contract(a, b, dims):
    return lax.dot_general(a, b, (dims, ((), ())), preferred_element_type=F32)


def product(a, b, dims=((1,), (0,))):
    return contract(a[0], b[0], dims) + (contract(a[0], b[1], dims) + contract(a[1], b[0], dims))


def identity(n):
    rows = lax.broadcasted_iota(jnp.int32, (n, n), 0)
    return (rows == lax.broadcasted_iota(jnp.int32, (n, n), 1)).astype(F32)


def dense_kernel(cols_ref, blocks_ref, order_ref, high_ref, low_ref, columns):
    block_rows, per_row = cols_ref.shape
    blk = blocks_ref.shape[1]
    rows = block_rows * blk
    columns[...] = jnp.zeros_like(columns)
    for q in range(block_rows):
        for n in range(per_row):
            where = (cols_ref[q, n], slice(q * blk, (q + 1) * blk))
            columns[where] = columns[where] + blocks_ref[q * per_row + n]
    tree = jnp.concatenate([columns[c] for c in range(block_rows)], axis=1)
    bead = lax.broadcasted_iota(jnp.int32, (rows, rows), 0)
    select = (bead == order_ref[...]).astype(F32).astype(BF16)
    for piece, out in zip(parts(tree), (high_ref, low_ref)):
        moved = contract(select, piece, ((1,), (0,))).astype(BF16)
        out[...] = contract(moved, select, ((1,), (1,))).astype(BF16)


def panel_kernel(basis_ref, high_ref, low_ref, out_ref, first_ref):
    reps, levels, narrow, rows = basis_ref.shape
    scale = 1.0 / math.sqrt(rows)
    width = reps * narrow
    for level in range(levels):
        basis = parts(basis_ref[:, level].reshape(width, rows))
        image = product(basis, (high_ref[...], low_ref[...]))
        panel = product(parts(image), basis, ((1,), (1,))) * scale
        if level == 0:
            first_ref[...] = panel
            pair = parts(panel)
            panel = product(pair, pair, ((0,), (0,))) * (1.0 / width)
        out_ref[level] = panel


def level_kernel(last, side_ref, own_ref, other_ref, panel_ref, q_ref, *outs):
    width = panel_ref.shape[0]
    eye = identity(width)
    own, other = own_ref[0], other_ref[0]
    total = own + other
    bound = 1.0 + 2.0 * jnp.max(jnp.sum(jnp.abs(total), axis=0))
    if last:
        matrices = [eye + other]
    else:
        matrices = [eye + 2.0 * total, eye + total, eye + other]
    pairs = [parts(matrix) for matrix in matrices]
    rho = (bound - 1.0) / (bound + 1.0)
    step = 2.0 / (bound + 1.0)
    scale = 2.0 / (2.0 - rho * rho)
    start = tuple(scale * step * (2.0 * eye - step * matrix) for matrix in matrices)

    def go_on(carry):
        return carry[0] > 1e-3

    def refine(carry):
        rho, inverses = carry
        scale = 2.0 / (2.0 - rho * rho)
        new = []
        for pair, inverse in zip(pairs, inverses):
            x = parts(inverse)
            image = parts(product(pair, x))
            new.append(scale * (2.0 * inverse - product(x, image)))
        return (rho * rho / (2.0 - rho * rho), tuple(new))

    _, inverses = lax.while_loop(go_on, refine, (rho * rho / (2.0 - rho * rho), start))
    final = []
    for pair, inverse in zip(pairs, inverses):
        x = parts(inverse)
        residual = parts(eye - product(pair, x))
        final.append(inverse + product(x, residual))
    panel = parts(panel_ref[...])
    if not last:
        c_ref, pg_ref, next_panel_ref, next_q_ref, next_ref = outs
        root_half = math.sqrt(0.5)
        next_panel = (own_ref[1] + other_ref[1]) * root_half
        next_panel_ref[...] = next_panel
        pair = parts(next_panel)
        half = parts(0.5 * (eye + final[0]))
        next_ref[0] = product(pair, parts(product(half, pair)), ((0,), (0,))) * (1.0 / width)
        next_q_ref[...] = 2.0 * eye - final[1]
        for upper in range(1, next_ref.shape[0]):
            next_ref[upper] = (own_ref[upper + 1] + other_ref[upper + 1]) * root_half
    else:
        c_ref, pg_ref = outs
    gain = parts(jnp.where(side_ref[0] == 1, final[-1], eye))
    pg = product(panel, gain)
    pg_ref[...] = pg
    c_ref[...] = q_ref[...] + product(parts(pg), panel, ((1,), (1,))) * (1.0 / width)


def whiten_kernel(rep_ref, *refs):
    levels = (len(refs) - 2) // 2
    c_refs, x_refs, out_ref, turned = refs[:levels], refs[levels:2 * levels], refs[-2], refs[-1]
    width = c_refs[0].shape[0]
    narrow = out_ref.shape[1]
    lane = lax.broadcasted_iota(jnp.int32, (8, width), 1)
    sub = lax.broadcasted_iota(jnp.int32, (8, width), 0)
    count = PANEL // 8
    state = [jnp.concatenate([c[...], x[...]], axis=1) for c, x in zip(c_refs, x_refs)]
    done = [[] for _ in range(levels)]
    for top in range(0, width, PANEL):
        left = [[s[8 * j:8 * j + 8, :width] for j in range(count)] for s in state]
        right = [[s[8 * j:8 * j + 8, width:] for j in range(count)] for s in state]
        for kk in range(PANEL):
            k, block, row = top + kk, kk // 8, kk % 8
            for m in range(levels):
                v, w = left[m], right[m]
                line = jnp.broadcast_to(v[block][row:row + 1], (8, width))
                line_x = jnp.broadcast_to(w[block][row:row + 1], (8, width))
                pivot = jnp.broadcast_to(line[:, k:k + 1], (8, width))
                inverse = 1.0 / pivot
                for j in range(block, count):
                    if j == block and row == 7:
                        continue
                    factor = jnp.broadcast_to(v[j][:, k:k + 1], (8, width)) * inverse
                    if j == block:
                        factor = jnp.where(sub > row, factor, 0.0)
                    v[j] = v[j] - factor * line
                    w[j] = w[j] - factor * line_x
        for m in range(levels):
            for j in range(count):
                diagonal = jnp.sum(jnp.where(lane == sub + (top + 8 * j), left[m][j], 0.0), axis=1, keepdims=True)
                root = lax.rsqrt(diagonal)
                left[m][j] = left[m][j] * root
                right[m][j] = right[m][j] * root
            done[m].extend(right[m])
            rest = width - top - PANEL
            if rest:
                upper = jnp.concatenate(left[m], axis=0)
                both = jnp.concatenate([upper, jnp.concatenate(right[m], axis=0)], axis=1)
                change = product(parts(upper.T[top + PANEL:]), parts(both))
                state[m] = state[m][PANEL:] - change
    for m in range(levels):
        turned[m] = jnp.concatenate(done[m], axis=0).T
        out_ref[m] = turned[m, pl.ds(pl.multiple_of(rep_ref[0] * narrow, narrow), narrow), :]


def call(kernel, out_shape, n_smem, n_vmem, scratch=()):
    return pl.pallas_call(
        kernel,
        out_shape=out_shape,
        in_specs=[pl.BlockSpec(memory_space=pltpu.SMEM)] * n_smem
        + [pl.BlockSpec(memory_space=pltpu.VMEM)] * n_vmem,
        out_specs=jax.tree.map(lambda _: pl.BlockSpec(memory_space=pltpu.VMEM), out_shape),
        scratch_shapes=list(scratch),
        compiler_params=pltpu.CompilerParams(vmem_limit_bytes=VMEM_BYTES),
    )


def partner(leaf, bit):
    if bit == 0:
        return leaf ^ 1
    if bit == 1:
        return leaf ^ 2
    if bit == 2:
        return leaf ^ 6
    if bit == 4:
        return leaf ^ 24
    if bit == 6:
        z = leaf >> 3
        z = (z + 4) % 16 if z & 4 else (z - 4) % 16
        return z * 8 + (leaf & 7)
    return leaf ^ (1 << bit)


def swapped(value, axis, bit):
    pairs = [(source, partner(source, bit)) for source in range(lax.axis_size(axis))]
    return lax.ppermute(value, axis, pairs)


def local(basis, near_blocks, near_cols, bead_order):
    levels, narrow, rows = basis.shape
    block_rows, per_row = near_cols.shape
    blk = rows // block_rows
    gathered = lax.all_gather(basis, "rep", axis=0)
    width = gathered.shape[0] * narrow
    square = jax.ShapeDtypeStruct((width, width), F32)
    tiles = near_blocks.reshape(block_rows * per_row, blk, blk)
    dense = [jax.ShapeDtypeStruct((rows, rows), BF16)] * 2
    high, low = call(dense_kernel, dense, 1, 2, [pltpu.VMEM((block_rows, rows, blk), F32)])(
        near_cols, tiles, bead_order
    )
    sent, panel = call(
        panel_kernel, [jax.ShapeDtypeStruct((levels, width, width), F32), square], 0, 3
    )(gathered, high, low)
    leaf_index = lax.axis_index("leaf")
    rep_index = lax.axis_index("rep")
    q = jnp.eye(width, dtype=F32)
    c_list, x_list = [], []
    for bit in range(levels):
        last = bit == levels - 1
        received = swapped(sent, "leaf", bit)
        side = (leaf_index >> bit & 1).astype(jnp.int32).reshape(1)
        shapes = [square, square]
        if not last:
            shapes += [square, square, jax.ShapeDtypeStruct((levels - bit - 1, width, width), F32)]
        outs = call(functools.partial(level_kernel, last), shapes, 1, 4)(side, sent, received, panel, q)
        c_list.append(outs[0])
        x_list.append(outs[1])
        if not last:
            panel, q, sent = outs[2:]
    out = jax.ShapeDtypeStruct((levels, narrow, width), F32)
    return call(whiten_kernel, out, 1, 2 * levels, [pltpu.VMEM((levels, width, width), F32)])(
        rep_index.astype(jnp.int32).reshape(1), *c_list, *x_list
    )


def solution(mesh):
    return jax.shard_map(
        local,
        mesh=mesh,
        in_specs=(P(None, "rep", "leaf"), P("leaf", None, None), P("leaf", None), P("leaf", None)),
        out_specs=P(None, "rep", "leaf"),
        check_vma=False,
    )
```

time: 629 us -> 181 us (0.29); the launches traced: 619 us -> 181 us
  other arithmetic: 384 us -> 0.01 us
  Pallas kernels: 0 us -> 49.9 us
  local copies, waits for them, and re-layouts: 45.9 us -> 3.14 us
  matrix products: 23.5 us -> 0 us
  blocking collectives: 13.2 us -> 0 us
  between operations: 23.6 us -> 13.6 us
  waiting for transfers between devices: 91.7 us -> 84.1 us
    another operation x75 -> x0, other arithmetic: 381 us -> none  [the longest x49 242 us: merge_pair(): factor = jnp.linalg.cholesky(capacity)]
    pallas_call x0 -> x10, Pallas kernels: none -> 49.9 us  [the longest x7 23.6 us: local(): call(functools.partial(level_kernel, last), shapes, 1, 4)]
    another operation x72 -> x0, local copies, waits for them, and re-layouts: 28.1 us -> none  [the longest x50 27 us: merge_pair(): whitened = jax.scipy.linalg.solve_triangular(factor, panels, lower=True)]
    ppermute x7, waiting for transfers between devices: 67.1 us -> 44.6 us  [swapped(): return lax.ppermute(value, axis, pairs)]
    dot_general x15 -> x0, matrix products: 14.2 us -> none  [the longest x1 5.56 us: near_field(): jnp.einsum('qnij,lcqnj->lcqi', tiles, picked, precision=lax.Precision.HIG...]
    all_gather x1, waiting for transfers between devices: 24.6 us -> 38.8 us  [local(): gathered = lax.all_gather(basis, 'rep', axis=0)]
    all_gather x1 -> x0, blocking collectives: 13.2 us -> none  [local(): panels = lax.all_gather(columns, 'rep', axis=2, tiled=True)]
    gather x5 -> x0, local copies, waits for them, and re-layouts: 12.1 us -> none  [the longest x2 7.03 us: near_field(): jnp.take(blocked, near_cols.reshape(-1), axis=2)]
  transfers between devices with their start and end apart: 8 -> 8, of which waited for: 8 -> 8; matrix products, arithmetic and copies ran while one was open for 3% -> 1% of each run, Pallas kernels for 0% -> 1%
where the time goes in v1:
time: 181 us
  waiting for transfers between devices  84.1 us (46%)
  Pallas kernels  49.9 us (28%)
  starting transfers between devices  30.2 us (17%)
  between operations  13.6 us (8%)
  local copies, waits for them, and re-layouts  3.14 us (2%)
    ppermute x7, waiting for transfers between devices, swapped(): return lax.ppermute(value, axis, pairs)  44.6 us
    all_gather x1, waiting for transfers between devices, local(): gathered = lax.all_gather(basis, 'rep', axis=0)  38.8 us
    ppermute x7, starting transfers between devices, swapped(): return lax.ppermute(value, axis, pairs)  30.2 us
    pallas_call x7, Pallas kernels, local(): call(functools.partial(level_kernel, last), shapes, 1, 4)  23.6 us
    pallas_call x1, Pallas kernels, local(): call(whiten_kernel, out, 1, 2 * levels, [pltpu.VMEM((levels, width, width...  19 us
    pallas_call x1, Pallas kernels, local(): call(panel_kernel, [jax.ShapeDtypeStruct((levels, width, width), F32), sq...  4.91 us
  transfers between devices with their start and end apart: 8, of which 8 were waited for; matrix products, arithmetic and copies ran while one was open for 1% of the time, Pallas kernels for 1%

profile of v1, /device:TPU:24, one launch (start us, length us, event | category | flops | bytes accessed | tf_op | source)
XLA Modules:
  0.0 180.9 jit_solution(17722098890362995303)
XLA Ops:
  6.5 0.0 copy-start.2
  6.5 0.0 copy-start.1
  6.5 0.0 all-gather.3.cloned.1.call-start
  6.5 0.7 all-gather.3.cloned.1.call-update
  7.3 1.6 reshape.29.blocks_ref
  8.8 0.0 copy-done.2
  8.8 0.1 copy.6.cols_ref
  8.9 0.0 copy-done.1
  8.9 2.4 %shard_map.46 = (bf16[512,512]{1,0:T(8,128)(2,1)S(1)}, bf16[512,512]{1,0:T(8,128)(2,1)S(1)}) custom-call(s32[8,4]{1,0:T(8,128)S(1)} %copy.6.cols_ref, f32[32,64,64]{2,1,0:T(8,128)S(1)} %reshape.29.blocks_ref, s32[1,512]{1,0:T(1,128)S(1)} %copy-done.1), custom_call_target="tpu_custom_call" | custom-call | tf_op jit(solution)/shard_map/pallas_call | solution.py:211
  11.3 38.8 %all-gather.3.cloned.1.call-done = f32[28,32,512]{2,1,0:T(8,128)} async-done(((f32[7,32,512]{2,1,0:T(8,128)}), f32[28,32,512]{2,1,0:T(8,128)}) %all-gather.3.cloned.1.call-update) | async-done | bytes 1835024 | tf_op jit(solution)/shard_map/all_gather | solution.py:206
  50.0 0.0 copy-start
  50.0 1.5 copy-done
  51.5 4.9 %shard_map.47 = (f32[7,128,128]{2,1,0:T(8,128)S(1)}, f32[128,128]{1,0:T(8,128)S(1)}) custom-call(f32[4,7,32,512]{3,2,1,0:T(8,128)S(1)} %bitcast.9, bf16[512,512]{1,0:T(8,128)(2,1)S(1)} %get-tuple-element.41.high_ref, bf16[512,512]{1,0:T(8,128)(2,1)S(1)} %get-tuple-element.42.low_ref), custom_call_target="tpu_custom_call" | custom-call | tf_op jit(solution)/shard_map/pallas_call | solution.py:214
  56.4 1.9 %collective-permute-start = (f32[7,128,128]{2,1,0:T(8,128)S(1)}, f32[7,128,128]{2,1,0:T(8,128)S(1)}, u32[]{:S(2)}, u32[]{:S(2)}) collective-permute-start(f32[7,128,128]{2,1,0:T(8,128)S(1)} %get-tuple-element.43.own_ref), channel_id=1, source_target_pairs={{0,4},{4,0},{8,12},{12,8},{16,20},{20,16},{24,28},{28,24},{32,36},... | collective-permute-start | bytes 1376264 | tf_op jit(solution)/shard_map/ppermute | solution.py:199
  58.4 1.8 collective-permute-done.other_ref
  60.2 3.1 %shard_map.48 = (f32[128,128]{1,0:T(8,128)S(1)}, f32[128,128]{1,0:T(8,128)S(1)}, f32[128,128]{1,0:T(8,128)S(1)}, f32[128,128]{1,0:T(8,128)S(1)}, f32[6,128,128]{2,1,0:T(8,128)S(1)}) custom-call(s32[1]{0:T(128)} %bitcast.1.side_ref, f32[7,128,128]{2,1,0:T(8,128)S(1)} %get-tuple-element.43.own_ref, f32[7,128,128]{2,1,0:T(8,128)S(1)} %collective-permute-done.other_ref, ...), custom_call_target="tpu_custom_call" | custom-call | tf_op jit(solution)/shard_map/pallas_call | solution.py:228
  63.2 3.2 %collective-permute-start.1 = (f32[6,128,128]{2,1,0:T(8,128)S(1)}, f32[6,128,128]{2,1,0:T(8,128)S(1)}, u32[]{:S(2)}, u32[]{:S(2)}) collective-permute-start(f32[6,128,128]{2,1,0:T(8,128)S(1)} %get-tuple-element.46.own_ref), channel_id=1, source_target_pairs={{0,8},{4,12},{8,0},{12,4},{16,24},{20,28},{24,16},{28,20},{32,40},... | collective-permute-start | bytes 1179656 | tf_op jit(solution)/shard_map/ppermute | solution.py:199
  66.4 9.8 %collective-permute-done.1.other_ref = f32[6,128,128]{2,1,0:T(8,128)S(1)} collective-permute-done((f32[6,128,128]{2,1,0:T(8,128)S(1)}, f32[6,128,128]{2,1,0:T(8,128)S(1)}, u32[]{:S(2)}, u32[]{:S(2)}) %collective-permute-start.1) | collective-permute-done | bytes 393248 | tf_op jit(solution)/shard_map/ppermute | solution.py:199
  76.3 3.5 %shard_map.49 = (f32[128,128]{1,0:T(8,128)S(1)}, f32[128,128]{1,0:T(8,128)S(1)}, f32[128,128]{1,0:T(8,128)S(1)}, f32[128,128]{1,0:T(8,128)S(1)}, f32[5,128,128]{2,1,0:T(8,128)S(1)}) custom-call(s32[1]{0:T(128)} %bitcast.3.side_ref, f32[6,128,128]{2,1,0:T(8,128)S(1)} %get-tuple-element.46.own_ref, f32[6,128,128]{2,1,0:T(8,128)S(1)} %collective-permute-done.1.other_ref, ...), custom_call_target="tpu_custom_call" | custom-call | tf_op jit(solution)/shard_map/pallas_call | solution.py:228
  79.8 2.4 %collective-permute-start.2 = (f32[5,128,128]{2,1,0:T(8,128)S(1)}, f32[5,128,128]{2,1,0:T(8,128)S(1)}, u32[]{:S(2)}, u32[]{:S(2)}) collective-permute-start(f32[5,128,128]{2,1,0:T(8,128)S(1)} %get-tuple-element.50.own_ref), channel_id=1, source_target_pairs={{0,24},{4,28},{8,16},{12,20},{16,8},{20,12},{24,0},{28,4},{32,56},... | collective-permute-start | bytes 983048 | tf_op jit(solution)/shard_map/ppermute | solution.py:199
  82.2 9.6 %collective-permute-done.2.other_ref = f32[5,128,128]{2,1,0:T(8,128)S(1)} collective-permute-done((f32[5,128,128]{2,1,0:T(8,128)S(1)}, f32[5,128,128]{2,1,0:T(8,128)S(1)}, u32[]{:S(2)}, u32[]{:S(2)}) %collective-permute-start.2) | collective-permute-done | bytes 327712 | tf_op jit(solution)/shard_map/ppermute | solution.py:199
  91.9 3.5 %shard_map.50 = (f32[128,128]{1,0:T(8,128)S(1)}, f32[128,128]{1,0:T(8,128)S(1)}, f32[128,128]{1,0:T(8,128)S(1)}, f32[128,128]{1,0:T(8,128)S(1)}, f32[4,128,128]{2,1,0:T(8,128)S(1)}) custom-call(s32[1]{0:T(128)} %bitcast.4.side_ref, f32[5,128,128]{2,1,0:T(8,128)S(1)} %get-tuple-element.50.own_ref, f32[5,128,128]{2,1,0:T(8,128)S(1)} %collective-permute-done.2.other_ref, ...), custom_call_target="tpu_custom_call" | custom-call | tf_op jit(solution)/shard_map/pallas_call | solution.py:228
  95.4 3.9 %collective-permute-start.3 = (f32[4,128,128]{2,1,0:T(8,128)S(1)}, f32[4,128,128]{2,1,0:T(8,128)S(1)}, u32[]{:S(2)}, u32[]{:S(2)}) collective-permute-start(f32[4,128,128]{2,1,0:T(8,128)S(1)} %get-tuple-element.54.own_ref), channel_id=1, source_target_pairs={{0,32},{4,36},{8,40},{12,44},{16,48},{20,52},{24,56},{28,60},{32,0... | collective-permute-start | bytes 786440 | tf_op jit(solution)/shard_map/ppermute | solution.py:199
  99.3 4.8 %collective-permute-done.3.other_ref = f32[4,128,128]{2,1,0:T(8,128)S(1)} collective-permute-done((f32[4,128,128]{2,1,0:T(8,128)S(1)}, f32[4,128,128]{2,1,0:T(8,128)S(1)}, u32[]{:S(2)}, u32[]{:S(2)}) %collective-permute-start.3) | collective-permute-done | bytes 262176 | tf_op jit(solution)/shard_map/ppermute | solution.py:199
  104.1 3.5 %shard_map.51 = (f32[128,128]{1,0:T(8,128)S(1)}, f32[128,128]{1,0:T(8,128)S(1)}, f32[128,128]{1,0:T(8,128)S(1)}, f32[128,128]{1,0:T(8,128)S(1)}, f32[3,128,128]{2,1,0:T(8,128)S(1)}) custom-call(s32[1]{0:T(128)} %bitcast.5.side_ref, f32[4,128,128]{2,1,0:T(8,128)S(1)} %get-tuple-element.54.own_ref, f32[4,128,128]{2,1,0:T(8,128)S(1)} %collective-permute-done.3.other_ref, ...), custom_call_target="tpu_custom_call" | custom-call | tf_op jit(solution)/shard_map/pallas_call | solution.py:228
  107.7 5.6 %collective-permute-start.4 = (f32[3,128,128]{2,1,0:T(8,128)S(1)}, f32[3,128,128]{2,1,0:T(8,128)S(1)}, u32[]{:S(2)}, u32[]{:S(2)}) collective-permute-start(f32[3,128,128]{2,1,0:T(8,128)S(1)} %get-tuple-element.58.own_ref), channel_id=1, source_target_pairs={{0,96},{4,100},{8,104},{12,108},{16,112},{20,116},{24,120},{28,124... | collective-permute-start | bytes 589832 | tf_op jit(solution)/shard_map/ppermute | solution.py:199
  113.3 3.8 %collective-permute-done.4.other_ref = f32[3,128,128]{2,1,0:T(8,128)S(1)} collective-permute-done((f32[3,128,128]{2,1,0:T(8,128)S(1)}, f32[3,128,128]{2,1,0:T(8,128)S(1)}, u32[]{:S(2)}, u32[]{:S(2)}) %collective-permute-start.4) | collective-permute-done | bytes 196640 | tf_op jit(solution)/shard_map/ppermute | solution.py:199
  117.2 3.5 %shard_map.52 = (f32[128,128]{1,0:T(8,128)S(1)}, f32[128,128]{1,0:T(8,128)S(1)}, f32[128,128]{1,0:T(8,128)S(1)}, f32[128,128]{1,0:T(8,128)S(1)}, f32[2,128,128]{2,1,0:T(8,128)S(1)}) custom-call(s32[1]{0:T(128)} %bitcast.6.side_ref, f32[3,128,128]{2,1,0:T(8,128)S(1)} %get-tuple-element.58.own_ref, f32[3,128,128]{2,1,0:T(8,128)S(1)} %collective-permute-done.4.other_ref, ...), custom_call_target="tpu_custom_call" | custom-call | tf_op jit(solution)/shard_map/pallas_call | solution.py:228
  120.7 7.9 %collective-permute-start.5 = (f32[2,128,128]{2,1,0:T(8,128)S(1)}, f32[2,128,128]{2,1,0:T(8,128)S(1)}, u32[]{:S(2)}, u32[]{:S(2)}) collective-permute-start(f32[2,128,128]{2,1,0:T(8,128)S(1)} %get-tuple-element.62.own_ref), channel_id=1, source_target_pairs={{0,128},{4,132},{8,136},{12,140},{16,144},{20,148},{24,152},{28,15... | collective-permute-start | bytes 393224 | tf_op jit(solution)/shard_map/ppermute | solution.py:199
  128.6 10.0 %collective-permute-done.5.other_ref = f32[2,128,128]{2,1,0:T(8,128)S(1)} collective-permute-done((f32[2,128,128]{2,1,0:T(8,128)S(1)}, f32[2,128,128]{2,1,0:T(8,128)S(1)}, u32[]{:S(2)}, u32[]{:S(2)}) %collective-permute-start.5) | collective-permute-done | bytes 131104 | tf_op jit(solution)/shard_map/ppermute | solution.py:199
  138.5 3.5 %shard_map.53 = (f32[128,128]{1,0:T(8,128)S(1)}, f32[128,128]{1,0:T(8,128)S(1)}, f32[128,128]{1,0:T(8,128)S(1)}, f32[128,128]{1,0:T(8,128)S(1)}, f32[1,128,128]{2,1,0:T(8,128)S(1)}) custom-call(s32[1]{0:T(128)} %bitcast.7.side_ref, f32[2,128,128]{2,1,0:T(8,128)S(1)} %get-tuple-element.62.own_ref, f32[2,128,128]{2,1,0:T(8,128)S(1)} %collective-permute-done.5.other_ref, ...), custom_call_target="tpu_custom_call" | custom-call | tf_op jit(solution)/shard_map/pallas_call | solution.py:228
  142.1 5.3 %collective-permute-start.6 = (f32[1,128,128]{2,1,0:T(8,128)S(1)}, f32[1,128,128]{2,1,0:T(8,128)S(1)}, u32[]{:S(2)}, u32[]{:S(2)}) collective-permute-start(f32[1,128,128]{2,1,0:T(8,128)S(1)} %get-tuple-element.66.own_ref), channel_id=1, source_target_pairs={{0,384},{4,388},{8,392},{12,396},{16,400},{20,404},{24,408},{28,41... | collective-permute-start | bytes 196616 | tf_op jit(solution)/shard_map/ppermute | solution.py:199
  147.4 4.8 %collective-permute-done.6.other_ref = f32[1,128,128]{2,1,0:T(8,128)S(1)} collective-permute-done((f32[1,128,128]{2,1,0:T(8,128)S(1)}, f32[1,128,128]{2,1,0:T(8,128)S(1)}, u32[]{:S(2)}, u32[]{:S(2)}) %collective-permute-start.6) | collective-permute-done | bytes 65568 | tf_op jit(solution)/shard_map/ppermute | solution.py:199
  152.2 2.9 %shard_map.54 = (f32[128,128]{1,0:T(8,128)S(1)}, f32[128,128]{1,0:T(8,128)S(1)}) custom-call(s32[1]{0:T(128)} %bitcast.8.side_ref, f32[1,128,128]{2,1,0:T(8,128)S(1)} %get-tuple-element.66.own_ref, f32[1,128,128]{2,1,0:T(8,128)S(1)} %collective-permute-done.6.other_ref, f32[128,128]{1,0:T(8,128)S(1)} %get-tuple-element.67.panel_ref, ...), custom_call_target="tpu_custom_call" | custom-call | tf_op jit(solution)/shard_map/pallas_call | solution.py:228
  155.1 19.0 %shard_map.55 = f32[7,32,128]{2,1,0:T(8,128)} custom-call(s32[1]{0:T(128)} %bitcast.rep_ref, f32[128,128]{1,0:T(8,128)S(1)} %get-tuple-element.45.refs_0_, f32[128,128]{1,0:T(8,128)S(1)} %get-tuple-element.49.refs_1_, f32[128,128]{1,0:T(8,128)S(1)} %get-tuple-element.53.refs_2_, f32[128,128]{1,0:T(8,128)S(1)} %get-tuple-element.57.refs_3_, ...), custom_call_target="tpu_custom_call" | custom-call | tf_op jit(solution)/shard_map/pallas_call | solution.py:234
  (1 shorter events, 0.0 us)
Async XLA Ops:
  6.5 2.3 %copy-start.2 = (s32[8,4]{0,1:T(4,128)S(1)}, s32[8,4]{0,1:T(4,128)}, u32[]{:S(2)}) copy-start(s32[8,4]{0,1:T(4,128)} %param.6) | copy-start | bytes 388
  6.5 2.4 %copy-start.1 = (s32[1,512]{1,0:T(1,128)S(1)}, s32[1,512]{1,0:T(1,128)}, u32[]{:S(2)}) copy-start(s32[1,512]{1,0:T(1,128)} %order_ref.1) | copy-start | bytes 6148
  6.5 43.5 %all-gather.3.cloned.1.call-start = ((), (), s32[]{:S(2)}) async-start(), calls=%async_computation | async-start | bytes 2293760 | tf_op jit(solution)/shard_map/all_gather | solution.py:206
  50.0 1.5 copy-start
  56.4 3.7 %collective-permute-start = (f32[7,128,128]{2,1,0:T(8,128)S(1)}, f32[7,128,128]{2,1,0:T(8,128)S(1)}, u32[]{:S(2)}, u32[]{:S(2)}) collective-permute-start(f32[7,128,128]{2,1,0:T(8,128)S(1)} %get-tuple-element.43.own_ref), channel_id=1, source_target_pairs={{0,4},{4,0},{8,12},{12,8},{16,20},{20,16},{24,28},{28,24},{32,36},... | collective-permute-start | bytes 1376264 | tf_op jit(solution)/shard_map/ppermute | solution.py:199
  63.2 13.1 %collective-permute-start.1 = (f32[6,128,128]{2,1,0:T(8,128)S(1)}, f32[6,128,128]{2,1,0:T(8,128)S(1)}, u32[]{:S(2)}, u32[]{:S(2)}) collective-permute-start(f32[6,128,128]{2,1,0:T(8,128)S(1)} %get-tuple-element.46.own_ref), channel_id=1, source_target_pairs={{0,8},{4,12},{8,0},{12,4},{16,24},{20,28},{24,16},{28,20},{32,40},... | collective-permute-start | bytes 1179656 | tf_op jit(solution)/shard_map/ppermute | solution.py:199
  79.8 12.0 %collective-permute-start.2 = (f32[5,128,128]{2,1,0:T(8,128)S(1)}, f32[5,128,128]{2,1,0:T(8,128)S(1)}, u32[]{:S(2)}, u32[]{:S(2)}) collective-permute-start(f32[5,128,128]{2,1,0:T(8,128)S(1)} %get-tuple-element.50.own_ref), channel_id=1, source_target_pairs={{0,24},{4,28},{8,16},{12,20},{16,8},{20,12},{24,0},{28,4},{32,56},... | collective-permute-start | bytes 983048 | tf_op jit(solution)/shard_map/ppermute | solution.py:199
  95.4 8.8 %collective-permute-start.3 = (f32[4,128,128]{2,1,0:T(8,128)S(1)}, f32[4,128,128]{2,1,0:T(8,128)S(1)}, u32[]{:S(2)}, u32[]{:S(2)}) collective-permute-start(f32[4,128,128]{2,1,0:T(8,128)S(1)} %get-tuple-element.54.own_ref), channel_id=1, source_target_pairs={{0,32},{4,36},{8,40},{12,44},{16,48},{20,52},{24,56},{28,60},{32,0... | collective-permute-start | bytes 786440 | tf_op jit(solution)/shard_map/ppermute | solution.py:199
  107.7 9.5 %collective-permute-start.4 = (f32[3,128,128]{2,1,0:T(8,128)S(1)}, f32[3,128,128]{2,1,0:T(8,128)S(1)}, u32[]{:S(2)}, u32[]{:S(2)}) collective-permute-start(f32[3,128,128]{2,1,0:T(8,128)S(1)} %get-tuple-element.58.own_ref), channel_id=1, source_target_pairs={{0,96},{4,100},{8,104},{12,108},{16,112},{20,116},{24,120},{28,124... | collective-permute-start | bytes 589832 | tf_op jit(solution)/shard_map/ppermute | solution.py:199
  120.7 17.8 %collective-permute-start.5 = (f32[2,128,128]{2,1,0:T(8,128)S(1)}, f32[2,128,128]{2,1,0:T(8,128)S(1)}, u32[]{:S(2)}, u32[]{:S(2)}) collective-permute-start(f32[2,128,128]{2,1,0:T(8,128)S(1)} %get-tuple-element.62.own_ref), channel_id=1, source_target_pairs={{0,128},{4,132},{8,136},{12,140},{16,144},{20,148},{24,152},{28,15... | collective-permute-start | bytes 393224 | tf_op jit(solution)/shard_map/ppermute | solution.py:199
  142.1 10.1 %collective-permute-start.6 = (f32[1,128,128]{2,1,0:T(8,128)S(1)}, f32[1,128,128]{2,1,0:T(8,128)S(1)}, u32[]{:S(2)}, u32[]{:S(2)}) collective-permute-start(f32[1,128,128]{2,1,0:T(8,128)S(1)} %get-tuple-element.66.own_ref), channel_id=1, source_target_pairs={{0,384},{4,388},{8,392},{12,396},{16,400},{20,404},{24,408},{28,41... | collective-permute-start | bytes 196616 | tf_op jit(solution)/shard_map/ppermute | solution.py:199
Sparse Core Ops, SparseCore 0:
  9.5 40.5 all-gather.2

commit v2 on v1

--- a/solution.py
+++ b/solution.py
@@ -49,25 +49,44 @@
         out[...] = contract(moved, select, ((1,), (1,))).astype(BF16)
 
 
-def panel_kernel(basis_ref, high_ref, low_ref, out_ref, first_ref):
-    reps, levels, narrow, rows = basis_ref.shape
+def panel_kernel(rep_ref, own_ref, *refs):
+    reps = len(refs) - 3
+    pieces, (high_ref, low_ref, out_ref, basis_scr) = (own_ref, *refs[: reps - 1]), refs[reps - 1:]
+    own_levels, narrow, rows = own_ref.shape
     scale = 1.0 / math.sqrt(rows)
     width = reps * narrow
-    for level in range(levels):
-        basis = parts(basis_ref[:, level].reshape(width, rows))
+    rep = rep_ref[0]
+    for shift, piece in enumerate(pieces):
+        source = lax.rem(rep + reps - shift, reps)
+        basis_scr[:, pl.ds(pl.multiple_of(source * narrow, narrow), narrow), :] = piece[...]
+    panels = []
+    for level in range(own_levels):
+        basis = parts(basis_scr[level])
         image = product(basis, (high_ref[...], low_ref[...]))
-        panel = product(parts(image), basis, ((1,), (1,))) * scale
-        if level == 0:
-            first_ref[...] = panel
-            pair = parts(panel)
-            panel = product(pair, pair, ((0,), (0,))) * (1.0 / width)
-        out_ref[level] = panel
-
-
-def level_kernel(last, side_ref, own_ref, other_ref, panel_ref, q_ref, *outs):
-    width = panel_ref.shape[0]
+        panels.append(product(parts(image), basis, ((1,), (1,))) * scale)
+    pair = parts(panels[0])
+    first = product(pair, pair, ((0,), (0,))) * (1.0 / width)
+    out_ref[0] = panels[0]
+    out_ref[1] = jnp.where(rep == 0, first, panels[1])
+
+
+def level_kernel(first, last, side_ref, own_ref, pair_ref, *refs):
+    width = own_ref.shape[1]
     eye = identity(width)
-    own, other = own_ref[0], other_ref[0]
+    side = side_ref[0]
+    skip = 1 if first else 0
+    if first:
+        panel, q, outs = own_ref[0], eye, refs
+    else:
+        panel, q, outs = refs[0][...], refs[1][...], refs[2:]
+
+    def theirs(n):
+        return pair_ref[1 - side, n]
+
+    def ours(n):
+        return own_ref[n + skip]
+
+    own, other = ours(0), theirs(0)
     total = own + other
     bound = 1.0 + 2.0 * jnp.max(jnp.sum(jnp.abs(total), axis=0))
     if last:
@@ -99,24 +118,33 @@
         x = parts(inverse)
         residual = parts(eye - product(pair, x))
         final.append(inverse + product(x, residual))
-    panel = parts(panel_ref[...])
+    panel = parts(panel)
     if not last:
         c_ref, pg_ref, next_panel_ref, next_q_ref, next_ref = outs
         root_half = math.sqrt(0.5)
-        next_panel = (own_ref[1] + other_ref[1]) * root_half
+        next_panel = (ours(1) + theirs(1)) * root_half
         next_panel_ref[...] = next_panel
         pair = parts(next_panel)
         half = parts(0.5 * (eye + final[0]))
         next_ref[0] = product(pair, parts(product(half, pair)), ((0,), (0,))) * (1.0 / width)
         next_q_ref[...] = 2.0 * eye - final[1]
         for upper in range(1, next_ref.shape[0]):
-            next_ref[upper] = (own_ref[upper + 1] + other_ref[upper + 1]) * root_half
+            next_ref[upper] = (ours(upper + 1) + theirs(upper + 1)) * root_half
     else:
         c_ref, pg_ref = outs
-    gain = parts(jnp.where(side_ref[0] == 1, final[-1], eye))
+    gain = parts(jnp.where(side == 1, final[-1], eye))
     pg = product(panel, gain)
     pg_ref[...] = pg
-    c_ref[...] = q_ref[...] + product(parts(pg), panel, ((1,), (1,))) * (1.0 / width)
+    c_ref[...] = q + product(parts(pg), panel, ((1,), (1,))) * (1.0 / width)
+
+
+def spread(x):
+    return jnp.broadcast_to(x, (8, 128))
+
+
+def reciprocal(x):
+    guess = pl.reciprocal(x, approx=True)
+    return guess * (2.0 - x * guess)
 
 
 def whiten_kernel(rep_ref, *refs):
@@ -132,22 +160,30 @@
     for top in range(0, width, PANEL):
         left = [[s[8 * j:8 * j + 8, :width] for j in range(count)] for s in state]
         right = [[s[8 * j:8 * j + 8, width:] for j in range(count)] for s in state]
-        for kk in range(PANEL):
+        for kk in range(0, PANEL, 2):
             k, block, row = top + kk, kk // 8, kk % 8
             for m in range(levels):
                 v, w = left[m], right[m]
-                line = jnp.broadcast_to(v[block][row:row + 1], (8, width))
-                line_x = jnp.broadcast_to(w[block][row:row + 1], (8, width))
-                pivot = jnp.broadcast_to(line[:, k:k + 1], (8, width))
-                inverse = 1.0 / pivot
+                line0, line1 = spread(v[block][row:row + 1]), spread(v[block][row + 1:row + 2])
+                line0_x, line1_x = spread(w[block][row:row + 1]), spread(w[block][row + 1:row + 2])
+                p00, p01 = spread(line0[:, k:k + 1]), spread(line0[:, k + 1:k + 2])
+                p11 = spread(line1[:, k + 1:k + 2])
+                inverse = reciprocal(p00 * p11 - p01 * p01)
+                i00, i01, i11 = p11 * inverse, p01 * inverse, p00 * inverse
+                ratio = p01 * reciprocal(p00)
                 for j in range(block, count):
-                    if j == block and row == 7:
+                    if j == block and row == 6:
+                        f0 = jnp.where(sub == row + 1, ratio, 0.0)
+                        v[j] = v[j] - f0 * line0
+                        w[j] = w[j] - f0 * line0_x
                         continue
-                    factor = jnp.broadcast_to(v[j][:, k:k + 1], (8, width)) * inverse
+                    c0, c1 = spread(v[j][:, k:k + 1]), spread(v[j][:, k + 1:k + 2])
+                    f0, f1 = i00 * c0 - i01 * c1, i11 * c1 - i01 * c0
                     if j == block:
-                        factor = jnp.where(sub > row, factor, 0.0)
-                    v[j] = v[j] - factor * line
-                    w[j] = w[j] - factor * line_x
+                        f0 = jnp.where(sub > row + 1, f0, jnp.where(sub == row + 1, ratio, 0.0))
+                        f1 = jnp.where(sub > row + 1, f1, 0.0)
+                    v[j] = v[j] - f0 * line0 - f1 * line1
+                    w[j] = w[j] - f0 * line0_x - f1 * line1_x
         for m in range(levels):
             for j in range(count):
                 diagonal = jnp.sum(jnp.where(lane == sub + (top + 8 * j), left[m][j], 0.0), axis=1, keepdims=True)
@@ -194,45 +230,58 @@
     return leaf ^ (1 << bit)
 
 
-def swapped(value, axis, bit):
-    pairs = [(source, partner(source, bit)) for source in range(lax.axis_size(axis))]
-    return lax.ppermute(value, axis, pairs)
+def pair_gathered(value, axis, bit):
+    leaves = range(lax.axis_size(axis))
+    groups = [[leaf, partner(leaf, bit)] for leaf in leaves if not leaf >> bit & 1]
+    return lax.all_gather(value, axis, axis=0, axis_index_groups=groups)
 
 
 def local(basis, near_blocks, near_cols, bead_order):
     levels, narrow, rows = basis.shape
     block_rows, per_row = near_cols.shape
     blk = rows // block_rows
-    gathered = lax.all_gather(basis, "rep", axis=0)
-    width = gathered.shape[0] * narrow
+    reps = lax.axis_size("rep")
+    width = reps * narrow
+    leaf_index = lax.axis_index("leaf")
+    rep_index = lax.axis_index("rep")
+    rep_scalar = rep_index.astype(jnp.int32).reshape(1)
     square = jax.ShapeDtypeStruct((width, width), F32)
+
+    def levels_of(rep):
+        return lax.dynamic_slice_in_dim(basis, jnp.maximum(2 * rep - 1, 0), 2, 0)
+
+    pieces = [levels_of(rep_index)]
+    for shift in range(1, reps):
+        pairs = [(source, (source + shift) % reps) for source in range(reps)]
+        pieces.append(lax.ppermute(levels_of(lax.rem(rep_index + shift, reps)), "rep", pairs))
     tiles = near_blocks.reshape(block_rows * per_row, blk, blk)
     dense = [jax.ShapeDtypeStruct((rows, rows), BF16)] * 2
     high, low = call(dense_kernel, dense, 1, 2, [pltpu.VMEM((block_rows, rows, blk), F32)])(
         near_cols, tiles, bead_order
     )
-    sent, panel = call(
-        panel_kernel, [jax.ShapeDtypeStruct((levels, width, width), F32), square], 0, 3
-    )(gathered, high, low)
-    leaf_index = lax.axis_index("leaf")
-    rep_index = lax.axis_index("rep")
-    q = jnp.eye(width, dtype=F32)
+    two = jax.ShapeDtypeStruct((2, width, width), F32)
+    mine = call(panel_kernel, two, 1, reps + 2, [pltpu.VMEM((2, width, rows), F32)])(
+        rep_scalar, *pieces, high, low
+    )
+    sent = lax.all_gather(mine, "rep", axis=0, tiled=True)
+    state = []
     c_list, x_list = [], []
     for bit in range(levels):
-        last = bit == levels - 1
-        received = swapped(sent, "leaf", bit)
+        first, last = bit == 0, bit == levels - 1
+        pair = pair_gathered(sent[1:] if first else sent, "leaf", bit)
         side = (leaf_index >> bit & 1).astype(jnp.int32).reshape(1)
         shapes = [square, square]
         if not last:
             shapes += [square, square, jax.ShapeDtypeStruct((levels - bit - 1, width, width), F32)]
-        outs = call(functools.partial(level_kernel, last), shapes, 1, 4)(side, sent, received, panel, q)
-        c_list.append(outs[0])
-        x_list.append(outs[1])
+        kernel = functools.partial(level_kernel, first, last)
+        c, x, *rest = call(kernel, shapes, 1, 2 + len(state))(side, sent, pair, *state)
+        c_list.append(c)
+        x_list.append(x)
         if not last:
-            panel, q, sent = outs[2:]
+            *state, sent = rest
     out = jax.ShapeDtypeStruct((levels, narrow, width), F32)
     return call(whiten_kernel, out, 1, 2 * levels, [pltpu.VMEM((levels, width, width), F32)])(
-        rep_index.astype(jnp.int32).reshape(1), *c_list, *x_list
+        rep_scalar, *c_list, *x_list
     )
 
 

time: 181 us -> 137 us (0.76)
  waiting for transfers between devices: 84.1 us -> 0.01 us
  blocking collectives: 0 us -> 82.3 us
  starting transfers between devices: 30.2 us -> 11.4 us
  between operations: 13.6 us -> 0.16 us
  Pallas kernels: 49.9 us -> 39.4 us
    all_gather x0 -> x8, blocking collectives: none -> 82.3 us  [the longest x7 68.9 us: pair_gathered(): return lax.all_gather(value, axis, axis=0, axis_index_groups=groups)]
    ppermute x7 -> x3, waiting for transfers between devices: 44.6 us -> 0.01 us  [local(): lax.ppermute(levels_of(lax.rem(rep_index + shift, reps)), 'rep', pairs)]
    all_gather x1 -> x0, waiting for transfers between devices: 38.8 us -> none  [local(): gathered = lax.all_gather(basis, 'rep', axis=0)]
    ppermute x7 -> x3, starting transfers between devices: 30.2 us -> 11.4 us  [local(): lax.ppermute(levels_of(lax.rem(rep_index + shift, reps)), 'rep', pairs)]
    pallas_call x1, Pallas kernels: 19 us -> 13 us  [local(): call(whiten_kernel, out, 1, 2 * levels, [pltpu.VMEM((levels, width, width...]
    pallas_call x8, Pallas kernels: 28.5 us -> 24.1 us  [the longest x7 22.9 us: local(): call(kernel, shapes, 1, 2 + len(state))(side, sent, pair, *state)]
  transfers between devices with their start and end apart: 8 -> 3, of which waited for: 8 -> 0; matrix products, arithmetic and copies ran while one was open for 1% -> 0% of each run, Pallas kernels for 1% -> 2%
where the time goes in v2:
time: 137 us; the launch traced here: 136 us
  blocking collectives  82.3 us (60%)
  Pallas kernels  39.4 us (29%)
  starting transfers between devices  11.4 us (8%)
  local copies, waits for them, and re-layouts  2.67 us (2%)
    all_gather x7, blocking collectives, pair_gathered(): return lax.all_gather(value, axis, axis=0, axis_index_groups=groups)  68.9 us
    pallas_call x7, Pallas kernels, local(): call(kernel, shapes, 1, 2 + len(state))(side, sent, pair, *state)  22.9 us
    all_gather x1, blocking collectives, local(): sent = lax.all_gather(mine, 'rep', axis=0, tiled=True)  13.4 us
    pallas_call x1, Pallas kernels, local(): call(whiten_kernel, out, 1, 2 * levels, [pltpu.VMEM((levels, width, width...  13 us
    ppermute x3, starting transfers between devices, local(): lax.ppermute(levels_of(lax.rem(rep_index + shift, reps)), 'rep', pairs)  11.4 us
  transfers between devices with their start and end apart: 3, of which 0 were waited for; matrix products, arithmetic and copies ran while one was open for 0% of the time, Pallas kernels for 2%

profile of v2, /device:TPU:24, one launch (start us, length us, event | category | flops | bytes accessed | tf_op | source)
XLA Modules:
  0.0 135.9 jit_solution(14208812517929373636)
XLA Ops:
  0.0 0.0 copy-start.1
  0.0 1.2 constant_dynamic-slice_fusion
  1.2 3.4 %collective-permute-start = (f32[2,32,512]{2,1,0:T(8,128)S(1)}, f32[2,32,512]{2,1,0:T(8,128)S(1)}, u32[]{:S(2)}, u32[]{:S(2)}) collective-permute-start(f32[2,32,512]{2,1,0:T(8,128)S(1)} %get-tuple-element.74), channel_id=1, source_target_pairs={{0,1},{1,2},{2,3},{3,0},{4,5},{5,6},{6,7},{7,4},{8,9},{9,10},{10,1... | collective-permute-start | bytes 393224 | tf_op jit(solution)/shard_map/ppermute | solution.py:256
  4.6 4.6 %collective-permute-start.1 = (f32[2,32,512]{2,1,0:T(8,128)S(1)}, f32[2,32,512]{2,1,0:T(8,128)S(1)}, u32[]{:S(2)}, u32[]{:S(2)}) collective-permute-start(f32[2,32,512]{2,1,0:T(8,128)S(1)} %get-tuple-element.76), channel_id=1, source_target_pairs={{0,2},{1,3},{2,0},{3,1},{4,6},{5,7},{6,4},{7,5},{8,10},{9,11},{10,... | collective-permute-start | bytes 393224 | tf_op jit(solution)/shard_map/ppermute | solution.py:256
  9.3 3.3 %collective-permute-start.2 = (f32[2,32,512]{2,1,0:T(8,128)S(1)}, f32[2,32,512]{2,1,0:T(8,128)S(1)}, u32[]{:S(2)}, u32[]{:S(2)}) collective-permute-start(f32[2,32,512]{2,1,0:T(8,128)S(1)} %get-tuple-element.73), channel_id=1, source_target_pairs={{0,3},{1,0},{2,1},{3,2},{4,7},{5,4},{6,5},{7,6},{8,11},{9,8},{10,9... | collective-permute-start | bytes 393224 | tf_op jit(solution)/shard_map/ppermute | solution.py:256
  12.6 0.0 copy-done.1
  12.6 0.0 copy-start.2
  12.6 0.5 reshape.29.blocks_ref
  13.2 0.1 copy-done.2
  13.3 0.1 copy.6.cols_ref
  13.4 0.0 copy-start
  13.4 0.7 copy-done
  14.1 2.3 %shard_map.46 = (bf16[512,512]{1,0:T(8,128)(2,1)S(1)}, bf16[512,512]{1,0:T(8,128)(2,1)S(1)}) custom-call(s32[8,4]{1,0:T(8,128)S(1)} %copy.6.cols_ref, f32[32,64,64]{2,1,0:T(8,128)S(1)} %reshape.29.blocks_ref, s32[1,512]{1,0:T(1,128)S(1)} %copy-done), custom_call_target="tpu_custom_call" | custom-call | tf_op jit(solution)/shard_map/pallas_call | solution.py:259
  16.4 0.0 collective-permute-done.refs_0_
  16.4 0.0 collective-permute-done.1.refs_1_
  16.4 0.0 collective-permute-done.2.refs_2_
  16.4 1.2 shard_map.47
  17.7 13.4 %all_gather.45.own_ref = f32[8,128,128]{2,1,0:T(8,128)S(1)} all-gather(f32[2,128,128]{2,1,0:T(8,128)S(1)} %shard_map.47), channel_id=1, replica_groups=mesh['leaf'=128,'rep'=4] {'rep'}, dimensions={0}, use_global_device_ids=true | all-gather | bytes 655360 | tf_op jit(solution)/shard_map/all_gather | solution.py:266
  31.1 2.5 %all-gather = f32[14,128,128]{2,1,0:T(8,128)S(1)} all-gather(f32[7,128,128]{2,1,0:T(8,128)S(1)} %slice.4), channel_id=2, replica_groups={{0,4},{8,12},{16,20},{24,28},{32,36},{40,44},{48,52},{56,60},{64,68},{7..., dimensions={0}, use_global_device_ids=true | all-gather | bytes 1376256 | tf_op jit(solution)/shard_map/all_gather | solution.py:236
  33.5 3.5 %shard_map.48 = (f32[128,128]{1,0:T(8,128)S(1)}, f32[128,128]{1,0:T(8,128)S(1)}, f32[128,128]{1,0:T(8,128)S(1)}, f32[128,128]{1,0:T(8,128)S(1)}, f32[6,128,128]{2,1,0:T(8,128)S(1)}) custom-call(s32[1]{0:T(128)} %bitcast.1.side_ref, f32[8,128,128]{2,1,0:T(8,128)S(1)} %all_gather.45.own_ref, f32[2,7,128,128]{3,2,1,0:T(8,128)S(1)} %bitcast.15), custom_call_target="tpu_custom_call" | custom-call | tf_op jit(solution)/shard_map/pallas_call | solution.py:277
  37.1 11.8 %all-gather.1 = f32[12,128,128]{2,1,0:T(8,128)S(1)} all-gather(f32[6,128,128]{2,1,0:T(8,128)S(1)} %get-tuple-element.42.own_ref), channel_id=3, replica_groups={{0,8},{4,12},{16,24},{20,28},{32,40},{36,44},{48,56},{52,60},{64,72},{6..., dimensions={0}, use_global_device_ids=true | all-gather | bytes 1179648 | tf_op jit(solution)/shard_map/all_gather | solution.py:236
  48.9 3.5 %shard_map.49 = (f32[128,128]{1,0:T(8,128)S(1)}, f32[128,128]{1,0:T(8,128)S(1)}, f32[128,128]{1,0:T(8,128)S(1)}, f32[128,128]{1,0:T(8,128)S(1)}, f32[5,128,128]{2,1,0:T(8,128)S(1)}) custom-call(s32[1]{0:T(128)} %bitcast.3.side_ref, f32[6,128,128]{2,1,0:T(8,128)S(1)} %get-tuple-element.42.own_ref, f32[2,6,128,128]{3,2,1,0:T(8,128)S(1)} %bitcast.16, ...), custom_call_target="tpu_custom_call" | custom-call | tf_op jit(solution)/shard_map/pallas_call | solution.py:277
  52.5 11.1 %all-gather.2 = f32[10,128,128]{2,1,0:T(8,128)S(1)} all-gather(f32[5,128,128]{2,1,0:T(8,128)S(1)} %get-tuple-element.46.own_ref), channel_id=4, replica_groups={{0,24},{4,28},{8,16},{12,20},{32,56},{36,60},{40,48},{44,52},{64,88},{6..., dimensions={0}, use_global_device_ids=true | all-gather | bytes 983040 | tf_op jit(solution)/shard_map/all_gather | solution.py:236
  63.6 3.5 %shard_map.50 = (f32[128,128]{1,0:T(8,128)S(1)}, f32[128,128]{1,0:T(8,128)S(1)}, f32[128,128]{1,0:T(8,128)S(1)}, f32[128,128]{1,0:T(8,128)S(1)}, f32[4,128,128]{2,1,0:T(8,128)S(1)}) custom-call(s32[1]{0:T(128)} %bitcast.5.side_ref, f32[5,128,128]{2,1,0:T(8,128)S(1)} %get-tuple-element.46.own_ref, f32[2,5,128,128]{3,2,1,0:T(8,128)S(1)} %bitcast.17, ...), custom_call_target="tpu_custom_call" | custom-call | tf_op jit(solution)/shard_map/pallas_call | solution.py:277
  67.1 7.6 %all-gather.3 = f32[8,128,128]{2,1,0:T(8,128)S(1)} all-gather(f32[4,128,128]{2,1,0:T(8,128)S(1)} %get-tuple-element.50.own_ref), channel_id=5, replica_groups={{0,32},{4,36},{8,40},{12,44},{16,48},{20,52},{24,56},{28,60},{64,96},{6..., dimensions={0}, use_global_device_ids=true | all-gather | bytes 786432 | tf_op jit(solution)/shard_map/all_gather | solution.py:236
  74.7 3.1 %shard_map.51 = (f32[128,128]{1,0:T(8,128)S(1)}, f32[128,128]{1,0:T(8,128)S(1)}, f32[128,128]{1,0:T(8,128)S(1)}, f32[128,128]{1,0:T(8,128)S(1)}, f32[3,128,128]{2,1,0:T(8,128)S(1)}) custom-call(s32[1]{0:T(128)} %bitcast.7.side_ref, f32[4,128,128]{2,1,0:T(8,128)S(1)} %get-tuple-element.50.own_ref, f32[2,4,128,128]{3,2,1,0:T(8,128)S(1)} %bitcast.18, ...), custom_call_target="tpu_custom_call" | custom-call | tf_op jit(solution)/shard_map/pallas_call | solution.py:277
  77.8 8.4 %all-gather.4 = f32[6,128,128]{2,1,0:T(8,128)S(1)} all-gather(f32[3,128,128]{2,1,0:T(8,128)S(1)} %get-tuple-element.54.own_ref), channel_id=6, replica_groups={{0,96},{4,100},{8,104},{12,108},{16,112},{20,116},{24,120},{28,124},{32..., dimensions={0}, use_global_device_ids=true | all-gather | bytes 589824 | tf_op jit(solution)/shard_map/all_gather | solution.py:236
  86.2 3.5 %shard_map.52 = (f32[128,128]{1,0:T(8,128)S(1)}, f32[128,128]{1,0:T(8,128)S(1)}, f32[128,128]{1,0:T(8,128)S(1)}, f32[128,128]{1,0:T(8,128)S(1)}, f32[2,128,128]{2,1,0:T(8,128)S(1)}) custom-call(s32[1]{0:T(128)} %bitcast.9.side_ref, f32[3,128,128]{2,1,0:T(8,128)S(1)} %get-tuple-element.54.own_ref, f32[2,3,128,128]{3,2,1,0:T(8,128)S(1)} %bitcast.19, ...), custom_call_target="tpu_custom_call" | custom-call | tf_op jit(solution)/shard_map/pallas_call | solution.py:277
  89.8 18.6 %all-gather.5 = f32[4,128,128]{2,1,0:T(8,128)S(1)} all-gather(f32[2,128,128]{2,1,0:T(8,128)S(1)} %get-tuple-element.58.own_ref), channel_id=7, replica_groups={{0,128},{4,132},{8,136},{12,140},{16,144},{20,148},{24,152},{28,156},{3..., dimensions={0}, use_global_device_ids=true | all-gather | bytes 393216 | tf_op jit(solution)/shard_map/all_gather | solution.py:236
  108.3 3.1 %shard_map.53 = (f32[128,128]{1,0:T(8,128)S(1)}, f32[128,128]{1,0:T(8,128)S(1)}, f32[128,128]{1,0:T(8,128)S(1)}, f32[128,128]{1,0:T(8,128)S(1)}, f32[1,128,128]{2,1,0:T(8,128)S(1)}) custom-call(s32[1]{0:T(128)} %bitcast.11.side_ref, f32[2,128,128]{2,1,0:T(8,128)S(1)} %get-tuple-element.58.own_ref, f32[2,2,128,128]{3,2,1,0:T(8,128)S(1)} %bitcast.20, ...), custom_call_target="tpu_custom_call" | custom-call | tf_op jit(solution)/shard_map/pallas_call | solution.py:277
  111.4 9.0 %all-gather.6 = f32[2,128,128]{2,1,0:T(8,128)S(1)} all-gather(f32[1,128,128]{2,1,0:T(8,128)S(1)} %get-tuple-element.62.own_ref), channel_id=8, replica_groups={{0,384},{4,388},{8,392},{12,396},{16,400},{20,404},{24,408},{28,412},{3..., dimensions={0}, use_global_device_ids=true | all-gather | bytes 196608 | tf_op jit(solution)/shard_map/all_gather | solution.py:236
  120.4 2.6 %shard_map.54 = (f32[128,128]{1,0:T(8,128)S(1)}, f32[128,128]{1,0:T(8,128)S(1)}) custom-call(s32[1]{0:T(128)} %bitcast.13.side_ref, f32[1,128,128]{2,1,0:T(8,128)S(1)} %get-tuple-element.62.own_ref, f32[2,1,128,128]{3,2,1,0:T(8,128)S(1)} %bitcast.21, f32[128,128]{1,0:T(8,128)S(1)} %get-tuple-element.63.refs_0_, f32[128,128]{1,0:T(8,128)S(1)} %get-tuple-element.64.refs_1_), custom_call_target="tpu_custom_call" | custom-call | tf_op jit(solution)/shard_map/pallas_call | solution.py:277
  123.0 13.0 %shard_map.55 = f32[7,32,128]{2,1,0:T(8,128)} custom-call(s32[1]{0:T(128)} %bitcast.rep_ref, f32[128,128]{1,0:T(8,128)S(1)} %get-tuple-element.41.refs_0_, f32[128,128]{1,0:T(8,128)S(1)} %get-tuple-element.45.refs_1_, f32[128,128]{1,0:T(8,128)S(1)} %get-tuple-element.49.refs_2_, f32[128,128]{1,0:T(8,128)S(1)} %get-tuple-element.53.refs_3_, ...), custom_call_target="tpu_custom_call" | custom-call | tf_op jit(solution)/shard_map/pallas_call | solution.py:283
  (1 shorter events, 0.0 us)
Async XLA Ops:
  0.0 12.6 %copy-start.1 = (f32[8,4,4096]{2,1,0:T(4,128)S(1)}, f32[8,4,4096]{2,1,0:T(4,128)}, u32[]{:S(2)}) copy-start(f32[8,4,4096]{2,1,0:T(4,128)} %param.5) | copy-start | bytes 1572868
  1.2 15.2 %collective-permute-start = (f32[2,32,512]{2,1,0:T(8,128)S(1)}, f32[2,32,512]{2,1,0:T(8,128)S(1)}, u32[]{:S(2)}, u32[]{:S(2)}) collective-permute-start(f32[2,32,512]{2,1,0:T(8,128)S(1)} %get-tuple-element.74), channel_id=1, source_target_pairs={{0,1},{1,2},{2,3},{3,0},{4,5},{5,6},{6,7},{7,4},{8,9},{9,10},{10,1... | collective-permute-start | bytes 393224 | tf_op jit(solution)/shard_map/ppermute | solution.py:256
  4.6 11.8 %collective-permute-start.1 = (f32[2,32,512]{2,1,0:T(8,128)S(1)}, f32[2,32,512]{2,1,0:T(8,128)S(1)}, u32[]{:S(2)}, u32[]{:S(2)}) collective-permute-start(f32[2,32,512]{2,1,0:T(8,128)S(1)} %get-tuple-element.76), channel_id=1, source_target_pairs={{0,2},{1,3},{2,0},{3,1},{4,6},{5,7},{6,4},{7,5},{8,10},{9,11},{10,... | collective-permute-start | bytes 393224 | tf_op jit(solution)/shard_map/ppermute | solution.py:256
  9.3 7.2 %collective-permute-start.2 = (f32[2,32,512]{2,1,0:T(8,128)S(1)}, f32[2,32,512]{2,1,0:T(8,128)S(1)}, u32[]{:S(2)}, u32[]{:S(2)}) collective-permute-start(f32[2,32,512]{2,1,0:T(8,128)S(1)} %get-tuple-element.73), channel_id=1, source_target_pairs={{0,3},{1,0},{2,1},{3,2},{4,7},{5,4},{6,5},{7,6},{8,11},{9,8},{10,9... | collective-permute-start | bytes 393224 | tf_op jit(solution)/shard_map/ppermute | solution.py:256
  12.6 0.7 copy-start.2
  13.4 0.7 copy-start

commit v3 on v2

v3 whole, which is shorter than its diff:
```python
import functools
import math

import jax
import jax.numpy as jnp
from jax import lax
from jax.experimental import pallas as pl
from jax.experimental.pallas import tpu as pltpu
from jax.sharding import PartitionSpec as P

F32 = jnp.float32
BF16 = jnp.bfloat16
PANEL = 32
EXCHANGE = ("pair",) * 7
VMEM_BYTES = 48 * 1024 * 1024


def parts(x):
    high = x.astype(BF16)
    return high, (x - high.astype(F32)).astype(BF16)


def contract(a, b, dims):
    return lax.dot_general(a, b, (dims, ((), ())), preferred_element_type=F32)


def product(a, b, dims=((1,), (0,))):
    return contract(a[0], b[0], dims) + (contract(a[0], b[1], dims) + contract(a[1], b[0], dims))


def identity(n):
    rows = lax.broadcasted_iota(jnp.int32, (n, n), 0)
    return (rows == lax.broadcasted_iota(jnp.int32, (n, n), 1)).astype(F32)


def dense_kernel(cols_ref, blocks_ref, order_ref, high_ref, low_ref, columns):
    block_rows, per_row = cols_ref.shape
    blk = blocks_ref.shape[1]
    rows = block_rows * blk
    columns[...] = jnp.zeros_like(columns)
    for q in range(block_rows):
        for n in range(per_row):
            where = (cols_ref[q, n], slice(q * blk, (q + 1) * blk))
            columns[where] = columns[where] + blocks_ref[q * per_row + n]
    tree = jnp.concatenate([columns[c] for c in range(block_rows)], axis=1)
    bead = lax.broadcasted_iota(jnp.int32, (rows, rows), 0)
    select = (bead == order_ref[...]).astype(F32).astype(BF16)
    for piece, out in zip(parts(tree), (high_ref, low_ref)):
        moved = contract(select, piece, ((1,), (0,))).astype(BF16)
        out[...] = contract(moved, select, ((1,), (1,))).astype(BF16)


def panel_kernel(rep_ref, own_ref, *refs):
    reps = len(refs) - 3
    pieces, (high_ref, low_ref, out_ref, basis_scr) = (own_ref, *refs[: reps - 1]), refs[reps - 1:]
    own_levels, narrow, rows = own_ref.shape
    scale = 1.0 / math.sqrt(rows)
    width = reps * narrow
    rep = rep_ref[0]
    for shift, piece in enumerate(pieces):
        source = lax.rem(rep + reps - shift, reps)
        basis_scr[:, pl.ds(pl.multiple_of(source * narrow, narrow), narrow), :] = piece[...]
    panels = []
    for level in range(own_levels):
        basis = parts(basis_scr[level])
        image = product(basis, (high_ref[...], low_ref[...]))
        panels.append(product(parts(image), basis, ((1,), (1,))) * scale)
    pair = parts(panels[0])
    first = product(pair, pair, ((0,), (0,))) * (1.0 / width)
    out_ref[0] = panels[0]
    out_ref[1] = jnp.where(rep == 0, first, panels[1])


def level_kernel(first, last, kind, split, side_ref, core_ref, own_ref, pair_ref, *refs):
    width = own_ref.shape[1]
    eye = identity(width)
    side = side_ref[0]
    skip = 1 if first else 0
    if first:
        panel, outs = own_ref[0], refs
    else:
        panel, outs = refs[0][...], refs[1:]

    def theirs(n):
        if kind == "other":
            return pair_ref[n]
        if kind == "pair":
            return pair_ref[1 - side, n]
        if kind == "halfother":
            return jnp.concatenate([pair_ref[core, n] for core in range(2)], axis=0)
        return jnp.concatenate([pair_ref[core, 1 - side, n] for core in range(2)], axis=0)

    def ours(n):
        return own_ref[n + skip]

    own, other = ours(0), theirs(0)
    total = own + other
    bound = 1.0 + 2.0 * jnp.max(jnp.sum(jnp.abs(total), axis=0))
    if last:
        matrices = [eye + other]
    else:
        matrices = [eye + other, eye + total, eye + 2.0 * total]
        root_half = math.sqrt(0.5)
        next_panel = (ours(1) + theirs(1)) * root_half
    step = 2.0 / (bound + 1.0)
    start = ((bound - 1.0) / (bound + 1.0), tuple((step * eye, eye - step * matrix) for matrix in matrices))

    def go_on(carry):
        return carry[0] > 1e-2

    def refine(carry):
        rho, inverses = carry
        scale = 2.0 / (2.0 - rho * rho)
        new = []
        for inverse, residual in inverses:
            e = parts(residual)
            better = scale * (inverse + product(parts(inverse), e))
            new.append((better, (1.0 - scale) * eye + scale * product(e, e)))
        return (rho * rho / (2.0 - rho * rho), tuple(new))

    _, inverses = lax.while_loop(go_on, refine, start)
    pairs = [parts(matrix) for matrix in matrices]

    def correct(_, found):
        new = []
        for inverse, pair in zip(found, pairs):
            x = parts(inverse)
            new.append(inverse + product(x, parts(eye - product(pair, x))))
        return tuple(new)

    extra = jnp.where(bound > 200.0, 3, 0)
    inverses = lax.fori_loop(0, extra, correct, tuple(inverse for inverse, _ in inverses))
    x = [parts(inverse) for inverse in inverses]
    residuals = [parts(eye - product(pair, inverse)) for pair, inverse in zip(pairs, x)]
    if not last:
        next_panel_ref, next_q_ref, next_ref = outs[1:4]
        p = parts(next_panel)
        r = residuals[2]
        y = product(x[2], p)
        ry, rp = product(r, parts(y)), product(r, p)
        sum_y = next_panel + y
        plain = product(p, parts(sum_y), ((0,), (0,)))
        bent = product(parts(ry), parts(next_panel + rp), ((0,), (0,)))
        next_ref[0] = (plain + bent) * (0.5 / width)
        next_panel_ref[...] = next_panel
        for upper in range(1, next_ref.shape[0]):
            next_ref[upper] = (ours(upper + 1) + theirs(upper + 1)) * root_half
        if split:
            half_rows = width // 2
            outs[4][...] = next_ref[:, pl.ds(pl.multiple_of(core_ref[0] * half_rows, half_rows), half_rows), :]
        r = residuals[1]
        both = eye - product(pairs[1], x[1]) + product(r, r)
        next_q_ref[...] = 2.0 * eye - (inverses[1] + product(x[1], parts(both)))
    r = residuals[0]
    v = product(parts(panel), x[0])
    vr = product(parts(v), r)
    gained = v + vr + product(parts(vr), r)
    outs[0][...] = jnp.where(side == 1, gained, panel)


def spread(x):
    return jnp.broadcast_to(x, (8, 128))


def reciprocal(x):
    guess = pl.reciprocal(x, approx=True)
    return guess * (2.0 - x * guess)


def eliminate(v, w, k, block, row, sub):
    count = len(v)
    line = [spread(v[block][row + i:row + i + 1]) for i in range(4)]
    line_w = [spread(w[block][row + i:row + i + 1]) for i in range(4)] if w else []
    column = {j: [spread(v[j][:, k + i:k + i + 1]) for i in range(4)] for j in range(block, count)}
    p = {(i, h): spread(column[block][i][row + h:row + h + 1]) for i in range(4) for h in range(i, 4)}
    inverse = reciprocal(p[0, 0] * p[1, 1] - p[0, 1] * p[0, 1])
    i00, i01, i11 = p[1, 1] * inverse, -(p[0, 1] * inverse), p[0, 0] * inverse
    f02, f12 = i00 * p[0, 2] + i01 * p[1, 2], i01 * p[0, 2] + i11 * p[1, 2]
    f03, f13 = i00 * p[0, 3] + i01 * p[1, 3], i01 * p[0, 3] + i11 * p[1, 3]
    s22 = p[2, 2] - (p[0, 2] * f02 + p[1, 2] * f12)
    s23 = p[2, 3] - (p[0, 2] * f03 + p[1, 2] * f13)
    s33 = p[3, 3] - (p[0, 3] * f03 + p[1, 3] * f13)
    inverse = reciprocal(s22 * s33 - s23 * s23)
    j22, j23, j33 = s33 * inverse, -(s23 * inverse), s22 * inverse
    f01, f23 = p[0, 1] * reciprocal(p[0, 0]), s23 * reciprocal(s22)
    for lines in (line, line_w)[:2 if w else 1]:
        lines[2] = lines[2] - f02 * lines[0] - f12 * lines[1]
        lines[3] = lines[3] - f03 * lines[0] - f13 * lines[1]
    for j in range(block, count):
        c = column[j]
        if j > block or row == 0:
            g0, g1 = i00 * c[0] + i01 * c[1], i01 * c[0] + i11 * c[1]
            e2 = c[2] - c[0] * f02 - c[1] * f12
            e3 = c[3] - c[0] * f03 - c[1] * f13
            g2, g3 = j22 * e2 + j23 * e3, j23 * e2 + j33 * e3
        else:
            g0 = g1 = g2 = g3 = 0.0
        if j == block:
            inside = jnp.where(sub == row + 1, f01, jnp.where(sub == row + 2, f02, jnp.where(sub == row + 3, f03, 0.0)))
            g0 = jnp.where(sub > row + 3, g0, inside)
            g1 = jnp.where(sub > row + 3, g1, jnp.where(sub == row + 2, f12, jnp.where(sub == row + 3, f13, 0.0)))
            g2 = jnp.where(sub > row + 3, g2, jnp.where(sub == row + 3, f23, 0.0))
            g3 = jnp.where(sub > row + 3, g3, 0.0)
        v[j] = v[j] - g0 * line[0] - g1 * line[1] - g2 * line[2] - g3 * line[3]
        if w:
            w[j] = w[j] - g0 * line_w[0] - g1 * line_w[1] - g2 * line_w[2] - g3 * line_w[3]


def whiten_kernel(levels, rep_ref, *refs):
    x_refs, p_refs, q_refs = refs[:levels], refs[levels:2 * levels], refs[2 * levels:-1]
    out_ref = refs[-1]
    width = x_refs[0].shape[0]
    narrow = out_ref.shape[1]
    lane = lax.broadcasted_iota(jnp.int32, (8, width), 1)
    sub = lax.broadcasted_iota(jnp.int32, (8, width), 0)
    count = PANEL // 8
    rows = lax.broadcasted_iota(jnp.int32, (width, width), 0)
    lanes = lax.broadcasted_iota(jnp.int32, (width, width), 1)
    select = ((rows == lanes + rep_ref[0] * narrow) & (lanes < narrow)).astype(F32).astype(BF16)
    state, columns = [], []
    for m in range(levels):
        x, p = x_refs[m][...], p_refs[m]
        p = p[0] if len(p.shape) == 3 else p[...]
        q = q_refs[m - 1][...] if m else identity(width)
        pair = parts(x)
        state.append(q + product(pair, parts(p), ((1,), (1,))) * (1.0 / width))
        rest = parts(x - pair[0].astype(F32) - pair[1].astype(F32))[0]
        columns.append(sum(contract(piece, select, ((1,), (0,))) for piece in (*pair, rest)))
    done = [[] for _ in range(levels)]
    for top in range(0, width, PANEL):
        left = [[s[8 * j:8 * j + 8] for j in range(count)] for s in state]
        right = [[c[8 * j:8 * j + 8] for j in range(count)] if top == 0 else [] for c in columns]
        for kk in range(0, PANEL, 4):
            for m in range(levels):
                eliminate(left[m], right[m], top + kk, kk // 8, kk % 8, sub)
        for m in range(levels):
            for j in range(count):
                diagonal = jnp.sum(jnp.where(lane == sub + (top + 8 * j), left[m][j], 0.0), axis=1, keepdims=True)
                root = lax.rsqrt(diagonal)
                left[m][j] = left[m][j] * root
                if top == 0:
                    right[m][j] = right[m][j] * root
            upper = jnp.concatenate(left[m], axis=0)
            both = upper
            if top == 0:
                both = jnp.where(lanes[:PANEL] < narrow, jnp.concatenate(right[m], axis=0), upper)
            done[m].append(both)
            if top + PANEL < width:
                rest = state[m][PANEL:]
                if top == 0:
                    rest = jnp.where(lanes[PANEL:] < narrow, columns[m][PANEL:], rest)
                state[m] = rest - product(parts(upper.T[top + PANEL:]), parts(both))
    for m in range(levels):
        out_ref[m] = jnp.concatenate(done[m], axis=0).T[:narrow]


def call(kernel, out_shape, n_smem, n_vmem, scratch=()):
    return pl.pallas_call(
        kernel,
        out_shape=out_shape,
        in_specs=[pl.BlockSpec(memory_space=pltpu.SMEM)] * n_smem
        + [pl.BlockSpec(memory_space=pltpu.VMEM)] * n_vmem,
        out_specs=jax.tree.map(lambda _: pl.BlockSpec(memory_space=pltpu.VMEM), out_shape),
        scratch_shapes=list(scratch),
        compiler_params=pltpu.CompilerParams(vmem_limit_bytes=VMEM_BYTES),
    )


def partner(leaf, bit):
    if bit == 0:
        return leaf ^ 1
    if bit == 1:
        return leaf ^ 2
    if bit == 2:
        return leaf ^ 6
    if bit == 4:
        return leaf ^ 24
    if bit == 6:
        z = leaf >> 3
        z = (z + 4) % 16 if z & 4 else (z - 4) % 16
        return z * 8 + (leaf & 7)
    return leaf ^ (1 << bit)


def pair_gathered(value, axis, bit):
    leaves = range(lax.axis_size(axis))
    groups = [[leaf, partner(leaf, bit)] for leaf in leaves if not leaf >> bit & 1]
    return lax.all_gather(value, axis, axis=0, axis_index_groups=groups)


def swapped(value, axis, bit):
    pairs = [(source, partner(source, bit)) for source in range(lax.axis_size(axis))]
    return lax.ppermute(value, axis, pairs)


def local(basis, near_blocks, near_cols, bead_order):
    levels, narrow, rows = basis.shape
    block_rows, per_row = near_cols.shape
    blk = rows // block_rows
    reps = lax.axis_size("rep")
    width = reps * narrow
    leaf_index = lax.axis_index("leaf")
    rep_index = lax.axis_index("rep")
    rep_scalar = rep_index.astype(jnp.int32).reshape(1)
    square = jax.ShapeDtypeStruct((width, width), F32)

    def levels_of(rep):
        return lax.dynamic_slice_in_dim(basis, jnp.maximum(2 * rep - 1, 0), 2, 0)

    pieces = [levels_of(rep_index)]
    for shift in range(1, reps):
        pairs = [(source, (source + shift) % reps) for source in range(reps)]
        pieces.append(lax.ppermute(levels_of(lax.rem(rep_index + shift, reps)), "rep", pairs))
    tiles = near_blocks.reshape(block_rows * per_row, blk, blk)
    dense = [jax.ShapeDtypeStruct((rows, rows), BF16)] * 2
    high, low = call(dense_kernel, dense, 1, 2, [pltpu.VMEM((block_rows, rows, blk), F32)])(
        near_cols, tiles, bead_order
    )
    two = jax.ShapeDtypeStruct((2, width, width), F32)
    mine = call(panel_kernel, two, 1, reps + 2, [pltpu.VMEM((2, width, rows), F32)])(
        rep_scalar, *pieces, high, low
    )
    sent = lax.all_gather(mine, "rep", axis=0, tiled=True)
    core = (leaf_index & 1).astype(jnp.int32).reshape(1)
    half = panel = None
    x_list, p_list, q_list = [], [sent], []
    for bit in range(levels):
        first, last = bit == 0, bit == levels - 1
        kind = EXCHANGE[bit]
        value = half if kind.startswith("half") else sent[1:] if first else sent
        pair = (swapped if kind.endswith("other") else pair_gathered)(value, "leaf", bit)
        if kind.startswith("half"):
            pair = pair_gathered(pair, "leaf", 0)
        side = (leaf_index >> bit & 1).astype(jnp.int32).reshape(1)
        split = not last and EXCHANGE[bit + 1].startswith("half")
        shapes = [square]
        if not last:
            count = levels - bit - 1
            shapes += [square, square, jax.ShapeDtypeStruct((count, width, width), F32)]
            if split:
                shapes.append(jax.ShapeDtypeStruct((count, width // 2, width), F32))
        kernel = functools.partial(level_kernel, first, last, kind, split)
        state = [] if first else [panel]
        x, *rest = call(kernel, shapes, 2, 2 + len(state))(side, core, sent, pair, *state)
        x_list.append(x)
        if not last:
            panel, q, sent = rest[:3]
            half = rest[-1]
            p_list.append(panel)
            q_list.append(q)
    out = jax.ShapeDtypeStruct((levels, narrow, width), F32)
    return call(functools.partial(whiten_kernel, levels), out, 1, 3 * levels - 1)(
        rep_scalar, *x_list, *p_list, *q_list
    )


def solution(mesh):
    return jax.shard_map(
        local,
        mesh=mesh,
        in_specs=(P(None, "rep", "leaf"), P("leaf", None, None), P("leaf", None), P("leaf", None)),
        out_specs=P(None, "rep", "leaf"),
        check_vma=False,
    )
```

time: 137 us -> 132 us (0.964)
  Pallas kernels: 39.4 us -> 34.5 us
    pallas_call x8, Pallas kernels: 35.8 us -> 31 us  [the longest x7 19.7 us: local(): call(kernel, shapes, 2, 2 + len(state))(side, core, sent, pair, *state)]
where the time goes in v3:
time: 132 us; the launch traced here: 131 us
  blocking collectives  82.2 us (62%)
  Pallas kernels  34.5 us (26%)
  starting transfers between devices  11.4 us (9%)
  local copies, waits for them, and re-layouts  2.67 us (2%)
    all_gather x7, blocking collectives, pair_gathered(): return lax.all_gather(value, axis, axis=0, axis_index_groups=groups)  68.8 us
    pallas_call x7, Pallas kernels, local(): call(kernel, shapes, 2, 2 + len(state))(side, core, sent, pair, *state)  19.7 us
    all_gather x1, blocking collectives, local(): sent = lax.all_gather(mine, 'rep', axis=0, tiled=True)  13.4 us
    ppermute x3, starting transfers between devices, local(): lax.ppermute(levels_of(lax.rem(rep_index + shift, reps)), 'rep', pairs)  11.4 us
    pallas_call x1, Pallas kernels, local(): call(functools.partial(whiten_kernel, levels), out, 1, 3 * levels - 1)  11.3 us
  transfers between devices with their start and end apart: 3, of which 0 were waited for; matrix products, arithmetic and copies ran while one was open for 0% of the time, Pallas kernels for 2%

profile of v3, /device:TPU:24, one launch (start us, length us, event | category | flops | bytes accessed | tf_op | source)
XLA Modules:
  0.0 130.9 jit_solution(695361085502442797)
XLA Ops:
  0.0 0.0 copy-start.1
  0.0 1.2 constant_dynamic-slice_fusion
  1.2 3.4 %collective-permute-start = (f32[2,32,512]{2,1,0:T(8,128)S(1)}, f32[2,32,512]{2,1,0:T(8,128)S(1)}, u32[]{:S(2)}, u32[]{:S(2)}) collective-permute-start(f32[2,32,512]{2,1,0:T(8,128)S(1)} %get-tuple-element.58), channel_id=1, source_target_pairs={{0,1},{1,2},{2,3},{3,0},{4,5},{5,6},{6,7},{7,4},{8,9},{9,10},{10,1... | collective-permute-start | bytes 393224 | tf_op jit(solution)/shard_map/ppermute | solution.py:313
  4.6 4.6 %collective-permute-start.1 = (f32[2,32,512]{2,1,0:T(8,128)S(1)}, f32[2,32,512]{2,1,0:T(8,128)S(1)}, u32[]{:S(2)}, u32[]{:S(2)}) collective-permute-start(f32[2,32,512]{2,1,0:T(8,128)S(1)} %get-tuple-element.60), channel_id=1, source_target_pairs={{0,2},{1,3},{2,0},{3,1},{4,6},{5,7},{6,4},{7,5},{8,10},{9,11},{10,... | collective-permute-start | bytes 393224 | tf_op jit(solution)/shard_map/ppermute | solution.py:313
  9.3 3.3 %collective-permute-start.2 = (f32[2,32,512]{2,1,0:T(8,128)S(1)}, f32[2,32,512]{2,1,0:T(8,128)S(1)}, u32[]{:S(2)}, u32[]{:S(2)}) collective-permute-start(f32[2,32,512]{2,1,0:T(8,128)S(1)} %get-tuple-element.57), channel_id=1, source_target_pairs={{0,3},{1,0},{2,1},{3,2},{4,7},{5,4},{6,5},{7,6},{8,11},{9,8},{10,9... | collective-permute-start | bytes 393224 | tf_op jit(solution)/shard_map/ppermute | solution.py:313
  12.6 0.0 copy-done.1
  12.6 0.0 copy-start.2
  12.6 0.5 reshape.33.blocks_ref
  13.2 0.1 copy-done.2
  13.3 0.1 copy.6.cols_ref
  13.4 0.0 copy-start
  13.4 0.7 copy-done
  14.1 2.3 %shard_map.46 = (bf16[512,512]{1,0:T(8,128)(2,1)S(1)}, bf16[512,512]{1,0:T(8,128)(2,1)S(1)}) custom-call(s32[8,4]{1,0:T(8,128)S(1)} %copy.6.cols_ref, f32[32,64,64]{2,1,0:T(8,128)S(1)} %reshape.33.blocks_ref, s32[1,512]{1,0:T(1,128)S(1)} %copy-done), custom_call_target="tpu_custom_call" | custom-call | tf_op jit(solution)/shard_map/pallas_call | solution.py:316
  16.4 0.0 collective-permute-done.refs_0_
  16.4 0.0 collective-permute-done.1.refs_1_
  16.4 0.0 collective-permute-done.2.refs_2_
  16.5 1.2 shard_map.47
  17.7 13.4 %all_gather.45.own_ref.refs_7_ = f32[8,128,128]{2,1,0:T(8,128)S(1)} all-gather(f32[2,128,128]{2,1,0:T(8,128)S(1)} %shard_map.47), channel_id=1, replica_groups=mesh['leaf'=128,'rep'=4] {'rep'}, dimensions={0}, use_global_device_ids=true | all-gather | bytes 655360 | tf_op jit(solution)/shard_map/all_gather | solution.py:323
  31.1 2.5 %all-gather = f32[14,128,128]{2,1,0:T(8,128)S(1)} all-gather(f32[7,128,128]{2,1,0:T(8,128)S(1)} %slice.4), channel_id=2, replica_groups={{0,4},{8,12},{16,20},{24,28},{32,36},{40,44},{48,52},{56,60},{64,68},{7..., dimensions={0}, use_global_device_ids=true | all-gather | bytes 1376256 | tf_op jit(solution)/shard_map/all_gather | solution.py:288
  33.5 3.0 %shard_map.48 = (f32[128,128]{1,0:T(8,128)S(1)}, f32[128,128]{1,0:T(8,128)S(1)}, f32[128,128]{1,0:T(8,128)S(1)}, f32[6,128,128]{2,1,0:T(8,128)S(1)}) custom-call(s32[1]{0:T(128)} %bitcast.1.side_ref, s32[1]{0:T(128)} %bitcast.2.core_ref, f32[8,128,128]{2,1,0:T(8,128)S(1)} %all_gather.45.own_ref.refs_7_, f32[2,7,128,128]{3,2,1,0:T(8,128)S(1)} %bitcast.16), custom_call_target="tpu_custom_call" | custom-call | tf_op jit(solution)/shard_map/pallas_call | solution.py:344
  36.5 11.8 %all-gather.1 = f32[12,128,128]{2,1,0:T(8,128)S(1)} all-gather(f32[6,128,128]{2,1,0:T(8,128)S(1)} %get-tuple-element.34.own_ref), channel_id=3, replica_groups={{0,8},{4,12},{16,24},{20,28},{32,40},{36,44},{48,56},{52,60},{64,72},{6..., dimensions={0}, use_global_device_ids=true | all-gather | bytes 1179648 | tf_op jit(solution)/shard_map/all_gather | solution.py:288
  48.3 3.0 %shard_map.49 = (f32[128,128]{1,0:T(8,128)S(1)}, f32[128,128]{1,0:T(8,128)S(1)}, f32[128,128]{1,0:T(8,128)S(1)}, f32[5,128,128]{2,1,0:T(8,128)S(1)}) custom-call(s32[1]{0:T(128)} %bitcast.4.side_ref, s32[1]{0:T(128)} %bitcast.2.core_ref, f32[6,128,128]{2,1,0:T(8,128)S(1)} %get-tuple-element.34.own_ref, f32[2,6,128,128]{3,2,1,0:T(8,128)S(1)} %bitcast.17, ...), custom_call_target="tpu_custom_call" | custom-call | tf_op jit(solution)/shard_map/pallas_call | solution.py:344
  51.3 11.1 %all-gather.2 = f32[10,128,128]{2,1,0:T(8,128)S(1)} all-gather(f32[5,128,128]{2,1,0:T(8,128)S(1)} %get-tuple-element.37.own_ref), channel_id=4, replica_groups={{0,24},{4,28},{8,16},{12,20},{32,56},{36,60},{40,48},{44,52},{64,88},{6..., dimensions={0}, use_global_device_ids=true | all-gather | bytes 983040 | tf_op jit(solution)/shard_map/all_gather | solution.py:288
  62.4 3.0 %shard_map.50 = (f32[128,128]{1,0:T(8,128)S(1)}, f32[128,128]{1,0:T(8,128)S(1)}, f32[128,128]{1,0:T(8,128)S(1)}, f32[4,128,128]{2,1,0:T(8,128)S(1)}) custom-call(s32[1]{0:T(128)} %bitcast.6.side_ref, s32[1]{0:T(128)} %bitcast.2.core_ref, f32[5,128,128]{2,1,0:T(8,128)S(1)} %get-tuple-element.37.own_ref, f32[2,5,128,128]{3,2,1,0:T(8,128)S(1)} %bitcast.18, ...), custom_call_target="tpu_custom_call" | custom-call | tf_op jit(solution)/shard_map/pallas_call | solution.py:344
  65.4 7.6 %all-gather.3 = f32[8,128,128]{2,1,0:T(8,128)S(1)} all-gather(f32[4,128,128]{2,1,0:T(8,128)S(1)} %get-tuple-element.40.own_ref), channel_id=5, replica_groups={{0,32},{4,36},{8,40},{12,44},{16,48},{20,52},{24,56},{28,60},{64,96},{6..., dimensions={0}, use_global_device_ids=true | all-gather | bytes 786432 | tf_op jit(solution)/shard_map/all_gather | solution.py:288
  73.0 3.0 %shard_map.51 = (f32[128,128]{1,0:T(8,128)S(1)}, f32[128,128]{1,0:T(8,128)S(1)}, f32[128,128]{1,0:T(8,128)S(1)}, f32[3,128,128]{2,1,0:T(8,128)S(1)}) custom-call(s32[1]{0:T(128)} %bitcast.8.side_ref, s32[1]{0:T(128)} %bitcast.2.core_ref, f32[4,128,128]{2,1,0:T(8,128)S(1)} %get-tuple-element.40.own_ref, f32[2,4,128,128]{3,2,1,0:T(8,128)S(1)} %bitcast.19, ...), custom_call_target="tpu_custom_call" | custom-call | tf_op jit(solution)/shard_map/pallas_call | solution.py:344
  75.9 10.1 %all-gather.4 = f32[6,128,128]{2,1,0:T(8,128)S(1)} all-gather(f32[3,128,128]{2,1,0:T(8,128)S(1)} %get-tuple-element.43.own_ref), channel_id=6, replica_groups={{0,96},{4,100},{8,104},{12,108},{16,112},{20,116},{24,120},{28,124},{32..., dimensions={0}, use_global_device_ids=true | all-gather | bytes 589824 | tf_op jit(solution)/shard_map/all_gather | solution.py:288
  86.1 3.0 %shard_map.52 = (f32[128,128]{1,0:T(8,128)S(1)}, f32[128,128]{1,0:T(8,128)S(1)}, f32[128,128]{1,0:T(8,128)S(1)}, f32[2,128,128]{2,1,0:T(8,128)S(1)}) custom-call(s32[1]{0:T(128)} %bitcast.10.side_ref, s32[1]{0:T(128)} %bitcast.2.core_ref, f32[3,128,128]{2,1,0:T(8,128)S(1)} %get-tuple-element.43.own_ref, f32[2,3,128,128]{3,2,1,0:T(8,128)S(1)} %bitcast.20, ...), custom_call_target="tpu_custom_call" | custom-call | tf_op jit(solution)/shard_map/pallas_call | solution.py:344
  89.0 16.8 %all-gather.5 = f32[4,128,128]{2,1,0:T(8,128)S(1)} all-gather(f32[2,128,128]{2,1,0:T(8,128)S(1)} %get-tuple-element.46.own_ref), channel_id=7, replica_groups={{0,128},{4,132},{8,136},{12,140},{16,144},{20,148},{24,152},{28,156},{3..., dimensions={0}, use_global_device_ids=true | all-gather | bytes 393216 | tf_op jit(solution)/shard_map/all_gather | solution.py:288
  105.8 3.0 %shard_map.53 = (f32[128,128]{1,0:T(8,128)S(1)}, f32[128,128]{1,0:T(8,128)S(1)}, f32[128,128]{1,0:T(8,128)S(1)}, f32[1,128,128]{2,1,0:T(8,128)S(1)}) custom-call(s32[1]{0:T(128)} %bitcast.12.side_ref, s32[1]{0:T(128)} %bitcast.2.core_ref, f32[2,128,128]{2,1,0:T(8,128)S(1)} %get-tuple-element.46.own_ref, f32[2,2,128,128]{3,2,1,0:T(8,128)S(1)} %bitcast.21, ...), custom_call_target="tpu_custom_call" | custom-call | tf_op jit(solution)/shard_map/pallas_call | solution.py:344
  108.8 9.0 %all-gather.6 = f32[2,128,128]{2,1,0:T(8,128)S(1)} all-gather(f32[1,128,128]{2,1,0:T(8,128)S(1)} %get-tuple-element.49.own_ref), channel_id=8, replica_groups={{0,384},{4,388},{8,392},{12,396},{16,400},{20,404},{24,408},{28,412},{3..., dimensions={0}, use_global_device_ids=true | all-gather | bytes 196608 | tf_op jit(solution)/shard_map/all_gather | solution.py:288
  117.7 1.9 %shard_map.54.refs_6_ = f32[128,128]{1,0:T(8,128)S(1)} custom-call(s32[1]{0:T(128)} %bitcast.14.side_ref, s32[1]{0:T(128)} %bitcast.2.core_ref, f32[1,128,128]{2,1,0:T(8,128)S(1)} %get-tuple-element.49.own_ref, f32[2,1,128,128]{3,2,1,0:T(8,128)S(1)} %bitcast.22, f32[128,128]{1,0:T(8,128)S(1)} %get-tuple-element.50.refs_0_.refs_13_), custom_call_target="tpu_custom_call" | custom-call | tf_op jit(solution)/shard_map/pallas_call | solution.py:344
  119.6 11.3 %shard_map.55 = f32[7,32,128]{2,1,0:T(8,128)} custom-call(s32[1]{0:T(128)} %bitcast.rep_ref, f32[128,128]{1,0:T(8,128)S(1)} %get-tuple-element.33.refs_0_, f32[128,128]{1,0:T(8,128)S(1)} %get-tuple-element.36.refs_1_, f32[128,128]{1,0:T(8,128)S(1)} %get-tuple-element.39.refs_2_, f32[128,128]{1,0:T(8,128)S(1)} %get-tuple-element.42.refs_3_, ...), custom_call_target="tpu_custom_call" | custom-call | tf_op jit(solution)/shard_map/pallas_call | solution.py:352
  (1 shorter events, 0.0 us)
Async XLA Ops:
  0.0 12.6 %copy-start.1 = (f32[8,4,4096]{2,1,0:T(4,128)S(1)}, f32[8,4,4096]{2,1,0:T(4,128)}, u32[]{:S(2)}) copy-start(f32[8,4,4096]{2,1,0:T(4,128)} %param.5) | copy-start | bytes 1572868
  1.2 15.2 %collective-permute-start = (f32[2,32,512]{2,1,0:T(8,128)S(1)}, f32[2,32,512]{2,1,0:T(8,128)S(1)}, u32[]{:S(2)}, u32[]{:S(2)}) collective-permute-start(f32[2,32,512]{2,1,0:T(8,128)S(1)} %get-tuple-element.58), channel_id=1, source_target_pairs={{0,1},{1,2},{2,3},{3,0},{4,5},{5,6},{6,7},{7,4},{8,9},{9,10},{10,1... | collective-permute-start | bytes 393224 | tf_op jit(solution)/shard_map/ppermute | solution.py:313
  4.6 11.8 %collective-permute-start.1 = (f32[2,32,512]{2,1,0:T(8,128)S(1)}, f32[2,32,512]{2,1,0:T(8,128)S(1)}, u32[]{:S(2)}, u32[]{:S(2)}) collective-permute-start(f32[2,32,512]{2,1,0:T(8,128)S(1)} %get-tuple-element.60), channel_id=1, source_target_pairs={{0,2},{1,3},{2,0},{3,1},{4,6},{5,7},{6,4},{7,5},{8,10},{9,11},{10,... | collective-permute-start | bytes 393224 | tf_op jit(solution)/shard_map/ppermute | solution.py:313
  9.3 7.2 %collective-permute-start.2 = (f32[2,32,512]{2,1,0:T(8,128)S(1)}, f32[2,32,512]{2,1,0:T(8,128)S(1)}, u32[]{:S(2)}, u32[]{:S(2)}) collective-permute-start(f32[2,32,512]{2,1,0:T(8,128)S(1)} %get-tuple-element.57), channel_id=1, source_target_pairs={{0,3},{1,0},{2,1},{3,2},{4,7},{5,4},{6,5},{7,6},{8,11},{9,8},{10,9... | collective-permute-start | bytes 393224 | tf_op jit(solution)/shard_map/ppermute | solution.py:313
  12.6 0.7 copy-start.2
  13.4 0.7 copy-start

commit v4 on v3

--- a/solution.py
+++ b/solution.py
@@ -26,6 +26,15 @@
 
 def product(a, b, dims=((1,), (0,))):
     return contract(a[0], b[0], dims) + (contract(a[0], b[1], dims) + contract(a[1], b[0], dims))
+
+
+def wide_product(a, b, dims=((1,), (0,))):
+    (ca,), (cb,) = dims
+    above = jnp.concatenate([b[0], b[1]], axis=1 - cb)
+    below = jnp.concatenate([b[0], jnp.zeros_like(b[1])], axis=1 - cb)
+    both = contract(jnp.concatenate([a[0], a[1]], axis=ca), jnp.concatenate([above, below], axis=cb), dims)
+    half = both.shape[1] // 2
+    return both[:, :half] + both[:, half:]
 
 
 def identity(n):
@@ -103,7 +112,14 @@
         root_half = math.sqrt(0.5)
         next_panel = (ours(1) + theirs(1)) * root_half
     step = 2.0 / (bound + 1.0)
-    start = ((bound - 1.0) / (bound + 1.0), tuple((step * eye, eye - step * matrix) for matrix in matrices))
+    rho = 1.0 - step
+    scale = 2.0 / (2.0 - rho * rho)
+    begun = []
+    for matrix in matrices:
+        residual = eye - step * matrix
+        e = parts(residual)
+        begun.append(((scale * step) * (eye + residual), (1.0 - scale) * eye + scale * wide_product(e, e)))
+    start = (0.5 * scale * rho * rho, tuple(begun))
 
     def go_on(carry):
         return carry[0] > 1e-2
@@ -114,9 +130,9 @@
         new = []
         for inverse, residual in inverses:
             e = parts(residual)
-            better = scale * (inverse + product(parts(inverse), e))
-            new.append((better, (1.0 - scale) * eye + scale * product(e, e)))
-        return (rho * rho / (2.0 - rho * rho), tuple(new))
+            better = scale * (inverse + wide_product(parts(inverse), e))
+            new.append((better, (1.0 - scale) * eye + scale * wide_product(e, e)))
+        return (0.5 * scale * rho * rho, tuple(new))
 
     _, inverses = lax.while_loop(go_on, refine, start)
     pairs = [parts(matrix) for matrix in matrices]
@@ -125,22 +141,22 @@
         new = []
         for inverse, pair in zip(found, pairs):
             x = parts(inverse)
-            new.append(inverse + product(x, parts(eye - product(pair, x))))
+            new.append(inverse + wide_product(x, parts(eye - wide_product(pair, x))))
         return tuple(new)
 
     extra = jnp.where(bound > 200.0, 3, 0)
     inverses = lax.fori_loop(0, extra, correct, tuple(inverse for inverse, _ in inverses))
     x = [parts(inverse) for inverse in inverses]
-    residuals = [parts(eye - product(pair, inverse)) for pair, inverse in zip(pairs, x)]
+    residuals = [parts(eye - wide_product(pair, inverse)) for pair, inverse in zip(pairs, x)]
     if not last:
         next_panel_ref, next_q_ref, next_ref = outs[1:4]
         p = parts(next_panel)
         r = residuals[2]
-        y = product(x[2], p)
-        ry, rp = product(r, parts(y)), product(r, p)
+        y = wide_product(x[2], p)
+        ry, rp = wide_product(r, parts(y)), wide_product(r, p)
         sum_y = next_panel + y
-        plain = product(p, parts(sum_y), ((0,), (0,)))
-        bent = product(parts(ry), parts(next_panel + rp), ((0,), (0,)))
+        plain = wide_product(p, parts(sum_y), ((0,), (0,)))
+        bent = wide_product(parts(ry), parts(next_panel + rp), ((0,), (0,)))
         next_ref[0] = (plain + bent) * (0.5 / width)
         next_panel_ref[...] = next_panel
         for upper in range(1, next_ref.shape[0]):
@@ -149,12 +165,12 @@
             half_rows = width // 2
             outs[4][...] = next_ref[:, pl.ds(pl.multiple_of(core_ref[0] * half_rows, half_rows), half_rows), :]
         r = residuals[1]
-        both = eye - product(pairs[1], x[1]) + product(r, r)
-        next_q_ref[...] = 2.0 * eye - (inverses[1] + product(x[1], parts(both)))
+        both = eye - wide_product(pairs[1], x[1]) + wide_product(r, r)
+        next_q_ref[...] = 2.0 * eye - (inverses[1] + wide_product(x[1], parts(both)))
     r = residuals[0]
-    v = product(parts(panel), x[0])
-    vr = product(parts(v), r)
-    gained = v + vr + product(parts(vr), r)
+    v = wide_product(parts(panel), x[0])
+    vr = wide_product(parts(v), r)
+    gained = v + vr + wide_product(parts(vr), r)
     outs[0][...] = jnp.where(side == 1, gained, panel)
 
 
@@ -214,9 +230,7 @@
     lane = lax.broadcasted_iota(jnp.int32, (8, width), 1)
     sub = lax.broadcasted_iota(jnp.int32, (8, width), 0)
     count = PANEL // 8
-    rows = lax.broadcasted_iota(jnp.int32, (width, width), 0)
     lanes = lax.broadcasted_iota(jnp.int32, (width, width), 1)
-    select = ((rows == lanes + rep_ref[0] * narrow) & (lanes < narrow)).astype(F32).astype(BF16)
     state, columns = [], []
     for m in range(levels):
         x, p = x_refs[m][...], p_refs[m]
@@ -224,8 +238,7 @@
         q = q_refs[m - 1][...] if m else identity(width)
         pair = parts(x)
         state.append(q + product(pair, parts(p), ((1,), (1,))) * (1.0 / width))
-        rest = parts(x - pair[0].astype(F32) - pair[1].astype(F32))[0]
-        columns.append(sum(contract(piece, select, ((1,), (0,))) for piece in (*pair, rest)))
+        columns.append(pltpu.roll(x, width - rep_ref[0] * narrow, 1))
     done = [[] for _ in range(levels)]
     for top in range(0, width, PANEL):
         left = [[s[8 * j:8 * j + 8] for j in range(count)] for s in state]
@@ -252,6 +265,13 @@
                 state[m] = rest - product(parts(upper.T[top + PANEL:]), parts(both))
     for m in range(levels):
         out_ref[m] = jnp.concatenate(done[m], axis=0).T[:narrow]
+
+
+def last_kernel(levels, kind, side_ref, core_ref, rep_ref, own_ref, pair_ref, *refs):
+    x_refs, p_refs, q_refs = refs[: levels - 1], refs[levels - 1:2 * levels - 1], refs[2 * levels - 1:-2]
+    out_ref, x_last = refs[-2:]
+    level_kernel(False, True, kind, False, side_ref, core_ref, own_ref, pair_ref, p_refs[-1], x_last)
+    whiten_kernel(levels, rep_ref, *x_refs, x_last, *p_refs, *q_refs, out_ref)
 
 
 def call(kernel, out_shape, n_smem, n_vmem, scratch=()):
@@ -341,17 +361,17 @@
                 shapes.append(jax.ShapeDtypeStruct((count, width // 2, width), F32))
         kernel = functools.partial(level_kernel, first, last, kind, split)
         state = [] if first else [panel]
-        x, *rest = call(kernel, shapes, 2, 2 + len(state))(side, core, sent, pair, *state)
+        if last:
+            out = jax.ShapeDtypeStruct((levels, narrow, width), F32)
+            kernel = functools.partial(last_kernel, levels, kind)
+            return call(kernel, out, 3, 3 * levels, [pltpu.VMEM((width, width), F32)])(
+                side, core, rep_scalar, sent, pair, *x_list, *p_list, *q_list
+            )
+        x, panel, q, sent, *rest = call(kernel, shapes, 2, 2 + len(state))(side, core, sent, pair, *state)
+        half = rest[0] if rest else None
         x_list.append(x)
-        if not last:
-            panel, q, sent = rest[:3]
-            half = rest[-1]
-            p_list.append(panel)
-            q_list.append(q)
-    out = jax.ShapeDtypeStruct((levels, narrow, width), F32)
-    return call(functools.partial(whiten_kernel, levels), out, 1, 3 * levels - 1)(
-        rep_scalar, *x_list, *p_list, *q_list
-    )
+        p_list.append(panel)
+        q_list.append(q)
 
 
 def solution(mesh):

time: 132 us -> 133 us (level)
  blocking collectives: 82.2 us -> 86.6 us
  Pallas kernels: 34.5 us -> 31.5 us
    all_gather x7, blocking collectives: 68.8 us -> 73.2 us  [pair_gathered(): return lax.all_gather(value, axis, axis=0, axis_index_groups=groups)]
    pallas_call x7 -> x6, Pallas kernels: 19.7 us -> 15.6 us  [local(): call(kernel, shapes, 2, 2 + len(state))(side, core, sent, pair, *state)]
where the time goes in v4:
time: 133 us; the launch traced here: 132 us
  blocking collectives  86.6 us (65%)
  Pallas kernels  31.5 us (24%)
  starting transfers between devices  11.4 us (9%)
  local copies, waits for them, and re-layouts  2.67 us (2%)
    all_gather x7, blocking collectives, pair_gathered(): return lax.all_gather(value, axis, axis=0, axis_index_groups=groups)  73.2 us
    pallas_call x6, Pallas kernels, local(): call(kernel, shapes, 2, 2 + len(state))(side, core, sent, pair, *state)  15.6 us
    all_gather x1, blocking collectives, local(): sent = lax.all_gather(mine, 'rep', axis=0, tiled=True)  13.4 us
    pallas_call x1, Pallas kernels, local(): call(kernel, out, 3, 3 * levels, [pltpu.VMEM((width, width), F32)])  12.4 us
    ppermute x3, starting transfers between devices, local(): lax.ppermute(levels_of(lax.rem(rep_index + shift, reps)), 'rep', pairs)  11.4 us
  transfers between devices with their start and end apart: 3, of which 0 were waited for; matrix products, arithmetic and copies ran while one was open for 0% of the time, Pallas kernels for 2%

profile of v4, /device:TPU:24, one launch (start us, length us, event | category | flops | bytes accessed | tf_op | source)
XLA Modules:
  0.0 132.3 jit_solution(7957580318413572561)
XLA Ops:
  0.0 0.0 copy-start.1
  0.0 1.2 constant_dynamic-slice_fusion
  1.2 3.4 %collective-permute-start = (f32[2,32,512]{2,1,0:T(8,128)S(1)}, f32[2,32,512]{2,1,0:T(8,128)S(1)}, u32[]{:S(2)}, u32[]{:S(2)}) collective-permute-start(f32[2,32,512]{2,1,0:T(8,128)S(1)} %get-tuple-element.58), channel_id=1, source_target_pairs={{0,1},{1,2},{2,3},{3,0},{4,5},{5,6},{6,7},{7,4},{8,9},{9,10},{10,1... | collective-permute-start | bytes 393224 | tf_op jit(solution)/shard_map/ppermute | solution.py:333
  4.6 4.6 %collective-permute-start.1 = (f32[2,32,512]{2,1,0:T(8,128)S(1)}, f32[2,32,512]{2,1,0:T(8,128)S(1)}, u32[]{:S(2)}, u32[]{:S(2)}) collective-permute-start(f32[2,32,512]{2,1,0:T(8,128)S(1)} %get-tuple-element.60), channel_id=1, source_target_pairs={{0,2},{1,3},{2,0},{3,1},{4,6},{5,7},{6,4},{7,5},{8,10},{9,11},{10,... | collective-permute-start | bytes 393224 | tf_op jit(solution)/shard_map/ppermute | solution.py:333
  9.3 3.3 %collective-permute-start.2 = (f32[2,32,512]{2,1,0:T(8,128)S(1)}, f32[2,32,512]{2,1,0:T(8,128)S(1)}, u32[]{:S(2)}, u32[]{:S(2)}) collective-permute-start(f32[2,32,512]{2,1,0:T(8,128)S(1)} %get-tuple-element.57), channel_id=1, source_target_pairs={{0,3},{1,0},{2,1},{3,2},{4,7},{5,4},{6,5},{7,6},{8,11},{9,8},{10,9... | collective-permute-start | bytes 393224 | tf_op jit(solution)/shard_map/ppermute | solution.py:333
  12.6 0.0 copy-done.1
  12.6 0.0 copy-start.2
  12.6 0.5 reshape.39.blocks_ref
  13.2 0.1 copy-done.2
  13.3 0.1 copy.6.cols_ref
  13.4 0.0 copy-start
  13.4 0.7 copy-done
  14.1 2.3 %shard_map.46 = (bf16[512,512]{1,0:T(8,128)(2,1)S(1)}, bf16[512,512]{1,0:T(8,128)(2,1)S(1)}) custom-call(s32[8,4]{1,0:T(8,128)S(1)} %copy.6.cols_ref, f32[32,64,64]{2,1,0:T(8,128)S(1)} %reshape.39.blocks_ref, s32[1,512]{1,0:T(1,128)S(1)} %copy-done), custom_call_target="tpu_custom_call" | custom-call | tf_op jit(solution)/shard_map/pallas_call | solution.py:336
  16.4 0.0 collective-permute-done.refs_0_
  16.4 0.0 collective-permute-done.1.refs_1_
  16.4 0.0 collective-permute-done.2.refs_2_
  16.5 1.2 shard_map.47
  17.7 13.4 %all_gather.45.own_ref.refs_6_ = f32[8,128,128]{2,1,0:T(8,128)S(1)} all-gather(f32[2,128,128]{2,1,0:T(8,128)S(1)} %shard_map.47), channel_id=1, replica_groups=mesh['leaf'=128,'rep'=4] {'rep'}, dimensions={0}, use_global_device_ids=true | all-gather | bytes 655360 | tf_op jit(solution)/shard_map/all_gather | solution.py:343
  31.1 2.5 %all-gather = f32[14,128,128]{2,1,0:T(8,128)S(1)} all-gather(f32[7,128,128]{2,1,0:T(8,128)S(1)} %slice.4), channel_id=2, replica_groups={{0,4},{8,12},{16,20},{24,28},{32,36},{40,44},{48,52},{56,60},{64,68},{7..., dimensions={0}, use_global_device_ids=true | all-gather | bytes 1376256 | tf_op jit(solution)/shard_map/all_gather | solution.py:308
  33.5 2.5 %shard_map.48 = (f32[128,128]{1,0:T(8,128)S(1)}, f32[128,128]{1,0:T(8,128)S(1)}, f32[128,128]{1,0:T(8,128)S(1)}, f32[6,128,128]{2,1,0:T(8,128)S(1)}) custom-call(s32[1]{0:T(128)} %bitcast.8.side_ref, s32[1]{0:T(128)} %bitcast.1.core_ref, f32[8,128,128]{2,1,0:T(8,128)S(1)} %all_gather.45.own_ref.refs_6_, f32[2,7,128,128]{3,2,1,0:T(8,128)S(1)} %bitcast.16), custom_call_target="tpu_custom_call" | custom-call | tf_op jit(solution)/shard_map/pallas_call | solution.py:370
  36.1 11.8 %all-gather.1 = f32[12,128,128]{2,1,0:T(8,128)S(1)} all-gather(f32[6,128,128]{2,1,0:T(8,128)S(1)} %get-tuple-element.33.own_ref), channel_id=3, replica_groups={{0,8},{4,12},{16,24},{20,28},{32,40},{36,44},{48,56},{52,60},{64,72},{6..., dimensions={0}, use_global_device_ids=true | all-gather | bytes 1179648 | tf_op jit(solution)/shard_map/all_gather | solution.py:308
  47.9 2.5 %shard_map.49 = (f32[128,128]{1,0:T(8,128)S(1)}, f32[128,128]{1,0:T(8,128)S(1)}, f32[128,128]{1,0:T(8,128)S(1)}, f32[5,128,128]{2,1,0:T(8,128)S(1)}) custom-call(s32[1]{0:T(128)} %bitcast.7.side_ref, s32[1]{0:T(128)} %bitcast.1.core_ref, f32[6,128,128]{2,1,0:T(8,128)S(1)} %get-tuple-element.33.own_ref, f32[2,6,128,128]{3,2,1,0:T(8,128)S(1)} %bitcast.17, ...), custom_call_target="tpu_custom_call" | custom-call | tf_op jit(solution)/shard_map/pallas_call | solution.py:370
  50.4 11.4 %all-gather.2 = f32[10,128,128]{2,1,0:T(8,128)S(1)} all-gather(f32[5,128,128]{2,1,0:T(8,128)S(1)} %get-tuple-element.35.own_ref), channel_id=4, replica_groups={{0,24},{4,28},{8,16},{12,20},{32,56},{36,60},{40,48},{44,52},{64,88},{6..., dimensions={0}, use_global_device_ids=true | all-gather | bytes 983040 | tf_op jit(solution)/shard_map/all_gather | solution.py:308
  61.9 2.5 %shard_map.50 = (f32[128,128]{1,0:T(8,128)S(1)}, f32[128,128]{1,0:T(8,128)S(1)}, f32[128,128]{1,0:T(8,128)S(1)}, f32[4,128,128]{2,1,0:T(8,128)S(1)}) custom-call(s32[1]{0:T(128)} %bitcast.6.side_ref, s32[1]{0:T(128)} %bitcast.1.core_ref, f32[5,128,128]{2,1,0:T(8,128)S(1)} %get-tuple-element.35.own_ref, f32[2,5,128,128]{3,2,1,0:T(8,128)S(1)} %bitcast.18, ...), custom_call_target="tpu_custom_call" | custom-call | tf_op jit(solution)/shard_map/pallas_call | solution.py:370
  64.4 8.1 %all-gather.3 = f32[8,128,128]{2,1,0:T(8,128)S(1)} all-gather(f32[4,128,128]{2,1,0:T(8,128)S(1)} %get-tuple-element.37.own_ref), channel_id=5, replica_groups={{0,32},{4,36},{8,40},{12,44},{16,48},{20,52},{24,56},{28,60},{64,96},{6..., dimensions={0}, use_global_device_ids=true | all-gather | bytes 786432 | tf_op jit(solution)/shard_map/all_gather | solution.py:308
  72.5 2.5 %shard_map.51 = (f32[128,128]{1,0:T(8,128)S(1)}, f32[128,128]{1,0:T(8,128)S(1)}, f32[128,128]{1,0:T(8,128)S(1)}, f32[3,128,128]{2,1,0:T(8,128)S(1)}) custom-call(s32[1]{0:T(128)} %bitcast.5.side_ref, s32[1]{0:T(128)} %bitcast.1.core_ref, f32[4,128,128]{2,1,0:T(8,128)S(1)} %get-tuple-element.37.own_ref, f32[2,4,128,128]{3,2,1,0:T(8,128)S(1)} %bitcast.19, ...), custom_call_target="tpu_custom_call" | custom-call | tf_op jit(solution)/shard_map/pallas_call | solution.py:370
  75.0 12.4 %all-gather.4 = f32[6,128,128]{2,1,0:T(8,128)S(1)} all-gather(f32[3,128,128]{2,1,0:T(8,128)S(1)} %get-tuple-element.39.own_ref), channel_id=6, replica_groups={{0,96},{4,100},{8,104},{12,108},{16,112},{20,116},{24,120},{28,124},{32..., dimensions={0}, use_global_device_ids=true | all-gather | bytes 589824 | tf_op jit(solution)/shard_map/all_gather | solution.py:308
  87.4 2.5 %shard_map.52 = (f32[128,128]{1,0:T(8,128)S(1)}, f32[128,128]{1,0:T(8,128)S(1)}, f32[128,128]{1,0:T(8,128)S(1)}, f32[2,128,128]{2,1,0:T(8,128)S(1)}) custom-call(s32[1]{0:T(128)} %bitcast.4.side_ref, s32[1]{0:T(128)} %bitcast.1.core_ref, f32[3,128,128]{2,1,0:T(8,128)S(1)} %get-tuple-element.39.own_ref, f32[2,3,128,128]{3,2,1,0:T(8,128)S(1)} %bitcast.20, ...), custom_call_target="tpu_custom_call" | custom-call | tf_op jit(solution)/shard_map/pallas_call | solution.py:370
  90.0 18.1 %all-gather.5 = f32[4,128,128]{2,1,0:T(8,128)S(1)} all-gather(f32[2,128,128]{2,1,0:T(8,128)S(1)} %get-tuple-element.41.own_ref), channel_id=7, replica_groups={{0,128},{4,132},{8,136},{12,140},{16,144},{20,148},{24,152},{28,156},{3..., dimensions={0}, use_global_device_ids=true | all-gather | bytes 393216 | tf_op jit(solution)/shard_map/all_gather | solution.py:308
  108.1 3.0 %shard_map.53 = (f32[128,128]{1,0:T(8,128)S(1)}, f32[128,128]{1,0:T(8,128)S(1)}, f32[128,128]{1,0:T(8,128)S(1)}, f32[1,128,128]{2,1,0:T(8,128)S(1)}) custom-call(s32[1]{0:T(128)} %bitcast.3.side_ref, s32[1]{0:T(128)} %bitcast.1.core_ref, f32[2,128,128]{2,1,0:T(8,128)S(1)} %get-tuple-element.41.own_ref, f32[2,2,128,128]{3,2,1,0:T(8,128)S(1)} %bitcast.21, ...), custom_call_target="tpu_custom_call" | custom-call | tf_op jit(solution)/shard_map/pallas_call | solution.py:370
  111.1 8.9 %all-gather.6 = f32[2,128,128]{2,1,0:T(8,128)S(1)} all-gather(f32[1,128,128]{2,1,0:T(8,128)S(1)} %get-tuple-element.43.own_ref), channel_id=8, replica_groups={{0,384},{4,388},{8,392},{12,396},{16,400},{20,404},{24,408},{28,412},{3..., dimensions={0}, use_global_device_ids=true | all-gather | bytes 196608 | tf_op jit(solution)/shard_map/all_gather | solution.py:308
  120.0 12.4 %shard_map.54 = f32[7,32,128]{2,1,0:T(8,128)} custom-call(s32[1]{0:T(128)} %bitcast.side_ref, s32[1]{0:T(128)} %bitcast.1.core_ref, s32[1]{0:T(128)} %bitcast.2.rep_ref, f32[1,128,128]{2,1,0:T(8,128)S(1)} %get-tuple-element.43.own_ref, f32[2,1,128,128]{3,2,1,0:T(8,128)S(1)} %bitcast.22, f32[128,128]{1,0:T(8,128)S(1)} %get-tuple-element.44.refs_0_, ...), custom_call_target="tpu_custom_call" | custom-call | tf_op jit(solution)/shard_map/pallas_call | solution.py:367
  (1 shorter events, 0.0 us)
Async XLA Ops:
  0.0 12.6 %copy-start.1 = (f32[8,4,4096]{2,1,0:T(4,128)S(1)}, f32[8,4,4096]{2,1,0:T(4,128)}, u32[]{:S(2)}) copy-start(f32[8,4,4096]{2,1,0:T(4,128)} %param.5) | copy-start | bytes 1572868
  1.2 15.2 %collective-permute-start = (f32[2,32,512]{2,1,0:T(8,128)S(1)}, f32[2,32,512]{2,1,0:T(8,128)S(1)}, u32[]{:S(2)}, u32[]{:S(2)}) collective-permute-start(f32[2,32,512]{2,1,0:T(8,128)S(1)} %get-tuple-element.58), channel_id=1, source_target_pairs={{0,1},{1,2},{2,3},{3,0},{4,5},{5,6},{6,7},{7,4},{8,9},{9,10},{10,1... | collective-permute-start | bytes 393224 | tf_op jit(solution)/shard_map/ppermute | solution.py:333
  4.6 11.8 %collective-permute-start.1 = (f32[2,32,512]{2,1,0:T(8,128)S(1)}, f32[2,32,512]{2,1,0:T(8,128)S(1)}, u32[]{:S(2)}, u32[]{:S(2)}) collective-permute-start(f32[2,32,512]{2,1,0:T(8,128)S(1)} %get-tuple-element.60), channel_id=1, source_target_pairs={{0,2},{1,3},{2,0},{3,1},{4,6},{5,7},{6,4},{7,5},{8,10},{9,11},{10,... | collective-permute-start | bytes 393224 | tf_op jit(solution)/shard_map/ppermute | solution.py:333
  9.3 7.2 %collective-permute-start.2 = (f32[2,32,512]{2,1,0:T(8,128)S(1)}, f32[2,32,512]{2,1,0:T(8,128)S(1)}, u32[]{:S(2)}, u32[]{:S(2)}) collective-permute-start(f32[2,32,512]{2,1,0:T(8,128)S(1)} %get-tuple-element.57), channel_id=1, source_target_pairs={{0,3},{1,0},{2,1},{3,2},{4,7},{5,4},{6,5},{7,6},{8,11},{9,8},{10,9... | collective-permute-start | bytes 393224 | tf_op jit(solution)/shard_map/ppermute | solution.py:333
  12.6 0.7 copy-start.2
  13.4 0.7 copy-start

commit v5 on v4

--- a/solution.py
+++ b/solution.py
@@ -183,12 +183,18 @@
     return guess * (2.0 - x * guess)
 
 
-def eliminate(v, w, k, block, row, sub):
+def eliminate(v, w, k, block, row, sub, area):
     count = len(v)
-    line = [spread(v[block][row + i:row + i + 1]) for i in range(4)]
-    line_w = [spread(w[block][row + i:row + i + 1]) for i in range(4)] if w else []
+    area[0] = v[block]
+    line = [spread(area[0, row + i:row + i + 1, :]) for i in range(4)]
+    line_w = []
+    if w:
+        area[1] = w[block]
+        line_w = [spread(area[1, row + i:row + i + 1, :]) for i in range(4)]
     column = {j: [spread(v[j][:, k + i:k + i + 1]) for i in range(4)] for j in range(block, count)}
-    p = {(i, h): spread(column[block][i][row + h:row + h + 1]) for i in range(4) for h in range(i, 4)}
+    for i in range(4):
+        area[2 + i] = column[block][i]
+    p = {(i, h): spread(area[2 + i, row + h:row + h + 1, :]) for i in range(4) for h in range(i, 4)}
     inverse = reciprocal(p[0, 0] * p[1, 1] - p[0, 1] * p[0, 1])
     i00, i01, i11 = p[1, 1] * inverse, -(p[0, 1] * inverse), p[0, 0] * inverse
     f02, f12 = i00 * p[0, 2] + i01 * p[1, 2], i01 * p[0, 2] + i11 * p[1, 2]
@@ -222,7 +228,7 @@
             w[j] = w[j] - g0 * line_w[0] - g1 * line_w[1] - g2 * line_w[2] - g3 * line_w[3]
 
 
-def whiten_kernel(levels, rep_ref, *refs):
+def whiten_kernel(levels, area, rep_ref, *refs):
     x_refs, p_refs, q_refs = refs[:levels], refs[levels:2 * levels], refs[2 * levels:-1]
     out_ref = refs[-1]
     width = x_refs[0].shape[0]
@@ -245,7 +251,7 @@
         right = [[c[8 * j:8 * j + 8] for j in range(count)] if top == 0 else [] for c in columns]
         for kk in range(0, PANEL, 4):
             for m in range(levels):
-                eliminate(left[m], right[m], top + kk, kk // 8, kk % 8, sub)
+                eliminate(left[m], right[m], top + kk, kk // 8, kk % 8, sub, area.at[m, kk // 4 % 2])
         for m in range(levels):
             for j in range(count):
                 diagonal = jnp.sum(jnp.where(lane == sub + (top + 8 * j), left[m][j], 0.0), axis=1, keepdims=True)
@@ -268,10 +274,10 @@
 
 
 def last_kernel(levels, kind, side_ref, core_ref, rep_ref, own_ref, pair_ref, *refs):
-    x_refs, p_refs, q_refs = refs[: levels - 1], refs[levels - 1:2 * levels - 1], refs[2 * levels - 1:-2]
-    out_ref, x_last = refs[-2:]
+    x_refs, p_refs, q_refs = refs[: levels - 1], refs[levels - 1:2 * levels - 1], refs[2 * levels - 1:-3]
+    out_ref, x_last, area = refs[-3:]
     level_kernel(False, True, kind, False, side_ref, core_ref, own_ref, pair_ref, p_refs[-1], x_last)
-    whiten_kernel(levels, rep_ref, *x_refs, x_last, *p_refs, *q_refs, out_ref)
+    whiten_kernel(levels, area, rep_ref, *x_refs, x_last, *p_refs, *q_refs, out_ref)
 
 
 def call(kernel, out_shape, n_smem, n_vmem, scratch=()):
@@ -364,7 +370,8 @@
         if last:
             out = jax.ShapeDtypeStruct((levels, narrow, width), F32)
             kernel = functools.partial(last_kernel, levels, kind)
-            return call(kernel, out, 3, 3 * levels, [pltpu.VMEM((width, width), F32)])(
+            scratch = [pltpu.VMEM((width, width), F32), pltpu.VMEM((levels, 2, 6, 8, width), F32)]
+            return call(kernel, out, 3, 3 * levels, scratch)(
                 side, core, rep_scalar, sent, pair, *x_list, *p_list, *q_list
             )
         x, panel, q, sent, *rest = call(kernel, shapes, 2, 2 + len(state))(side, core, sent, pair, *state)

time: 133 us -> 127 us (0.955)
  blocking collectives: 86.6 us -> 79.9 us
    all_gather x7, blocking collectives: 73.2 us -> 66.5 us  [pair_gathered(): return lax.all_gather(value, axis, axis=0, axis_index_groups=groups)]
    pallas_call x6, Pallas kernels: 15.6 us -> 18.8 us  [local(): call(kernel, shapes, 2, 2 + len(state))(side, core, sent, pair, *state)]
    pallas_call x1, Pallas kernels: 12.4 us -> 10.3 us  [local(): call(kernel, out, 3, 3 * levels, scratch)]
where the time goes in v5:
time: 127 us
  blocking collectives  79.9 us (63%)
  Pallas kernels  32.6 us (26%)
  starting transfers between devices  11.4 us (9%)
  local copies, waits for them, and re-layouts  2.67 us (2%)
    all_gather x7, blocking collectives, pair_gathered(): return lax.all_gather(value, axis, axis=0, axis_index_groups=groups)  66.5 us
    pallas_call x6, Pallas kernels, local(): call(kernel, shapes, 2, 2 + len(state))(side, core, sent, pair, *state)  18.8 us
    all_gather x1, blocking collectives, local(): sent = lax.all_gather(mine, 'rep', axis=0, tiled=True)  13.4 us
    ppermute x3, starting transfers between devices, local(): lax.ppermute(levels_of(lax.rem(rep_index + shift, reps)), 'rep', pairs)  11.4 us
    pallas_call x1, Pallas kernels, local(): call(kernel, out, 3, 3 * levels, scratch)  10.3 us
  transfers between devices with their start and end apart: 3, of which 0 were waited for; matrix products, arithmetic and copies ran while one was open for 0% of the time, Pallas kernels for 2%

profile of v5, /device:TPU:24, one launch (start us, length us, event | category | flops | bytes accessed | tf_op | source)
XLA Modules:
  0.0 126.7 jit_solution(9317459853365295813)
XLA Ops:
  0.0 0.0 copy-start.1
  0.0 1.2 constant_dynamic-slice_fusion
  1.2 3.4 %collective-permute-start = (f32[2,32,512]{2,1,0:T(8,128)S(1)}, f32[2,32,512]{2,1,0:T(8,128)S(1)}, u32[]{:S(2)}, u32[]{:S(2)}) collective-permute-start(f32[2,32,512]{2,1,0:T(8,128)S(1)} %get-tuple-element.58), channel_id=1, source_target_pairs={{0,1},{1,2},{2,3},{3,0},{4,5},{5,6},{6,7},{7,4},{8,9},{9,10},{10,1... | collective-permute-start | bytes 393224 | tf_op jit(solution)/shard_map/ppermute | solution.py:339
  4.6 4.6 %collective-permute-start.1 = (f32[2,32,512]{2,1,0:T(8,128)S(1)}, f32[2,32,512]{2,1,0:T(8,128)S(1)}, u32[]{:S(2)}, u32[]{:S(2)}) collective-permute-start(f32[2,32,512]{2,1,0:T(8,128)S(1)} %get-tuple-element.60), channel_id=1, source_target_pairs={{0,2},{1,3},{2,0},{3,1},{4,6},{5,7},{6,4},{7,5},{8,10},{9,11},{10,... | collective-permute-start | bytes 393224 | tf_op jit(solution)/shard_map/ppermute | solution.py:339
  9.3 3.3 %collective-permute-start.2 = (f32[2,32,512]{2,1,0:T(8,128)S(1)}, f32[2,32,512]{2,1,0:T(8,128)S(1)}, u32[]{:S(2)}, u32[]{:S(2)}) collective-permute-start(f32[2,32,512]{2,1,0:T(8,128)S(1)} %get-tuple-element.57), channel_id=1, source_target_pairs={{0,3},{1,0},{2,1},{3,2},{4,7},{5,4},{6,5},{7,6},{8,11},{9,8},{10,9... | collective-permute-start | bytes 393224 | tf_op jit(solution)/shard_map/ppermute | solution.py:339
  12.6 0.0 copy-done.1
  12.6 0.0 copy-start.2
  12.6 0.5 reshape.39.blocks_ref
  13.2 0.1 copy-done.2
  13.3 0.1 copy.6.cols_ref
  13.4 0.0 copy-start
  13.4 0.7 copy-done
  14.1 2.3 %shard_map.46 = (bf16[512,512]{1,0:T(8,128)(2,1)S(1)}, bf16[512,512]{1,0:T(8,128)(2,1)S(1)}) custom-call(s32[8,4]{1,0:T(8,128)S(1)} %copy.6.cols_ref, f32[32,64,64]{2,1,0:T(8,128)S(1)} %reshape.39.blocks_ref, s32[1,512]{1,0:T(1,128)S(1)} %copy-done), custom_call_target="tpu_custom_call" | custom-call | tf_op jit(solution)/shard_map/pallas_call | solution.py:342
  16.4 0.0 collective-permute-done.refs_0_
  16.4 0.0 collective-permute-done.1.refs_1_
  16.4 0.0 collective-permute-done.2.refs_2_
  16.5 1.2 shard_map.47
  17.7 13.4 %all_gather.45.own_ref.refs_6_ = f32[8,128,128]{2,1,0:T(8,128)S(1)} all-gather(f32[2,128,128]{2,1,0:T(8,128)S(1)} %shard_map.47), channel_id=1, replica_groups=mesh['leaf'=128,'rep'=4] {'rep'}, dimensions={0}, use_global_device_ids=true | all-gather | bytes 655360 | tf_op jit(solution)/shard_map/all_gather | solution.py:349
  31.1 2.5 %all-gather = f32[14,128,128]{2,1,0:T(8,128)S(1)} all-gather(f32[7,128,128]{2,1,0:T(8,128)S(1)} %slice.4), channel_id=2, replica_groups={{0,4},{8,12},{16,20},{24,28},{32,36},{40,44},{48,52},{56,60},{64,68},{7..., dimensions={0}, use_global_device_ids=true | all-gather | bytes 1376256 | tf_op jit(solution)/shard_map/all_gather | solution.py:314
  33.5 4.1 %shard_map.48 = (f32[128,128]{1,0:T(8,128)S(1)}, f32[128,128]{1,0:T(8,128)S(1)}, f32[128,128]{1,0:T(8,128)S(1)}, f32[6,128,128]{2,1,0:T(8,128)S(1)}) custom-call(s32[1]{0:T(128)} %bitcast.8.side_ref, s32[1]{0:T(128)} %bitcast.1.core_ref, f32[8,128,128]{2,1,0:T(8,128)S(1)} %all_gather.45.own_ref.refs_6_, f32[2,7,128,128]{3,2,1,0:T(8,128)S(1)} %bitcast.16), custom_call_target="tpu_custom_call" | custom-call | tf_op jit(solution)/shard_map/pallas_call | solution.py:377
  37.7 11.8 %all-gather.1 = f32[12,128,128]{2,1,0:T(8,128)S(1)} all-gather(f32[6,128,128]{2,1,0:T(8,128)S(1)} %get-tuple-element.33.own_ref), channel_id=3, replica_groups={{0,8},{4,12},{16,24},{20,28},{32,40},{36,44},{48,56},{52,60},{64,72},{6..., dimensions={0}, use_global_device_ids=true | all-gather | bytes 1179648 | tf_op jit(solution)/shard_map/all_gather | solution.py:314
  49.5 2.5 %shard_map.49 = (f32[128,128]{1,0:T(8,128)S(1)}, f32[128,128]{1,0:T(8,128)S(1)}, f32[128,128]{1,0:T(8,128)S(1)}, f32[5,128,128]{2,1,0:T(8,128)S(1)}) custom-call(s32[1]{0:T(128)} %bitcast.7.side_ref, s32[1]{0:T(128)} %bitcast.1.core_ref, f32[6,128,128]{2,1,0:T(8,128)S(1)} %get-tuple-element.33.own_ref, f32[2,6,128,128]{3,2,1,0:T(8,128)S(1)} %bitcast.17, ...), custom_call_target="tpu_custom_call" | custom-call | tf_op jit(solution)/shard_map/pallas_call | solution.py:377
  52.0 11.1 %all-gather.2 = f32[10,128,128]{2,1,0:T(8,128)S(1)} all-gather(f32[5,128,128]{2,1,0:T(8,128)S(1)} %get-tuple-element.35.own_ref), channel_id=4, replica_groups={{0,24},{4,28},{8,16},{12,20},{32,56},{36,60},{40,48},{44,52},{64,88},{6..., dimensions={0}, use_global_device_ids=true | all-gather | bytes 983040 | tf_op jit(solution)/shard_map/all_gather | solution.py:314
  63.2 4.1 %shard_map.50 = (f32[128,128]{1,0:T(8,128)S(1)}, f32[128,128]{1,0:T(8,128)S(1)}, f32[128,128]{1,0:T(8,128)S(1)}, f32[4,128,128]{2,1,0:T(8,128)S(1)}) custom-call(s32[1]{0:T(128)} %bitcast.6.side_ref, s32[1]{0:T(128)} %bitcast.1.core_ref, f32[5,128,128]{2,1,0:T(8,128)S(1)} %get-tuple-element.35.own_ref, f32[2,5,128,128]{3,2,1,0:T(8,128)S(1)} %bitcast.18, ...), custom_call_target="tpu_custom_call" | custom-call | tf_op jit(solution)/shard_map/pallas_call | solution.py:377
  67.3 7.6 %all-gather.3 = f32[8,128,128]{2,1,0:T(8,128)S(1)} all-gather(f32[4,128,128]{2,1,0:T(8,128)S(1)} %get-tuple-element.37.own_ref), channel_id=5, replica_groups={{0,32},{4,36},{8,40},{12,44},{16,48},{20,52},{24,56},{28,60},{64,96},{6..., dimensions={0}, use_global_device_ids=true | all-gather | bytes 786432 | tf_op jit(solution)/shard_map/all_gather | solution.py:314
  74.9 2.5 %shard_map.51 = (f32[128,128]{1,0:T(8,128)S(1)}, f32[128,128]{1,0:T(8,128)S(1)}, f32[128,128]{1,0:T(8,128)S(1)}, f32[3,128,128]{2,1,0:T(8,128)S(1)}) custom-call(s32[1]{0:T(128)} %bitcast.5.side_ref, s32[1]{0:T(128)} %bitcast.1.core_ref, f32[4,128,128]{2,1,0:T(8,128)S(1)} %get-tuple-element.37.own_ref, f32[2,4,128,128]{3,2,1,0:T(8,128)S(1)} %bitcast.19, ...), custom_call_target="tpu_custom_call" | custom-call | tf_op jit(solution)/shard_map/pallas_call | solution.py:377
  77.4 8.3 %all-gather.4 = f32[6,128,128]{2,1,0:T(8,128)S(1)} all-gather(f32[3,128,128]{2,1,0:T(8,128)S(1)} %get-tuple-element.39.own_ref), channel_id=6, replica_groups={{0,96},{4,100},{8,104},{12,108},{16,112},{20,116},{24,120},{28,124},{32..., dimensions={0}, use_global_device_ids=true | all-gather | bytes 589824 | tf_op jit(solution)/shard_map/all_gather | solution.py:314
  85.7 2.8 %shard_map.52 = (f32[128,128]{1,0:T(8,128)S(1)}, f32[128,128]{1,0:T(8,128)S(1)}, f32[128,128]{1,0:T(8,128)S(1)}, f32[2,128,128]{2,1,0:T(8,128)S(1)}) custom-call(s32[1]{0:T(128)} %bitcast.4.side_ref, s32[1]{0:T(128)} %bitcast.1.core_ref, f32[3,128,128]{2,1,0:T(8,128)S(1)} %get-tuple-element.39.own_ref, f32[2,3,128,128]{3,2,1,0:T(8,128)S(1)} %bitcast.20, ...), custom_call_target="tpu_custom_call" | custom-call | tf_op jit(solution)/shard_map/pallas_call | solution.py:377
  88.5 16.4 %all-gather.5 = f32[4,128,128]{2,1,0:T(8,128)S(1)} all-gather(f32[2,128,128]{2,1,0:T(8,128)S(1)} %get-tuple-element.41.own_ref), channel_id=7, replica_groups={{0,128},{4,132},{8,136},{12,140},{16,144},{20,148},{24,152},{28,156},{3..., dimensions={0}, use_global_device_ids=true | all-gather | bytes 393216 | tf_op jit(solution)/shard_map/all_gather | solution.py:314
  104.9 2.7 %shard_map.53 = (f32[128,128]{1,0:T(8,128)S(1)}, f32[128,128]{1,0:T(8,128)S(1)}, f32[128,128]{1,0:T(8,128)S(1)}, f32[1,128,128]{2,1,0:T(8,128)S(1)}) custom-call(s32[1]{0:T(128)} %bitcast.3.side_ref, s32[1]{0:T(128)} %bitcast.1.core_ref, f32[2,128,128]{2,1,0:T(8,128)S(1)} %get-tuple-element.41.own_ref, f32[2,2,128,128]{3,2,1,0:T(8,128)S(1)} %bitcast.21, ...), custom_call_target="tpu_custom_call" | custom-call | tf_op jit(solution)/shard_map/pallas_call | solution.py:377
  107.6 8.9 %all-gather.6 = f32[2,128,128]{2,1,0:T(8,128)S(1)} all-gather(f32[1,128,128]{2,1,0:T(8,128)S(1)} %get-tuple-element.43.own_ref), channel_id=8, replica_groups={{0,384},{4,388},{8,392},{12,396},{16,400},{20,404},{24,408},{28,412},{3..., dimensions={0}, use_global_device_ids=true | all-gather | bytes 196608 | tf_op jit(solution)/shard_map/all_gather | solution.py:314
  116.4 10.3 %shard_map.54 = f32[7,32,128]{2,1,0:T(8,128)} custom-call(s32[1]{0:T(128)} %bitcast.side_ref, s32[1]{0:T(128)} %bitcast.1.core_ref, s32[1]{0:T(128)} %bitcast.2.rep_ref, f32[1,128,128]{2,1,0:T(8,128)S(1)} %get-tuple-element.43.own_ref, f32[2,1,128,128]{3,2,1,0:T(8,128)S(1)} %bitcast.22, f32[128,128]{1,0:T(8,128)S(1)} %get-tuple-element.44.refs_0_, ...), custom_call_target="tpu_custom_call" | custom-call | tf_op jit(solution)/shard_map/pallas_call | solution.py:374
  (1 shorter events, 0.0 us)
Async XLA Ops:
  0.0 12.6 %copy-start.1 = (f32[8,4,4096]{2,1,0:T(4,128)S(1)}, f32[8,4,4096]{2,1,0:T(4,128)}, u32[]{:S(2)}) copy-start(f32[8,4,4096]{2,1,0:T(4,128)} %param.5) | copy-start | bytes 1572868
  1.2 15.2 %collective-permute-start = (f32[2,32,512]{2,1,0:T(8,128)S(1)}, f32[2,32,512]{2,1,0:T(8,128)S(1)}, u32[]{:S(2)}, u32[]{:S(2)}) collective-permute-start(f32[2,32,512]{2,1,0:T(8,128)S(1)} %get-tuple-element.58), channel_id=1, source_target_pairs={{0,1},{1,2},{2,3},{3,0},{4,5},{5,6},{6,7},{7,4},{8,9},{9,10},{10,1... | collective-permute-start | bytes 393224 | tf_op jit(solution)/shard_map/ppermute | solution.py:339
  4.6 11.8 %collective-permute-start.1 = (f32[2,32,512]{2,1,0:T(8,128)S(1)}, f32[2,32,512]{2,1,0:T(8,128)S(1)}, u32[]{:S(2)}, u32[]{:S(2)}) collective-permute-start(f32[2,32,512]{2,1,0:T(8,128)S(1)} %get-tuple-element.60), channel_id=1, source_target_pairs={{0,2},{1,3},{2,0},{3,1},{4,6},{5,7},{6,4},{7,5},{8,10},{9,11},{10,... | collective-permute-start | bytes 393224 | tf_op jit(solution)/shard_map/ppermute | solution.py:339
  9.3 7.2 %collective-permute-start.2 = (f32[2,32,512]{2,1,0:T(8,128)S(1)}, f32[2,32,512]{2,1,0:T(8,128)S(1)}, u32[]{:S(2)}, u32[]{:S(2)}) collective-permute-start(f32[2,32,512]{2,1,0:T(8,128)S(1)} %get-tuple-element.57), channel_id=1, source_target_pairs={{0,3},{1,0},{2,1},{3,2},{4,7},{5,4},{6,5},{7,6},{8,11},{9,8},{10,9... | collective-permute-start | bytes 393224 | tf_op jit(solution)/shard_map/ppermute | solution.py:339
  12.6 0.7 copy-start.2
  13.4 0.7 copy-start

commit v6 on v5

--- a/solution.py
+++ b/solution.py
@@ -37,12 +37,16 @@
     return both[:, :half] + both[:, half:]
 
 
+def first_level(rep):
+    return jnp.maximum(2 * rep - 1, 0)
+
+
 def identity(n):
     rows = lax.broadcasted_iota(jnp.int32, (n, n), 0)
     return (rows == lax.broadcasted_iota(jnp.int32, (n, n), 1)).astype(F32)
 
 
-def dense_kernel(cols_ref, blocks_ref, order_ref, high_ref, low_ref, columns):
+def dense_kernel(cols_ref, blocks_ref, order_ref, high_ref, low_ref, select_ref, columns):
     block_rows, per_row = cols_ref.shape
     blk = blocks_ref.shape[1]
     rows = block_rows * blk
@@ -51,29 +55,28 @@
         for n in range(per_row):
             where = (cols_ref[q, n], slice(q * blk, (q + 1) * blk))
             columns[where] = columns[where] + blocks_ref[q * per_row + n]
-    tree = jnp.concatenate([columns[c] for c in range(block_rows)], axis=1)
+    high_ref[...], low_ref[...] = parts(jnp.concatenate([columns[c] for c in range(block_rows)], axis=1))
     bead = lax.broadcasted_iota(jnp.int32, (rows, rows), 0)
-    select = (bead == order_ref[...]).astype(F32).astype(BF16)
-    for piece, out in zip(parts(tree), (high_ref, low_ref)):
-        moved = contract(select, piece, ((1,), (0,))).astype(BF16)
-        out[...] = contract(moved, select, ((1,), (1,))).astype(BF16)
-
-
-def panel_kernel(rep_ref, own_ref, *refs):
-    reps = len(refs) - 3
-    pieces, (high_ref, low_ref, out_ref, basis_scr) = (own_ref, *refs[: reps - 1]), refs[reps - 1:]
-    own_levels, narrow, rows = own_ref.shape
+    select_ref[...] = (bead == order_ref[...]).astype(F32).astype(BF16)
+
+
+def panel_kernel(rep_ref, basis_ref, *refs):
+    narrow, rows = basis_ref.shape[1:]
+    pieces, (high_ref, low_ref, select_ref, out_ref, basis_scr) = refs[:-5], refs[-5:]
+    reps = len(pieces) + 1
+    own_levels = out_ref.shape[0]
     scale = 1.0 / math.sqrt(rows)
     width = reps * narrow
     rep = rep_ref[0]
-    for shift, piece in enumerate(pieces):
+    for shift in range(reps):
         source = lax.rem(rep + reps - shift, reps)
-        basis_scr[:, pl.ds(pl.multiple_of(source * narrow, narrow), narrow), :] = piece[...]
+        piece = pieces[shift - 1][...] if shift else basis_ref[pl.ds(first_level(rep), own_levels)]
+        basis_scr[:, pl.ds(pl.multiple_of(source * narrow, narrow), narrow), :] = piece
     panels = []
     for level in range(own_levels):
-        basis = parts(basis_scr[level])
-        image = product(basis, (high_ref[...], low_ref[...]))
-        panels.append(product(parts(image), basis, ((1,), (1,))) * scale)
+        ordered = tuple(contract(piece, select_ref[...], ((1,), (0,))).astype(BF16) for piece in parts(basis_scr[level]))
+        image = product(ordered, (high_ref[...], low_ref[...]))
+        panels.append(product(parts(image), ordered, ((1,), (1,))) * scale)
     pair = parts(panels[0])
     first = product(pair, pair, ((0,), (0,))) * (1.0 / width)
     out_ref[0] = panels[0]
@@ -331,20 +334,20 @@
     square = jax.ShapeDtypeStruct((width, width), F32)
 
     def levels_of(rep):
-        return lax.dynamic_slice_in_dim(basis, jnp.maximum(2 * rep - 1, 0), 2, 0)
-
-    pieces = [levels_of(rep_index)]
+        return lax.dynamic_slice_in_dim(basis, first_level(rep), 2, 0)
+
+    pieces = []
     for shift in range(1, reps):
         pairs = [(source, (source + shift) % reps) for source in range(reps)]
         pieces.append(lax.ppermute(levels_of(lax.rem(rep_index + shift, reps)), "rep", pairs))
     tiles = near_blocks.reshape(block_rows * per_row, blk, blk)
-    dense = [jax.ShapeDtypeStruct((rows, rows), BF16)] * 2
-    high, low = call(dense_kernel, dense, 1, 2, [pltpu.VMEM((block_rows, rows, blk), F32)])(
+    dense = [jax.ShapeDtypeStruct((rows, rows), BF16)] * 3
+    near = call(dense_kernel, dense, 1, 2, [pltpu.VMEM((block_rows, rows, blk), F32)])(
         near_cols, tiles, bead_order
     )
     two = jax.ShapeDtypeStruct((2, width, width), F32)
-    mine = call(panel_kernel, two, 1, reps + 2, [pltpu.VMEM((2, width, rows), F32)])(
-        rep_scalar, *pieces, high, low
+    mine = call(panel_kernel, two, 1, reps + 3, [pltpu.VMEM((2, width, rows), F32)])(
+        rep_scalar, basis, *pieces, *near
     )
     sent = lax.all_gather(mine, "rep", axis=0, tiled=True)
     core = (leaf_index & 1).astype(jnp.int32).reshape(1)

time: 127 us -> 128 us (level)
  Pallas kernels: 32.6 us -> 30.5 us
  blocking collectives: 79.9 us -> 81.8 us
    all_gather x7, blocking collectives: 66.5 us -> 68.4 us  [pair_gathered(): return lax.all_gather(value, axis, axis=0, axis_index_groups=groups)]
    pallas_call x6, Pallas kernels: 18.8 us -> 17 us  [local(): call(kernel, shapes, 2, 2 + len(state))(side, core, sent, pair, *state)]
  transfers between devices with their start and end apart: 3 -> 3, of which waited for: 0 -> 1; matrix products, arithmetic and copies ran while one was open for 0% -> 0% of each run, Pallas kernels for 2% -> 1%
where the time goes in v6:
time: 128 us; the launch traced here: 127 us
  blocking collectives  81.8 us (64%)
  Pallas kernels  30.5 us (24%)
  starting transfers between devices  11.4 us (9%)
  local copies, waits for them, and re-layouts  2.59 us (2%)
    all_gather x7, blocking collectives, pair_gathered(): return lax.all_gather(value, axis, axis=0, axis_index_groups=groups)  68.4 us
    pallas_call x6, Pallas kernels, local(): call(kernel, shapes, 2, 2 + len(state))(side, core, sent, pair, *state)  17 us
    all_gather x1, blocking collectives, local(): sent = lax.all_gather(mine, 'rep', axis=0, tiled=True)  13.4 us
    ppermute x3, starting transfers between devices, local(): lax.ppermute(levels_of(lax.rem(rep_index + shift, reps)), 'rep', pairs)  11.4 us
    pallas_call x1, Pallas kernels, local(): call(kernel, out, 3, 3 * levels, scratch)  10.4 us
  transfers between devices with their start and end apart: 3, of which 1 were waited for; matrix products, arithmetic and copies ran while one was open for 0% of the time, Pallas kernels for 1%

profile of v6, /device:TPU:24, one launch (start us, length us, event | category | flops | bytes accessed | tf_op | source)
XLA Modules:
  0.0 127.0 jit_solution(17827043871949356586)
XLA Ops:
  0.0 0.0 copy-start.2
  0.0 1.1 constant_dynamic-slice_fusion
  1.1 3.4 %collective-permute-start = (f32[2,32,512]{2,1,0:T(8,128)S(1)}, f32[2,32,512]{2,1,0:T(8,128)S(1)}, u32[]{:S(2)}, u32[]{:S(2)}) collective-permute-start(f32[2,32,512]{2,1,0:T(8,128)S(1)} %get-tuple-element.61), channel_id=1, source_target_pairs={{0,1},{1,2},{2,3},{3,0},{4,5},{5,6},{6,7},{7,4},{8,9},{9,10},{10,1... | collective-permute-start | bytes 393224 | tf_op jit(solution)/shard_map/ppermute | solution.py:342
  4.5 4.6 %collective-permute-start.1 = (f32[2,32,512]{2,1,0:T(8,128)S(1)}, f32[2,32,512]{2,1,0:T(8,128)S(1)}, u32[]{:S(2)}, u32[]{:S(2)}) collective-permute-start(f32[2,32,512]{2,1,0:T(8,128)S(1)} %get-tuple-element.60), channel_id=1, source_target_pairs={{0,2},{1,3},{2,0},{3,1},{4,6},{5,7},{6,4},{7,5},{8,10},{9,11},{10,... | collective-permute-start | bytes 393224 | tf_op jit(solution)/shard_map/ppermute | solution.py:342
  9.2 3.3 %collective-permute-start.2 = (f32[2,32,512]{2,1,0:T(8,128)S(1)}, f32[2,32,512]{2,1,0:T(8,128)S(1)}, u32[]{:S(2)}, u32[]{:S(2)}) collective-permute-start(f32[2,32,512]{2,1,0:T(8,128)S(1)} %get-tuple-element.59), channel_id=1, source_target_pairs={{0,3},{1,0},{2,1},{3,2},{4,7},{5,4},{6,5},{7,6},{8,11},{9,8},{10,9... | collective-permute-start | bytes 393224 | tf_op jit(solution)/shard_map/ppermute | solution.py:342
  12.5 0.0 copy-done.2
  12.5 0.0 copy-start.3
  12.6 0.5 reshape.39.blocks_ref
  13.1 0.1 copy-done.3
  13.2 0.1 copy.6.cols_ref
  13.3 0.0 copy-start.1
  13.3 0.7 copy-done.1
  14.0 0.0 copy-start
  14.0 1.4 %shard_map.46 = (bf16[512,512]{1,0:T(8,128)(2,1)S(1)}, bf16[512,512]{1,0:T(8,128)(2,1)S(1)}, bf16[512,512]{1,0:T(8,128)(2,1)S(1)}) custom-call(s32[8,4]{1,0:T(8,128)S(1)} %copy.6.cols_ref, f32[32,64,64]{2,1,0:T(8,128)S(1)} %reshape.39.blocks_ref, s32[1,512]{1,0:T(1,128)S(1)} %copy-done.1), custom_call_target="tpu_custom_call" | custom-call | tf_op jit(solution)/shard_map/pallas_call | solution.py:345
  15.4 0.0 collective-permute-done.refs_0_
  15.4 0.0 collective-permute-done.1.refs_1_
  15.4 0.6 collective-permute-done.2.refs_2_
  16.0 0.0 copy-done
  16.0 1.6 %shard_map.47 = f32[2,128,128]{2,1,0:T(8,128)S(1)} custom-call(s32[1]{0:T(128)} %bitcast.2.rep_ref, f32[7,32,512]{2,1,0:T(8,128)S(1)} %copy-done, f32[2,32,512]{2,1,0:T(8,128)S(1)} %collective-permute-done.refs_0_, f32[2,32,512]{2,1,0:T(8,128)S(1)} %collective-permute-done.1.refs_1_, f32[2,32,512]{2,1,0:T(8,128)S(1)} %collective-permute-done.2.refs_2_, ...), custom_call_target="tpu_custom_call" | custom-call | tf_op jit(solution)/shard_map/pallas_call | solution.py:349
  17.7 13.4 %all_gather.45.own_ref.refs_6_ = f32[8,128,128]{2,1,0:T(8,128)S(1)} all-gather(f32[2,128,128]{2,1,0:T(8,128)S(1)} %shard_map.47), channel_id=1, replica_groups=mesh['leaf'=128,'rep'=4] {'rep'}, dimensions={0}, use_global_device_ids=true | all-gather | bytes 655360 | tf_op jit(solution)/shard_map/all_gather | solution.py:352
  31.1 2.5 %all-gather = f32[14,128,128]{2,1,0:T(8,128)S(1)} all-gather(f32[7,128,128]{2,1,0:T(8,128)S(1)} %slice.4), channel_id=2, replica_groups={{0,4},{8,12},{16,20},{24,28},{32,36},{40,44},{48,52},{56,60},{64,68},{7..., dimensions={0}, use_global_device_ids=true | all-gather | bytes 1376256 | tf_op jit(solution)/shard_map/all_gather | solution.py:317
  33.6 4.1 %shard_map.48 = (f32[128,128]{1,0:T(8,128)S(1)}, f32[128,128]{1,0:T(8,128)S(1)}, f32[128,128]{1,0:T(8,128)S(1)}, f32[6,128,128]{2,1,0:T(8,128)S(1)}) custom-call(s32[1]{0:T(128)} %bitcast.8.side_ref, s32[1]{0:T(128)} %bitcast.1.core_ref, f32[8,128,128]{2,1,0:T(8,128)S(1)} %all_gather.45.own_ref.refs_6_, f32[2,7,128,128]{3,2,1,0:T(8,128)S(1)} %bitcast.16), custom_call_target="tpu_custom_call" | custom-call | tf_op jit(solution)/shard_map/pallas_call | solution.py:380
  37.8 11.8 %all-gather.1 = f32[12,128,128]{2,1,0:T(8,128)S(1)} all-gather(f32[6,128,128]{2,1,0:T(8,128)S(1)} %get-tuple-element.35.own_ref), channel_id=3, replica_groups={{0,8},{4,12},{16,24},{20,28},{32,40},{36,44},{48,56},{52,60},{64,72},{6..., dimensions={0}, use_global_device_ids=true | all-gather | bytes 1179648 | tf_op jit(solution)/shard_map/all_gather | solution.py:317
  49.6 2.8 %shard_map.49 = (f32[128,128]{1,0:T(8,128)S(1)}, f32[128,128]{1,0:T(8,128)S(1)}, f32[128,128]{1,0:T(8,128)S(1)}, f32[5,128,128]{2,1,0:T(8,128)S(1)}) custom-call(s32[1]{0:T(128)} %bitcast.7.side_ref, s32[1]{0:T(128)} %bitcast.1.core_ref, f32[6,128,128]{2,1,0:T(8,128)S(1)} %get-tuple-element.35.own_ref, f32[2,6,128,128]{3,2,1,0:T(8,128)S(1)} %bitcast.17, ...), custom_call_target="tpu_custom_call" | custom-call | tf_op jit(solution)/shard_map/pallas_call | solution.py:380
  52.4 10.8 %all-gather.2 = f32[10,128,128]{2,1,0:T(8,128)S(1)} all-gather(f32[5,128,128]{2,1,0:T(8,128)S(1)} %get-tuple-element.37.own_ref), channel_id=4, replica_groups={{0,24},{4,28},{8,16},{12,20},{32,56},{36,60},{40,48},{44,52},{64,88},{6..., dimensions={0}, use_global_device_ids=true | all-gather | bytes 983040 | tf_op jit(solution)/shard_map/all_gather | solution.py:317
  63.2 2.5 %shard_map.50 = (f32[128,128]{1,0:T(8,128)S(1)}, f32[128,128]{1,0:T(8,128)S(1)}, f32[128,128]{1,0:T(8,128)S(1)}, f32[4,128,128]{2,1,0:T(8,128)S(1)}) custom-call(s32[1]{0:T(128)} %bitcast.6.side_ref, s32[1]{0:T(128)} %bitcast.1.core_ref, f32[5,128,128]{2,1,0:T(8,128)S(1)} %get-tuple-element.37.own_ref, f32[2,5,128,128]{3,2,1,0:T(8,128)S(1)} %bitcast.18, ...), custom_call_target="tpu_custom_call" | custom-call | tf_op jit(solution)/shard_map/pallas_call | solution.py:380
  65.8 7.4 %all-gather.3 = f32[8,128,128]{2,1,0:T(8,128)S(1)} all-gather(f32[4,128,128]{2,1,0:T(8,128)S(1)} %get-tuple-element.39.own_ref), channel_id=5, replica_groups={{0,32},{4,36},{8,40},{12,44},{16,48},{20,52},{24,56},{28,60},{64,96},{6..., dimensions={0}, use_global_device_ids=true | all-gather | bytes 786432 | tf_op jit(solution)/shard_map/all_gather | solution.py:317
  73.2 2.5 %shard_map.51 = (f32[128,128]{1,0:T(8,128)S(1)}, f32[128,128]{1,0:T(8,128)S(1)}, f32[128,128]{1,0:T(8,128)S(1)}, f32[3,128,128]{2,1,0:T(8,128)S(1)}) custom-call(s32[1]{0:T(128)} %bitcast.5.side_ref, s32[1]{0:T(128)} %bitcast.1.core_ref, f32[4,128,128]{2,1,0:T(8,128)S(1)} %get-tuple-element.39.own_ref, f32[2,4,128,128]{3,2,1,0:T(8,128)S(1)} %bitcast.19, ...), custom_call_target="tpu_custom_call" | custom-call | tf_op jit(solution)/shard_map/pallas_call | solution.py:380
  75.7 8.3 %all-gather.4 = f32[6,128,128]{2,1,0:T(8,128)S(1)} all-gather(f32[3,128,128]{2,1,0:T(8,128)S(1)} %get-tuple-element.41.own_ref), channel_id=6, replica_groups={{0,96},{4,100},{8,104},{12,108},{16,112},{20,116},{24,120},{28,124},{32..., dimensions={0}, use_global_device_ids=true | all-gather | bytes 589824 | tf_op jit(solution)/shard_map/all_gather | solution.py:317
  84.0 2.5 %shard_map.52 = (f32[128,128]{1,0:T(8,128)S(1)}, f32[128,128]{1,0:T(8,128)S(1)}, f32[128,128]{1,0:T(8,128)S(1)}, f32[2,128,128]{2,1,0:T(8,128)S(1)}) custom-call(s32[1]{0:T(128)} %bitcast.4.side_ref, s32[1]{0:T(128)} %bitcast.1.core_ref, f32[3,128,128]{2,1,0:T(8,128)S(1)} %get-tuple-element.41.own_ref, f32[2,3,128,128]{3,2,1,0:T(8,128)S(1)} %bitcast.20, ...), custom_call_target="tpu_custom_call" | custom-call | tf_op jit(solution)/shard_map/pallas_call | solution.py:380
  86.5 18.7 %all-gather.5 = f32[4,128,128]{2,1,0:T(8,128)S(1)} all-gather(f32[2,128,128]{2,1,0:T(8,128)S(1)} %get-tuple-element.43.own_ref), channel_id=7, replica_groups={{0,128},{4,132},{8,136},{12,140},{16,144},{20,148},{24,152},{28,156},{3..., dimensions={0}, use_global_device_ids=true | all-gather | bytes 393216 | tf_op jit(solution)/shard_map/all_gather | solution.py:317
  105.2 2.5 %shard_map.53 = (f32[128,128]{1,0:T(8,128)S(1)}, f32[128,128]{1,0:T(8,128)S(1)}, f32[128,128]{1,0:T(8,128)S(1)}, f32[1,128,128]{2,1,0:T(8,128)S(1)}) custom-call(s32[1]{0:T(128)} %bitcast.3.side_ref, s32[1]{0:T(128)} %bitcast.1.core_ref, f32[2,128,128]{2,1,0:T(8,128)S(1)} %get-tuple-element.43.own_ref, f32[2,2,128,128]{3,2,1,0:T(8,128)S(1)} %bitcast.21, ...), custom_call_target="tpu_custom_call" | custom-call | tf_op jit(solution)/shard_map/pallas_call | solution.py:380
  107.7 8.9 %all-gather.6 = f32[2,128,128]{2,1,0:T(8,128)S(1)} all-gather(f32[1,128,128]{2,1,0:T(8,128)S(1)} %get-tuple-element.45.own_ref), channel_id=8, replica_groups={{0,384},{4,388},{8,392},{12,396},{16,400},{20,404},{24,408},{28,412},{3..., dimensions={0}, use_global_device_ids=true | all-gather | bytes 196608 | tf_op jit(solution)/shard_map/all_gather | solution.py:317
  116.6 10.4 %shard_map.54 = f32[7,32,128]{2,1,0:T(8,128)} custom-call(s32[1]{0:T(128)} %bitcast.side_ref, s32[1]{0:T(128)} %bitcast.1.core_ref, s32[1]{0:T(128)} %bitcast.2.rep_ref, f32[1,128,128]{2,1,0:T(8,128)S(1)} %get-tuple-element.45.own_ref, f32[2,1,128,128]{3,2,1,0:T(8,128)S(1)} %bitcast.22, f32[128,128]{1,0:T(8,128)S(1)} %get-tuple-element.46.refs_0_, ...), custom_call_target="tpu_custom_call" | custom-call | tf_op jit(solution)/shard_map/pallas_call | solution.py:377
  (1 shorter events, 0.0 us)
Async XLA Ops:
  0.0 12.5 %copy-start.2 = (f32[8,4,4096]{2,1,0:T(4,128)S(1)}, f32[8,4,4096]{2,1,0:T(4,128)}, u32[]{:S(2)}) copy-start(f32[8,4,4096]{2,1,0:T(4,128)} %param.5) | copy-start | bytes 1572868
  1.1 14.3 %collective-permute-start = (f32[2,32,512]{2,1,0:T(8,128)S(1)}, f32[2,32,512]{2,1,0:T(8,128)S(1)}, u32[]{:S(2)}, u32[]{:S(2)}) collective-permute-start(f32[2,32,512]{2,1,0:T(8,128)S(1)} %get-tuple-element.61), channel_id=1, source_target_pairs={{0,1},{1,2},{2,3},{3,0},{4,5},{5,6},{6,7},{7,4},{8,9},{9,10},{10,1... | collective-permute-start | bytes 393224 | tf_op jit(solution)/shard_map/ppermute | solution.py:342
  4.5 10.9 %collective-permute-start.1 = (f32[2,32,512]{2,1,0:T(8,128)S(1)}, f32[2,32,512]{2,1,0:T(8,128)S(1)}, u32[]{:S(2)}, u32[]{:S(2)}) collective-permute-start(f32[2,32,512]{2,1,0:T(8,128)S(1)} %get-tuple-element.60), channel_id=1, source_target_pairs={{0,2},{1,3},{2,0},{3,1},{4,6},{5,7},{6,4},{7,5},{8,10},{9,11},{10,... | collective-permute-start | bytes 393224 | tf_op jit(solution)/shard_map/ppermute | solution.py:342
  9.2 6.9 %collective-permute-start.2 = (f32[2,32,512]{2,1,0:T(8,128)S(1)}, f32[2,32,512]{2,1,0:T(8,128)S(1)}, u32[]{:S(2)}, u32[]{:S(2)}) collective-permute-start(f32[2,32,512]{2,1,0:T(8,128)S(1)} %get-tuple-element.59), channel_id=1, source_target_pairs={{0,3},{1,0},{2,1},{3,2},{4,7},{5,4},{6,5},{7,6},{8,11},{9,8},{10,9... | collective-permute-start | bytes 393224 | tf_op jit(solution)/shard_map/ppermute | solution.py:342
  12.5 0.7 copy-start.3
  13.3 0.7 copy-start.1
  14.0 2.0 %copy-start = (f32[7,32,512]{2,1,0:T(8,128)S(1)}, f32[7,32,512]{2,1,0:T(8,128)}, u32[]{:S(2)}) copy-start(f32[7,32,512]{2,1,0:T(8,128)} %basis_ref.1) | copy-start | bytes 1376260

commit v7 on v5

--- a/solution.py
+++ b/solution.py
@@ -11,7 +11,7 @@
 F32 = jnp.float32
 BF16 = jnp.bfloat16
 PANEL = 32
-EXCHANGE = ("pair",) * 7
+EXCHANGE = ("pair",) * 5 + ("packed", "packed")
 VMEM_BYTES = 48 * 1024 * 1024
 
 
@@ -80,6 +80,19 @@
     out_ref[1] = jnp.where(rep == 0, first, panels[1])
 
 
+def packed(matrix):
+    half = matrix.shape[0] // 2
+    block = matrix[half:, half:]
+    return jnp.concatenate([matrix[:half], jnp.concatenate([block[:half // 2], block[half // 2:]], axis=1)], axis=0)
+
+
+def unpacked(rows):
+    half = rows.shape[1] // 2
+    upper, block = rows[:half], rows[half:]
+    lower = jnp.concatenate([block[:, :half], block[:, half:]], axis=0)
+    return jnp.concatenate([upper, jnp.concatenate([upper[:, half:].T, lower], axis=1)], axis=0)
+
+
 def level_kernel(first, last, kind, split, side_ref, core_ref, own_ref, pair_ref, *refs):
     width = own_ref.shape[1]
     eye = identity(width)
@@ -95,6 +108,10 @@
             return pair_ref[n]
         if kind == "pair":
             return pair_ref[1 - side, n]
+        if kind == "packed":
+            if n:
+                return pair_ref[1 - side, width * n - width // 4:width * (n + 1) - width // 4, :]
+            return unpacked(pair_ref[1 - side, :width * 3 // 4, :])
         if kind == "halfother":
             return jnp.concatenate([pair_ref[core, n] for core in range(2)], axis=0)
         return jnp.concatenate([pair_ref[core, 1 - side, n] for core in range(2)], axis=0)
@@ -161,7 +178,11 @@
         next_panel_ref[...] = next_panel
         for upper in range(1, next_ref.shape[0]):
             next_ref[upper] = (ours(upper + 1) + theirs(upper + 1)) * root_half
-        if split:
+        if split == "packed":
+            outs[4][:width * 3 // 4] = packed(next_ref[0])
+            for upper in range(1, next_ref.shape[0]):
+                outs[4][width * upper - width // 4:width * (upper + 1) - width // 4] = next_ref[upper]
+        elif split:
             half_rows = width // 2
             outs[4][...] = next_ref[:, pl.ds(pl.multiple_of(core_ref[0] * half_rows, half_rows), half_rows), :]
         r = residuals[1]
@@ -353,17 +374,19 @@
     for bit in range(levels):
         first, last = bit == 0, bit == levels - 1
         kind = EXCHANGE[bit]
-        value = half if kind.startswith("half") else sent[1:] if first else sent
+        value = half if kind[0] in "hp" and half is not None else sent[1:] if first else sent
         pair = (swapped if kind.endswith("other") else pair_gathered)(value, "leaf", bit)
         if kind.startswith("half"):
             pair = pair_gathered(pair, "leaf", 0)
         side = (leaf_index >> bit & 1).astype(jnp.int32).reshape(1)
-        split = not last and EXCHANGE[bit + 1].startswith("half")
+        split = "" if last or EXCHANGE[bit + 1] in ("pair", "other") else EXCHANGE[bit + 1]
         shapes = [square]
         if not last:
             count = levels - bit - 1
             shapes += [square, square, jax.ShapeDtypeStruct((count, width, width), F32)]
-            if split:
+            if split == "packed":
+                shapes.append(jax.ShapeDtypeStruct((count * width - width // 4, width), F32))
+            elif split:
                 shapes.append(jax.ShapeDtypeStruct((count, width // 2, width), F32))
         kernel = functools.partial(level_kernel, first, last, kind, split)
         state = [] if first else [panel]

time: 127 us -> 127 us (level)
  Pallas kernels: 32.6 us -> 29.7 us
  blocking collectives: 79.9 us -> 81.9 us
    pallas_call x6, Pallas kernels: 18.8 us -> 15.7 us  [local(): call(kernel, shapes, 2, 2 + len(state))(side, core, sent, pair, *state)]
    all_gather x7, blocking collectives: 66.5 us -> 68.5 us  [pair_gathered(): return lax.all_gather(value, axis, axis=0, axis_index_groups=groups)]
where the time goes in v7:
time: 127 us; the launch traced here: 126 us
  blocking collectives  81.9 us (64%)
  Pallas kernels  29.7 us (23%)
  starting transfers between devices  11.4 us (9%)
  local copies, waits for them, and re-layouts  2.67 us (2%)
    all_gather x7, blocking collectives, pair_gathered(): return lax.all_gather(value, axis, axis=0, axis_index_groups=groups)  68.5 us
    pallas_call x6, Pallas kernels, local(): call(kernel, shapes, 2, 2 + len(state))(side, core, sent, pair, *state)  15.7 us
    all_gather x1, blocking collectives, local(): sent = lax.all_gather(mine, 'rep', axis=0, tiled=True)  13.4 us
    ppermute x3, starting transfers between devices, local(): lax.ppermute(levels_of(lax.rem(rep_index + shift, reps)), 'rep', pairs)  11.4 us
    pallas_call x1, Pallas kernels, local(): call(kernel, out, 3, 3 * levels, scratch)  10.4 us
  transfers between devices with their start and end apart: 3, of which 0 were waited for; matrix products, arithmetic and copies ran while one was open for 0% of the time, Pallas kernels for 2%

profile of v7, /device:TPU:24, one launch (start us, length us, event | category | flops | bytes accessed | tf_op | source)
XLA Modules:
  0.0 125.8 jit_solution(12666435477463196604)
XLA Ops:
  0.0 0.0 copy-start.1
  0.0 1.2 constant_dynamic-slice_fusion
  1.2 3.4 %collective-permute-start = (f32[2,32,512]{2,1,0:T(8,128)S(1)}, f32[2,32,512]{2,1,0:T(8,128)S(1)}, u32[]{:S(2)}, u32[]{:S(2)}) collective-permute-start(f32[2,32,512]{2,1,0:T(8,128)S(1)} %get-tuple-element.62), channel_id=1, source_target_pairs={{0,1},{1,2},{2,3},{3,0},{4,5},{5,6},{6,7},{7,4},{8,9},{9,10},{10,1... | collective-permute-start | bytes 393224 | tf_op jit(solution)/shard_map/ppermute | solution.py:360
  4.6 4.6 %collective-permute-start.1 = (f32[2,32,512]{2,1,0:T(8,128)S(1)}, f32[2,32,512]{2,1,0:T(8,128)S(1)}, u32[]{:S(2)}, u32[]{:S(2)}) collective-permute-start(f32[2,32,512]{2,1,0:T(8,128)S(1)} %get-tuple-element.64), channel_id=1, source_target_pairs={{0,2},{1,3},{2,0},{3,1},{4,6},{5,7},{6,4},{7,5},{8,10},{9,11},{10,... | collective-permute-start | bytes 393224 | tf_op jit(solution)/shard_map/ppermute | solution.py:360
  9.3 3.3 %collective-permute-start.2 = (f32[2,32,512]{2,1,0:T(8,128)S(1)}, f32[2,32,512]{2,1,0:T(8,128)S(1)}, u32[]{:S(2)}, u32[]{:S(2)}) collective-permute-start(f32[2,32,512]{2,1,0:T(8,128)S(1)} %get-tuple-element.61), channel_id=1, source_target_pairs={{0,3},{1,0},{2,1},{3,2},{4,7},{5,4},{6,5},{7,6},{8,11},{9,8},{10,9... | collective-permute-start | bytes 393224 | tf_op jit(solution)/shard_map/ppermute | solution.py:360
  12.6 0.0 copy-done.1
  12.6 0.0 copy-start.2
  12.6 0.5 reshape.39.blocks_ref
  13.2 0.1 copy-done.2
  13.3 0.1 copy.6.cols_ref
  13.4 0.0 copy-start
  13.4 0.7 copy-done
  14.1 2.3 %shard_map.46 = (bf16[512,512]{1,0:T(8,128)(2,1)S(1)}, bf16[512,512]{1,0:T(8,128)(2,1)S(1)}) custom-call(s32[8,4]{1,0:T(8,128)S(1)} %copy.6.cols_ref, f32[32,64,64]{2,1,0:T(8,128)S(1)} %reshape.39.blocks_ref, s32[1,512]{1,0:T(1,128)S(1)} %copy-done), custom_call_target="tpu_custom_call" | custom-call | tf_op jit(solution)/shard_map/pallas_call | solution.py:363
  16.4 0.0 collective-permute-done.refs_0_
  16.4 0.0 collective-permute-done.1.refs_1_
  16.4 0.0 collective-permute-done.2.refs_2_
  16.5 1.2 shard_map.47
  17.7 13.4 %all_gather.45.own_ref.refs_6_ = f32[8,128,128]{2,1,0:T(8,128)S(1)} all-gather(f32[2,128,128]{2,1,0:T(8,128)S(1)} %shard_map.47), channel_id=1, replica_groups=mesh['leaf'=128,'rep'=4] {'rep'}, dimensions={0}, use_global_device_ids=true | all-gather | bytes 655360 | tf_op jit(solution)/shard_map/all_gather | solution.py:370
  31.1 2.5 %all-gather = f32[14,128,128]{2,1,0:T(8,128)S(1)} all-gather(f32[7,128,128]{2,1,0:T(8,128)S(1)} %slice.4), channel_id=2, replica_groups={{0,4},{8,12},{16,20},{24,28},{32,36},{40,44},{48,52},{56,60},{64,68},{7..., dimensions={0}, use_global_device_ids=true | all-gather | bytes 1376256 | tf_op jit(solution)/shard_map/all_gather | solution.py:335
  33.5 2.8 %shard_map.48 = (f32[128,128]{1,0:T(8,128)S(1)}, f32[128,128]{1,0:T(8,128)S(1)}, f32[128,128]{1,0:T(8,128)S(1)}, f32[6,128,128]{2,1,0:T(8,128)S(1)}) custom-call(s32[1]{0:T(128)} %bitcast.8.side_ref, s32[1]{0:T(128)} %bitcast.1.core_ref, f32[8,128,128]{2,1,0:T(8,128)S(1)} %all_gather.45.own_ref.refs_6_, f32[2,7,128,128]{3,2,1,0:T(8,128)S(1)} %bitcast.16), custom_call_target="tpu_custom_call" | custom-call | tf_op jit(solution)/shard_map/pallas_call | solution.py:400
  36.4 11.8 %all-gather.1 = f32[12,128,128]{2,1,0:T(8,128)S(1)} all-gather(f32[6,128,128]{2,1,0:T(8,128)S(1)} %get-tuple-element.35.own_ref), channel_id=3, replica_groups={{0,8},{4,12},{16,24},{20,28},{32,40},{36,44},{48,56},{52,60},{64,72},{6..., dimensions={0}, use_global_device_ids=true | all-gather | bytes 1179648 | tf_op jit(solution)/shard_map/all_gather | solution.py:335
  48.2 2.5 %shard_map.49 = (f32[128,128]{1,0:T(8,128)S(1)}, f32[128,128]{1,0:T(8,128)S(1)}, f32[128,128]{1,0:T(8,128)S(1)}, f32[5,128,128]{2,1,0:T(8,128)S(1)}) custom-call(s32[1]{0:T(128)} %bitcast.7.side_ref, s32[1]{0:T(128)} %bitcast.1.core_ref, f32[6,128,128]{2,1,0:T(8,128)S(1)} %get-tuple-element.35.own_ref, f32[2,6,128,128]{3,2,1,0:T(8,128)S(1)} %bitcast.17, ...), custom_call_target="tpu_custom_call" | custom-call | tf_op jit(solution)/shard_map/pallas_call | solution.py:400
  50.7 10.8 %all-gather.2 = f32[10,128,128]{2,1,0:T(8,128)S(1)} all-gather(f32[5,128,128]{2,1,0:T(8,128)S(1)} %get-tuple-element.37.own_ref), channel_id=4, replica_groups={{0,24},{4,28},{8,16},{12,20},{32,56},{36,60},{40,48},{44,52},{64,88},{6..., dimensions={0}, use_global_device_ids=true | all-gather | bytes 983040 | tf_op jit(solution)/shard_map/all_gather | solution.py:335
  61.6 2.5 %shard_map.50 = (f32[128,128]{1,0:T(8,128)S(1)}, f32[128,128]{1,0:T(8,128)S(1)}, f32[128,128]{1,0:T(8,128)S(1)}, f32[4,128,128]{2,1,0:T(8,128)S(1)}) custom-call(s32[1]{0:T(128)} %bitcast.6.side_ref, s32[1]{0:T(128)} %bitcast.1.core_ref, f32[5,128,128]{2,1,0:T(8,128)S(1)} %get-tuple-element.37.own_ref, f32[2,5,128,128]{3,2,1,0:T(8,128)S(1)} %bitcast.18, ...), custom_call_target="tpu_custom_call" | custom-call | tf_op jit(solution)/shard_map/pallas_call | solution.py:400
  64.1 7.3 %all-gather.3 = f32[8,128,128]{2,1,0:T(8,128)S(1)} all-gather(f32[4,128,128]{2,1,0:T(8,128)S(1)} %get-tuple-element.39.own_ref), channel_id=5, replica_groups={{0,32},{4,36},{8,40},{12,44},{16,48},{20,52},{24,56},{28,60},{64,96},{6..., dimensions={0}, use_global_device_ids=true | all-gather | bytes 786432 | tf_op jit(solution)/shard_map/all_gather | solution.py:335
  71.4 2.5 %shard_map.51 = (f32[128,128]{1,0:T(8,128)S(1)}, f32[128,128]{1,0:T(8,128)S(1)}, f32[128,128]{1,0:T(8,128)S(1)}, f32[3,128,128]{2,1,0:T(8,128)S(1)}) custom-call(s32[1]{0:T(128)} %bitcast.5.side_ref, s32[1]{0:T(128)} %bitcast.1.core_ref, f32[4,128,128]{2,1,0:T(8,128)S(1)} %get-tuple-element.39.own_ref, f32[2,4,128,128]{3,2,1,0:T(8,128)S(1)} %bitcast.19, ...), custom_call_target="tpu_custom_call" | custom-call | tf_op jit(solution)/shard_map/pallas_call | solution.py:400
  73.9 8.7 %all-gather.4 = f32[6,128,128]{2,1,0:T(8,128)S(1)} all-gather(f32[3,128,128]{2,1,0:T(8,128)S(1)} %get-tuple-element.41.own_ref), channel_id=6, replica_groups={{0,96},{4,100},{8,104},{12,108},{16,112},{20,116},{24,120},{28,124},{32..., dimensions={0}, use_global_device_ids=true | all-gather | bytes 589824 | tf_op jit(solution)/shard_map/all_gather | solution.py:335
  82.6 2.5 %shard_map.52 = (f32[128,128]{1,0:T(8,128)S(1)}, f32[128,128]{1,0:T(8,128)S(1)}, f32[128,128]{1,0:T(8,128)S(1)}, f32[2,128,128]{2,1,0:T(8,128)S(1)}, f32[224,128]{1,0:T(8,128)S(1)}) custom-call(s32[1]{0:T(128)} %bitcast.4.side_ref, s32[1]{0:T(128)} %bitcast.1.core_ref, f32[3,128,128]{2,1,0:T(8,128)S(1)} %get-tuple-element.41.own_ref, ...), custom_call_target="tpu_custom_call" | custom-call | tf_op jit(solution)/shard_map/pallas_call | solution.py:400
  85.2 18.5 %all-gather.5 = f32[448,128]{1,0:T(8,128)S(1)} all-gather(f32[224,128]{1,0:T(8,128)S(1)} %get-tuple-element.44), channel_id=7, replica_groups={{0,128},{4,132},{8,136},{12,140},{16,144},{20,148},{24,152},{28,156},{3..., dimensions={0}, use_global_device_ids=true | all-gather | bytes 344064 | tf_op jit(solution)/shard_map/all_gather | solution.py:335
  103.6 2.8 %shard_map.53 = (f32[128,128]{1,0:T(8,128)S(1)}, f32[128,128]{1,0:T(8,128)S(1)}, f32[128,128]{1,0:T(8,128)S(1)}, f32[1,128,128]{2,1,0:T(8,128)S(1)}, f32[96,128]{1,0:T(8,128)S(1)}) custom-call(s32[1]{0:T(128)} %bitcast.3.side_ref, s32[1]{0:T(128)} %bitcast.1.core_ref, f32[2,128,128]{2,1,0:T(8,128)S(1)} %get-tuple-element.43.own_ref, ...), custom_call_target="tpu_custom_call" | custom-call | tf_op jit(solution)/shard_map/pallas_call | solution.py:400
  106.5 8.9 %all-gather.6 = f32[192,128]{1,0:T(8,128)S(1)} all-gather(f32[96,128]{1,0:T(8,128)S(1)} %get-tuple-element.47), channel_id=8, replica_groups={{0,384},{4,388},{8,392},{12,396},{16,400},{20,404},{24,408},{28,412},{3..., dimensions={0}, use_global_device_ids=true | all-gather | bytes 147456 | tf_op jit(solution)/shard_map/all_gather | solution.py:335
  115.4 10.4 %shard_map.54 = f32[7,32,128]{2,1,0:T(8,128)} custom-call(s32[1]{0:T(128)} %bitcast.side_ref, s32[1]{0:T(128)} %bitcast.1.core_ref, s32[1]{0:T(128)} %bitcast.2.rep_ref, f32[1,128,128]{2,1,0:T(8,128)S(1)} %get-tuple-element.46.own_ref, f32[2,96,128]{2,1,0:T(8,128)S(1)} %bitcast.22, f32[128,128]{1,0:T(8,128)S(1)} %get-tuple-element.48.refs_0_, ...), custom_call_target="tpu_custom_call" | custom-call | tf_op jit(solution)/shard_map/pallas_call | solution.py:397
  (1 shorter events, 0.0 us)
Async XLA Ops:
  0.0 12.6 %copy-start.1 = (f32[8,4,4096]{2,1,0:T(4,128)S(1)}, f32[8,4,4096]{2,1,0:T(4,128)}, u32[]{:S(2)}) copy-start(f32[8,4,4096]{2,1,0:T(4,128)} %param.5) | copy-start | bytes 1572868
  1.2 15.2 %collective-permute-start = (f32[2,32,512]{2,1,0:T(8,128)S(1)}, f32[2,32,512]{2,1,0:T(8,128)S(1)}, u32[]{:S(2)}, u32[]{:S(2)}) collective-permute-start(f32[2,32,512]{2,1,0:T(8,128)S(1)} %get-tuple-element.62), channel_id=1, source_target_pairs={{0,1},{1,2},{2,3},{3,0},{4,5},{5,6},{6,7},{7,4},{8,9},{9,10},{10,1... | collective-permute-start | bytes 393224 | tf_op jit(solution)/shard_map/ppermute | solution.py:360
  4.6 11.8 %collective-permute-start.1 = (f32[2,32,512]{2,1,0:T(8,128)S(1)}, f32[2,32,512]{2,1,0:T(8,128)S(1)}, u32[]{:S(2)}, u32[]{:S(2)}) collective-permute-start(f32[2,32,512]{2,1,0:T(8,128)S(1)} %get-tuple-element.64), channel_id=1, source_target_pairs={{0,2},{1,3},{2,0},{3,1},{4,6},{5,7},{6,4},{7,5},{8,10},{9,11},{10,... | collective-permute-start | bytes 393224 | tf_op jit(solution)/shard_map/ppermute | solution.py:360
  9.3 7.2 %collective-permute-start.2 = (f32[2,32,512]{2,1,0:T(8,128)S(1)}, f32[2,32,512]{2,1,0:T(8,128)S(1)}, u32[]{:S(2)}, u32[]{:S(2)}) collective-permute-start(f32[2,32,512]{2,1,0:T(8,128)S(1)} %get-tuple-element.61), channel_id=1, source_target_pairs={{0,3},{1,0},{2,1},{3,2},{4,7},{5,4},{6,5},{7,6},{8,11},{9,8},{10,9... | collective-permute-start | bytes 393224 | tf_op jit(solution)/shard_map/ppermute | solution.py:360
  12.6 0.7 copy-start.2
  13.4 0.7 copy-start

commit v8 on v7

--- a/solution.py
+++ b/solution.py
@@ -322,6 +322,8 @@
         return leaf ^ 6
     if bit == 4:
         return leaf ^ 24
+    if bit == 5:
+        return leaf ^ 56
     if bit == 6:
         z = leaf >> 3
         z = (z + 4) % 16 if z & 4 else (z - 4) % 16

time: 127 us -> 131 us (1.031)
  blocking collectives: 81.9 us -> 86.5 us
    all_gather x7, blocking collectives: 68.5 us -> 73.1 us  [pair_gathered(): return lax.all_gather(value, axis, axis=0, axis_index_groups=groups)]
where the time goes in v8:
time: 131 us; the launch traced here: 130 us
  blocking collectives  86.5 us (66%)
  Pallas kernels  29.7 us (23%)
  starting transfers between devices  11.4 us (9%)
  local copies, waits for them, and re-layouts  2.67 us (2%)
    all_gather x7, blocking collectives, pair_gathered(): return lax.all_gather(value, axis, axis=0, axis_index_groups=groups)  73.1 us
    pallas_call x6, Pallas kernels, local(): call(kernel, shapes, 2, 2 + len(state))(side, core, sent, pair, *state)  15.8 us
    all_gather x1, blocking collectives, local(): sent = lax.all_gather(mine, 'rep', axis=0, tiled=True)  13.4 us
    ppermute x3, starting transfers between devices, local(): lax.ppermute(levels_of(lax.rem(rep_index + shift, reps)), 'rep', pairs)  11.4 us
    pallas_call x1, Pallas kernels, local(): call(kernel, out, 3, 3 * levels, scratch)  10.4 us
  transfers between devices with their start and end apart: 3, of which 0 were waited for; matrix products, arithmetic and copies ran while one was open for 0% of the time, Pallas kernels for 2%

profile of v8, /device:TPU:24, one launch (start us, length us, event | category | flops | bytes accessed | tf_op | source)
XLA Modules:
  0.0 130.4 jit_solution(11518452827608907620)
XLA Ops:
  0.0 0.0 copy-start.1
  0.0 1.2 constant_dynamic-slice_fusion
  1.2 3.4 %collective-permute-start = (f32[2,32,512]{2,1,0:T(8,128)S(1)}, f32[2,32,512]{2,1,0:T(8,128)S(1)}, u32[]{:S(2)}, u32[]{:S(2)}) collective-permute-start(f32[2,32,512]{2,1,0:T(8,128)S(1)} %get-tuple-element.62), channel_id=1, source_target_pairs={{0,1},{1,2},{2,3},{3,0},{4,5},{5,6},{6,7},{7,4},{8,9},{9,10},{10,1... | collective-permute-start | bytes 393224 | tf_op jit(solution)/shard_map/ppermute | solution.py:362
  4.6 4.6 %collective-permute-start.1 = (f32[2,32,512]{2,1,0:T(8,128)S(1)}, f32[2,32,512]{2,1,0:T(8,128)S(1)}, u32[]{:S(2)}, u32[]{:S(2)}) collective-permute-start(f32[2,32,512]{2,1,0:T(8,128)S(1)} %get-tuple-element.64), channel_id=1, source_target_pairs={{0,2},{1,3},{2,0},{3,1},{4,6},{5,7},{6,4},{7,5},{8,10},{9,11},{10,... | collective-permute-start | bytes 393224 | tf_op jit(solution)/shard_map/ppermute | solution.py:362
  9.3 3.3 %collective-permute-start.2 = (f32[2,32,512]{2,1,0:T(8,128)S(1)}, f32[2,32,512]{2,1,0:T(8,128)S(1)}, u32[]{:S(2)}, u32[]{:S(2)}) collective-permute-start(f32[2,32,512]{2,1,0:T(8,128)S(1)} %get-tuple-element.61), channel_id=1, source_target_pairs={{0,3},{1,0},{2,1},{3,2},{4,7},{5,4},{6,5},{7,6},{8,11},{9,8},{10,9... | collective-permute-start | bytes 393224 | tf_op jit(solution)/shard_map/ppermute | solution.py:362
  12.6 0.0 copy-done.1
  12.6 0.0 copy-start.2
  12.6 0.5 reshape.39.blocks_ref
  13.2 0.1 copy-done.2
  13.3 0.1 copy.6.cols_ref
  13.4 0.0 copy-start
  13.4 0.7 copy-done
  14.1 2.3 %shard_map.46 = (bf16[512,512]{1,0:T(8,128)(2,1)S(1)}, bf16[512,512]{1,0:T(8,128)(2,1)S(1)}) custom-call(s32[8,4]{1,0:T(8,128)S(1)} %copy.6.cols_ref, f32[32,64,64]{2,1,0:T(8,128)S(1)} %reshape.39.blocks_ref, s32[1,512]{1,0:T(1,128)S(1)} %copy-done), custom_call_target="tpu_custom_call" | custom-call | tf_op jit(solution)/shard_map/pallas_call | solution.py:365
  16.4 0.0 collective-permute-done.refs_0_
  16.4 0.0 collective-permute-done.1.refs_1_
  16.4 0.0 collective-permute-done.2.refs_2_
  16.5 1.2 shard_map.47
  17.7 13.4 %all_gather.45.own_ref.refs_6_ = f32[8,128,128]{2,1,0:T(8,128)S(1)} all-gather(f32[2,128,128]{2,1,0:T(8,128)S(1)} %shard_map.47), channel_id=1, replica_groups=mesh['leaf'=128,'rep'=4] {'rep'}, dimensions={0}, use_global_device_ids=true | all-gather | bytes 655360 | tf_op jit(solution)/shard_map/all_gather | solution.py:372
  31.1 2.5 %all-gather = f32[14,128,128]{2,1,0:T(8,128)S(1)} all-gather(f32[7,128,128]{2,1,0:T(8,128)S(1)} %slice.4), channel_id=2, replica_groups={{0,4},{8,12},{16,20},{24,28},{32,36},{40,44},{48,52},{56,60},{64,68},{7..., dimensions={0}, use_global_device_ids=true | all-gather | bytes 1376256 | tf_op jit(solution)/shard_map/all_gather | solution.py:337
  33.5 2.8 %shard_map.48 = (f32[128,128]{1,0:T(8,128)S(1)}, f32[128,128]{1,0:T(8,128)S(1)}, f32[128,128]{1,0:T(8,128)S(1)}, f32[6,128,128]{2,1,0:T(8,128)S(1)}) custom-call(s32[1]{0:T(128)} %bitcast.8.side_ref, s32[1]{0:T(128)} %bitcast.1.core_ref, f32[8,128,128]{2,1,0:T(8,128)S(1)} %all_gather.45.own_ref.refs_6_, f32[2,7,128,128]{3,2,1,0:T(8,128)S(1)} %bitcast.16), custom_call_target="tpu_custom_call" | custom-call | tf_op jit(solution)/shard_map/pallas_call | solution.py:402
  36.4 12.1 %all-gather.1 = f32[12,128,128]{2,1,0:T(8,128)S(1)} all-gather(f32[6,128,128]{2,1,0:T(8,128)S(1)} %get-tuple-element.35.own_ref), channel_id=3, replica_groups={{0,8},{4,12},{16,24},{20,28},{32,40},{36,44},{48,56},{52,60},{64,72},{6..., dimensions={0}, use_global_device_ids=true | all-gather | bytes 1179648 | tf_op jit(solution)/shard_map/all_gather | solution.py:337
  48.5 2.5 %shard_map.49 = (f32[128,128]{1,0:T(8,128)S(1)}, f32[128,128]{1,0:T(8,128)S(1)}, f32[128,128]{1,0:T(8,128)S(1)}, f32[5,128,128]{2,1,0:T(8,128)S(1)}) custom-call(s32[1]{0:T(128)} %bitcast.7.side_ref, s32[1]{0:T(128)} %bitcast.1.core_ref, f32[6,128,128]{2,1,0:T(8,128)S(1)} %get-tuple-element.35.own_ref, f32[2,6,128,128]{3,2,1,0:T(8,128)S(1)} %bitcast.17, ...), custom_call_target="tpu_custom_call" | custom-call | tf_op jit(solution)/shard_map/pallas_call | solution.py:402
  51.0 12.1 %all-gather.2 = f32[10,128,128]{2,1,0:T(8,128)S(1)} all-gather(f32[5,128,128]{2,1,0:T(8,128)S(1)} %get-tuple-element.37.own_ref), channel_id=4, replica_groups={{0,24},{4,28},{8,16},{12,20},{32,56},{36,60},{40,48},{44,52},{64,88},{6..., dimensions={0}, use_global_device_ids=true | all-gather | bytes 983040 | tf_op jit(solution)/shard_map/all_gather | solution.py:337
  63.2 2.5 %shard_map.50 = (f32[128,128]{1,0:T(8,128)S(1)}, f32[128,128]{1,0:T(8,128)S(1)}, f32[128,128]{1,0:T(8,128)S(1)}, f32[4,128,128]{2,1,0:T(8,128)S(1)}) custom-call(s32[1]{0:T(128)} %bitcast.6.side_ref, s32[1]{0:T(128)} %bitcast.1.core_ref, f32[5,128,128]{2,1,0:T(8,128)S(1)} %get-tuple-element.37.own_ref, f32[2,5,128,128]{3,2,1,0:T(8,128)S(1)} %bitcast.18, ...), custom_call_target="tpu_custom_call" | custom-call | tf_op jit(solution)/shard_map/pallas_call | solution.py:402
  65.7 7.6 %all-gather.3 = f32[8,128,128]{2,1,0:T(8,128)S(1)} all-gather(f32[4,128,128]{2,1,0:T(8,128)S(1)} %get-tuple-element.39.own_ref), channel_id=5, replica_groups={{0,32},{4,36},{8,40},{12,44},{16,48},{20,52},{24,56},{28,60},{64,96},{6..., dimensions={0}, use_global_device_ids=true | all-gather | bytes 786432 | tf_op jit(solution)/shard_map/all_gather | solution.py:337
  73.3 2.5 %shard_map.51 = (f32[128,128]{1,0:T(8,128)S(1)}, f32[128,128]{1,0:T(8,128)S(1)}, f32[128,128]{1,0:T(8,128)S(1)}, f32[3,128,128]{2,1,0:T(8,128)S(1)}) custom-call(s32[1]{0:T(128)} %bitcast.5.side_ref, s32[1]{0:T(128)} %bitcast.1.core_ref, f32[4,128,128]{2,1,0:T(8,128)S(1)} %get-tuple-element.39.own_ref, f32[2,4,128,128]{3,2,1,0:T(8,128)S(1)} %bitcast.19, ...), custom_call_target="tpu_custom_call" | custom-call | tf_op jit(solution)/shard_map/pallas_call | solution.py:402
  75.8 8.7 %all-gather.4 = f32[6,128,128]{2,1,0:T(8,128)S(1)} all-gather(f32[3,128,128]{2,1,0:T(8,128)S(1)} %get-tuple-element.41.own_ref), channel_id=6, replica_groups={{0,96},{4,100},{8,104},{12,108},{16,112},{20,116},{24,120},{28,124},{32..., dimensions={0}, use_global_device_ids=true | all-gather | bytes 589824 | tf_op jit(solution)/shard_map/all_gather | solution.py:337
  84.5 2.5 %shard_map.52 = (f32[128,128]{1,0:T(8,128)S(1)}, f32[128,128]{1,0:T(8,128)S(1)}, f32[128,128]{1,0:T(8,128)S(1)}, f32[2,128,128]{2,1,0:T(8,128)S(1)}, f32[224,128]{1,0:T(8,128)S(1)}) custom-call(s32[1]{0:T(128)} %bitcast.4.side_ref, s32[1]{0:T(128)} %bitcast.1.core_ref, f32[3,128,128]{2,1,0:T(8,128)S(1)} %get-tuple-element.41.own_ref, ...), custom_call_target="tpu_custom_call" | custom-call | tf_op jit(solution)/shard_map/pallas_call | solution.py:402
  87.0 14.4 %all-gather.5 = f32[448,128]{1,0:T(8,128)S(1)} all-gather(f32[224,128]{1,0:T(8,128)S(1)} %get-tuple-element.44), channel_id=7, replica_groups={{0,224},{4,228},{8,232},{12,236},{16,240},{20,244},{24,248},{28,252},{3..., dimensions={0}, use_global_device_ids=true | all-gather | bytes 344064 | tf_op jit(solution)/shard_map/all_gather | solution.py:337
  101.5 2.8 %shard_map.53 = (f32[128,128]{1,0:T(8,128)S(1)}, f32[128,128]{1,0:T(8,128)S(1)}, f32[128,128]{1,0:T(8,128)S(1)}, f32[1,128,128]{2,1,0:T(8,128)S(1)}, f32[96,128]{1,0:T(8,128)S(1)}) custom-call(s32[1]{0:T(128)} %bitcast.3.side_ref, s32[1]{0:T(128)} %bitcast.1.core_ref, f32[2,128,128]{2,1,0:T(8,128)S(1)} %get-tuple-element.43.own_ref, ...), custom_call_target="tpu_custom_call" | custom-call | tf_op jit(solution)/shard_map/pallas_call | solution.py:402
  104.4 15.6 %all-gather.6 = f32[192,128]{1,0:T(8,128)S(1)} all-gather(f32[96,128]{1,0:T(8,128)S(1)} %get-tuple-element.47), channel_id=8, replica_groups={{0,384},{4,388},{8,392},{12,396},{16,400},{20,404},{24,408},{28,412},{3..., dimensions={0}, use_global_device_ids=true | all-gather | bytes 147456 | tf_op jit(solution)/shard_map/all_gather | solution.py:337
  120.0 10.4 %shard_map.54 = f32[7,32,128]{2,1,0:T(8,128)} custom-call(s32[1]{0:T(128)} %bitcast.side_ref, s32[1]{0:T(128)} %bitcast.1.core_ref, s32[1]{0:T(128)} %bitcast.2.rep_ref, f32[1,128,128]{2,1,0:T(8,128)S(1)} %get-tuple-element.46.own_ref, f32[2,96,128]{2,1,0:T(8,128)S(1)} %bitcast.22, f32[128,128]{1,0:T(8,128)S(1)} %get-tuple-element.48.refs_0_, ...), custom_call_target="tpu_custom_call" | custom-call | tf_op jit(solution)/shard_map/pallas_call | solution.py:399
  (1 shorter events, 0.0 us)
Async XLA Ops:
  0.0 12.6 %copy-start.1 = (f32[8,4,4096]{2,1,0:T(4,128)S(1)}, f32[8,4,4096]{2,1,0:T(4,128)}, u32[]{:S(2)}) copy-start(f32[8,4,4096]{2,1,0:T(4,128)} %param.5) | copy-start | bytes 1572868
  1.2 15.2 %collective-permute-start = (f32[2,32,512]{2,1,0:T(8,128)S(1)}, f32[2,32,512]{2,1,0:T(8,128)S(1)}, u32[]{:S(2)}, u32[]{:S(2)}) collective-permute-start(f32[2,32,512]{2,1,0:T(8,128)S(1)} %get-tuple-element.62), channel_id=1, source_target_pairs={{0,1},{1,2},{2,3},{3,0},{4,5},{5,6},{6,7},{7,4},{8,9},{9,10},{10,1... | collective-permute-start | bytes 393224 | tf_op jit(solution)/shard_map/ppermute | solution.py:362
  4.6 11.8 %collective-permute-start.1 = (f32[2,32,512]{2,1,0:T(8,128)S(1)}, f32[2,32,512]{2,1,0:T(8,128)S(1)}, u32[]{:S(2)}, u32[]{:S(2)}) collective-permute-start(f32[2,32,512]{2,1,0:T(8,128)S(1)} %get-tuple-element.64), channel_id=1, source_target_pairs={{0,2},{1,3},{2,0},{3,1},{4,6},{5,7},{6,4},{7,5},{8,10},{9,11},{10,... | collective-permute-start | bytes 393224 | tf_op jit(solution)/shard_map/ppermute | solution.py:362
  9.3 7.2 %collective-permute-start.2 = (f32[2,32,512]{2,1,0:T(8,128)S(1)}, f32[2,32,512]{2,1,0:T(8,128)S(1)}, u32[]{:S(2)}, u32[]{:S(2)}) collective-permute-start(f32[2,32,512]{2,1,0:T(8,128)S(1)} %get-tuple-element.61), channel_id=1, source_target_pairs={{0,3},{1,0},{2,1},{3,2},{4,7},{5,4},{6,5},{7,6},{8,11},{9,8},{10,9... | collective-permute-start | bytes 393224 | tf_op jit(solution)/shard_map/ppermute | solution.py:362
  12.6 0.7 copy-start.2
  13.4 0.7 copy-start

commit v9 on v8

--- a/solution.py
+++ b/solution.py
@@ -325,9 +325,7 @@
     if bit == 5:
         return leaf ^ 56
     if bit == 6:
-        z = leaf >> 3
-        z = (z + 4) % 16 if z & 4 else (z - 4) % 16
-        return z * 8 + (leaf & 7)
+        return leaf ^ 120
     return leaf ^ (1 << bit)
 
 

time: 131 us -> 127 us (0.969)
  the two profiles are of different devices: /device:TPU:24 before, /device:TPU:128 now
where the time goes in v9:
time: 127 us; the launch traced here: 125 us
  blocking collectives  81.3 us (64%)
  Pallas kernels  29.7 us (23%)
  starting transfers between devices  11.4 us (9%)
  local copies, waits for them, and re-layouts  2.67 us (2%)
    all_gather x7, blocking collectives, pair_gathered(): return lax.all_gather(value, axis, axis=0, axis_index_groups=groups)  67.9 us
    pallas_call x6, Pallas kernels, local(): call(kernel, shapes, 2, 2 + len(state))(side, core, sent, pair, *state)  15.7 us
    all_gather x1, blocking collectives, local(): sent = lax.all_gather(mine, 'rep', axis=0, tiled=True)  13.4 us
    ppermute x3, starting transfers between devices, local(): lax.ppermute(levels_of(lax.rem(rep_index + shift, reps)), 'rep', pairs)  11.4 us
    pallas_call x1, Pallas kernels, local(): call(kernel, out, 3, 3 * levels, scratch)  10.4 us
  transfers between devices with their start and end apart: 3, of which 0 were waited for; matrix products, arithmetic and copies ran while one was open for 0% of the time, Pallas kernels for 2%

profile of v9, /device:TPU:128, one launch (start us, length us, event | category | flops | bytes accessed | tf_op | source)
XLA Modules:
  0.0 125.2 jit_solution(5164716016268917926)
XLA Ops:
  0.0 0.0 copy-start.1
  0.0 1.2 constant_dynamic-slice_fusion
  1.2 3.4 %collective-permute-start = (f32[2,32,512]{2,1,0:T(8,128)S(1)}, f32[2,32,512]{2,1,0:T(8,128)S(1)}, u32[]{:S(2)}, u32[]{:S(2)}) collective-permute-start(f32[2,32,512]{2,1,0:T(8,128)S(1)} %get-tuple-element.62), channel_id=1, source_target_pairs={{0,1},{1,2},{2,3},{3,0},{4,5},{5,6},{6,7},{7,4},{8,9},{9,10},{10,1... | collective-permute-start | bytes 393224 | tf_op jit(solution)/shard_map/ppermute | solution.py:360
  4.6 4.6 %collective-permute-start.1 = (f32[2,32,512]{2,1,0:T(8,128)S(1)}, f32[2,32,512]{2,1,0:T(8,128)S(1)}, u32[]{:S(2)}, u32[]{:S(2)}) collective-permute-start(f32[2,32,512]{2,1,0:T(8,128)S(1)} %get-tuple-element.64), channel_id=1, source_target_pairs={{0,2},{1,3},{2,0},{3,1},{4,6},{5,7},{6,4},{7,5},{8,10},{9,11},{10,... | collective-permute-start | bytes 393224 | tf_op jit(solution)/shard_map/ppermute | solution.py:360
  9.3 3.3 %collective-permute-start.2 = (f32[2,32,512]{2,1,0:T(8,128)S(1)}, f32[2,32,512]{2,1,0:T(8,128)S(1)}, u32[]{:S(2)}, u32[]{:S(2)}) collective-permute-start(f32[2,32,512]{2,1,0:T(8,128)S(1)} %get-tuple-element.61), channel_id=1, source_target_pairs={{0,3},{1,0},{2,1},{3,2},{4,7},{5,4},{6,5},{7,6},{8,11},{9,8},{10,9... | collective-permute-start | bytes 393224 | tf_op jit(solution)/shard_map/ppermute | solution.py:360
  12.6 0.0 copy-done.1
  12.6 0.0 copy-start.2
  12.6 0.5 reshape.39.blocks_ref
  13.2 0.1 copy-done.2
  13.3 0.1 copy.6.cols_ref
  13.4 0.0 copy-start
  13.4 0.7 copy-done
  14.1 2.3 %shard_map.46 = (bf16[512,512]{1,0:T(8,128)(2,1)S(1)}, bf16[512,512]{1,0:T(8,128)(2,1)S(1)}) custom-call(s32[8,4]{1,0:T(8,128)S(1)} %copy.6.cols_ref, f32[32,64,64]{2,1,0:T(8,128)S(1)} %reshape.39.blocks_ref, s32[1,512]{1,0:T(1,128)S(1)} %copy-done), custom_call_target="tpu_custom_call" | custom-call | tf_op jit(solution)/shard_map/pallas_call | solution.py:363
  16.4 0.0 collective-permute-done.refs_0_
  16.4 0.0 collective-permute-done.1.refs_1_
  16.4 0.0 collective-permute-done.2.refs_2_
  16.5 1.2 shard_map.47
  17.7 13.4 %all_gather.45.own_ref.refs_6_ = f32[8,128,128]{2,1,0:T(8,128)S(1)} all-gather(f32[2,128,128]{2,1,0:T(8,128)S(1)} %shard_map.47), channel_id=1, replica_groups=mesh['leaf'=128,'rep'=4] {'rep'}, dimensions={0}, use_global_device_ids=true | all-gather | bytes 655360 | tf_op jit(solution)/shard_map/all_gather | solution.py:370
  31.1 2.5 %all-gather = f32[14,128,128]{2,1,0:T(8,128)S(1)} all-gather(f32[7,128,128]{2,1,0:T(8,128)S(1)} %slice.4), channel_id=2, replica_groups={{0,4},{8,12},{16,20},{24,28},{32,36},{40,44},{48,52},{56,60},{64,68},{7..., dimensions={0}, use_global_device_ids=true | all-gather | bytes 1376256 | tf_op jit(solution)/shard_map/all_gather | solution.py:335
  33.5 2.8 %shard_map.48 = (f32[128,128]{1,0:T(8,128)S(1)}, f32[128,128]{1,0:T(8,128)S(1)}, f32[128,128]{1,0:T(8,128)S(1)}, f32[6,128,128]{2,1,0:T(8,128)S(1)}) custom-call(s32[1]{0:T(128)} %bitcast.8.side_ref, s32[1]{0:T(128)} %bitcast.1.core_ref, f32[8,128,128]{2,1,0:T(8,128)S(1)} %all_gather.45.own_ref.refs_6_, f32[2,7,128,128]{3,2,1,0:T(8,128)S(1)} %bitcast.16), custom_call_target="tpu_custom_call" | custom-call | tf_op jit(solution)/shard_map/pallas_call | solution.py:400
  36.4 11.8 %all-gather.1 = f32[12,128,128]{2,1,0:T(8,128)S(1)} all-gather(f32[6,128,128]{2,1,0:T(8,128)S(1)} %get-tuple-element.35.own_ref), channel_id=3, replica_groups={{0,8},{4,12},{16,24},{20,28},{32,40},{36,44},{48,56},{52,60},{64,72},{6..., dimensions={0}, use_global_device_ids=true | all-gather | bytes 1179648 | tf_op jit(solution)/shard_map/all_gather | solution.py:335
  48.2 2.5 %shard_map.49 = (f32[128,128]{1,0:T(8,128)S(1)}, f32[128,128]{1,0:T(8,128)S(1)}, f32[128,128]{1,0:T(8,128)S(1)}, f32[5,128,128]{2,1,0:T(8,128)S(1)}) custom-call(s32[1]{0:T(128)} %bitcast.7.side_ref, s32[1]{0:T(128)} %bitcast.1.core_ref, f32[6,128,128]{2,1,0:T(8,128)S(1)} %get-tuple-element.35.own_ref, f32[2,6,128,128]{3,2,1,0:T(8,128)S(1)} %bitcast.17, ...), custom_call_target="tpu_custom_call" | custom-call | tf_op jit(solution)/shard_map/pallas_call | solution.py:400
  50.7 10.8 %all-gather.2 = f32[10,128,128]{2,1,0:T(8,128)S(1)} all-gather(f32[5,128,128]{2,1,0:T(8,128)S(1)} %get-tuple-element.37.own_ref), channel_id=4, replica_groups={{0,24},{4,28},{8,16},{12,20},{32,56},{36,60},{40,48},{44,52},{64,88},{6..., dimensions={0}, use_global_device_ids=true | all-gather | bytes 983040 | tf_op jit(solution)/shard_map/all_gather | solution.py:335
  61.6 2.5 %shard_map.50 = (f32[128,128]{1,0:T(8,128)S(1)}, f32[128,128]{1,0:T(8,128)S(1)}, f32[128,128]{1,0:T(8,128)S(1)}, f32[4,128,128]{2,1,0:T(8,128)S(1)}) custom-call(s32[1]{0:T(128)} %bitcast.6.side_ref, s32[1]{0:T(128)} %bitcast.1.core_ref, f32[5,128,128]{2,1,0:T(8,128)S(1)} %get-tuple-element.37.own_ref, f32[2,5,128,128]{3,2,1,0:T(8,128)S(1)} %bitcast.18, ...), custom_call_target="tpu_custom_call" | custom-call | tf_op jit(solution)/shard_map/pallas_call | solution.py:400
  64.1 9.1 %all-gather.3 = f32[8,128,128]{2,1,0:T(8,128)S(1)} all-gather(f32[4,128,128]{2,1,0:T(8,128)S(1)} %get-tuple-element.39.own_ref), channel_id=5, replica_groups={{0,32},{4,36},{8,40},{12,44},{16,48},{20,52},{24,56},{28,60},{64,96},{6..., dimensions={0}, use_global_device_ids=true | all-gather | bytes 786432 | tf_op jit(solution)/shard_map/all_gather | solution.py:335
  73.2 2.5 %shard_map.51 = (f32[128,128]{1,0:T(8,128)S(1)}, f32[128,128]{1,0:T(8,128)S(1)}, f32[128,128]{1,0:T(8,128)S(1)}, f32[3,128,128]{2,1,0:T(8,128)S(1)}) custom-call(s32[1]{0:T(128)} %bitcast.5.side_ref, s32[1]{0:T(128)} %bitcast.1.core_ref, f32[4,128,128]{2,1,0:T(8,128)S(1)} %get-tuple-element.39.own_ref, f32[2,4,128,128]{3,2,1,0:T(8,128)S(1)} %bitcast.19, ...), custom_call_target="tpu_custom_call" | custom-call | tf_op jit(solution)/shard_map/pallas_call | solution.py:400
  75.7 8.2 %all-gather.4 = f32[6,128,128]{2,1,0:T(8,128)S(1)} all-gather(f32[3,128,128]{2,1,0:T(8,128)S(1)} %get-tuple-element.41.own_ref), channel_id=6, replica_groups={{0,96},{4,100},{8,104},{12,108},{16,112},{20,116},{24,120},{28,124},{32..., dimensions={0}, use_global_device_ids=true | all-gather | bytes 589824 | tf_op jit(solution)/shard_map/all_gather | solution.py:335
  84.0 2.5 %shard_map.52 = (f32[128,128]{1,0:T(8,128)S(1)}, f32[128,128]{1,0:T(8,128)S(1)}, f32[128,128]{1,0:T(8,128)S(1)}, f32[2,128,128]{2,1,0:T(8,128)S(1)}, f32[224,128]{1,0:T(8,128)S(1)}) custom-call(s32[1]{0:T(128)} %bitcast.4.side_ref, s32[1]{0:T(128)} %bitcast.1.core_ref, f32[3,128,128]{2,1,0:T(8,128)S(1)} %get-tuple-element.41.own_ref, ...), custom_call_target="tpu_custom_call" | custom-call | tf_op jit(solution)/shard_map/pallas_call | solution.py:400
  86.5 14.1 %all-gather.5 = f32[448,128]{1,0:T(8,128)S(1)} all-gather(f32[224,128]{1,0:T(8,128)S(1)} %get-tuple-element.44), channel_id=7, replica_groups={{0,224},{4,228},{8,232},{12,236},{16,240},{20,244},{24,248},{28,252},{3..., dimensions={0}, use_global_device_ids=true | all-gather | bytes 344064 | tf_op jit(solution)/shard_map/all_gather | solution.py:335
  100.5 2.8 %shard_map.53 = (f32[128,128]{1,0:T(8,128)S(1)}, f32[128,128]{1,0:T(8,128)S(1)}, f32[128,128]{1,0:T(8,128)S(1)}, f32[1,128,128]{2,1,0:T(8,128)S(1)}, f32[96,128]{1,0:T(8,128)S(1)}) custom-call(s32[1]{0:T(128)} %bitcast.3.side_ref, s32[1]{0:T(128)} %bitcast.1.core_ref, f32[2,128,128]{2,1,0:T(8,128)S(1)} %get-tuple-element.43.own_ref, ...), custom_call_target="tpu_custom_call" | custom-call | tf_op jit(solution)/shard_map/pallas_call | solution.py:400
  103.4 11.4 %all-gather.6 = f32[192,128]{1,0:T(8,128)S(1)} all-gather(f32[96,128]{1,0:T(8,128)S(1)} %get-tuple-element.47), channel_id=8, replica_groups={{0,480},{4,484},{8,488},{12,492},{16,496},{20,500},{24,504},{28,508},{3..., dimensions={0}, use_global_device_ids=true | all-gather | bytes 147456 | tf_op jit(solution)/shard_map/all_gather | solution.py:335
  114.8 10.4 %shard_map.54 = f32[7,32,128]{2,1,0:T(8,128)} custom-call(s32[1]{0:T(128)} %bitcast.side_ref, s32[1]{0:T(128)} %bitcast.1.core_ref, s32[1]{0:T(128)} %bitcast.2.rep_ref, f32[1,128,128]{2,1,0:T(8,128)S(1)} %get-tuple-element.46.own_ref, f32[2,96,128]{2,1,0:T(8,128)S(1)} %bitcast.22, f32[128,128]{1,0:T(8,128)S(1)} %get-tuple-element.48.refs_0_, ...), custom_call_target="tpu_custom_call" | custom-call | tf_op jit(solution)/shard_map/pallas_call | solution.py:397
  (1 shorter events, 0.0 us)
Async XLA Ops:
  0.0 12.6 %copy-start.1 = (f32[8,4,4096]{2,1,0:T(4,128)S(1)}, f32[8,4,4096]{2,1,0:T(4,128)}, u32[]{:S(2)}) copy-start(f32[8,4,4096]{2,1,0:T(4,128)} %param.5) | copy-start | bytes 1572868
  1.2 15.2 %collective-permute-start = (f32[2,32,512]{2,1,0:T(8,128)S(1)}, f32[2,32,512]{2,1,0:T(8,128)S(1)}, u32[]{:S(2)}, u32[]{:S(2)}) collective-permute-start(f32[2,32,512]{2,1,0:T(8,128)S(1)} %get-tuple-element.62), channel_id=1, source_target_pairs={{0,1},{1,2},{2,3},{3,0},{4,5},{5,6},{6,7},{7,4},{8,9},{9,10},{10,1... | collective-permute-start | bytes 393224 | tf_op jit(solution)/shard_map/ppermute | solution.py:360
  4.6 11.8 %collective-permute-start.1 = (f32[2,32,512]{2,1,0:T(8,128)S(1)}, f32[2,32,512]{2,1,0:T(8,128)S(1)}, u32[]{:S(2)}, u32[]{:S(2)}) collective-permute-start(f32[2,32,512]{2,1,0:T(8,128)S(1)} %get-tuple-element.64), channel_id=1, source_target_pairs={{0,2},{1,3},{2,0},{3,1},{4,6},{5,7},{6,4},{7,5},{8,10},{9,11},{10,... | collective-permute-start | bytes 393224 | tf_op jit(solution)/shard_map/ppermute | solution.py:360
  9.3 7.2 %collective-permute-start.2 = (f32[2,32,512]{2,1,0:T(8,128)S(1)}, f32[2,32,512]{2,1,0:T(8,128)S(1)}, u32[]{:S(2)}, u32[]{:S(2)}) collective-permute-start(f32[2,32,512]{2,1,0:T(8,128)S(1)} %get-tuple-element.61), channel_id=1, source_target_pairs={{0,3},{1,0},{2,1},{3,2},{4,7},{5,4},{6,5},{7,6},{8,11},{9,8},{10,9... | collective-permute-start | bytes 393224 | tf_op jit(solution)/shard_map/ppermute | solution.py:360
  12.6 0.7 copy-start.2
  13.4 0.7 copy-start
